TPU v7x, 128 devices: a whole 4x4x4 slice. The times are simulated.
128 devices in a mesh: patch: 16 (over y, z), level: 8 (over x, core).
Axes of the slice: x: 4, y: 4, z: 4, core: 2. Of those that a mesh axis runs over, the one named last changes fastest.
Arguments:
- right_side: bfloat16 [64, 262144], P(None, ('patch', 'level')), may hold values from -6 to 6
- level_pairs: bfloat16 [10, 2048, 2, 128, 128], P(None, ('patch', 'level')), may hold values from -0.375 to 0.375
- near_blocks: bfloat16 [2048, 8, 128, 128], P(('patch', 'level')), may hold values from -0.1875 to 0.1875
- near_index: int32 [2048, 8], P(('patch', 'level')), may hold values from 0 to 47
- near_count: int32 [2048], P(('patch', 'level')), may hold values from 1 to 8, as said below
Outputs:
- solution: bfloat16 [64, 262144], P(None, ('patch', 'level'))
Inputs may be any that keep to these rules, and one draw needn't show every extreme that they name: `near_index`: slots at or past a block's near_count are not used. `near_count`: on every device some block uses all of that device's most slots, and on some device that most is 8.
All inputs are finite; a program needn't handle non-finite values.
Results may differ from a plain program's by a relative error of at most 0.035.
Values may be sent and summed in bfloat16 or wider, within the bound.
No kernel may reach another device: no remote copies, remote signals or barrier semaphores. Data moves between devices by JAX's collectives and lax.ppermute only.
A program may use at most 128 MiB of HBM per device.

v0:
```python
import jax
import jax.numpy as jnp
from jax import lax
from jax.sharding import PartitionSpec as P

ITERS = 3


coupling = 0.4


def extended(value, sides, width):
    for axis, dim in sides:
        devices, length = (lax.axis_size(axis), value.shape[dim])
        up = [(i, (i + 1) % devices) for i in range(devices)]
        down = [(j, i) for i, j in up]
        last = lax.slice_in_dim(value, length - width, length, axis=dim)
        leading = lax.slice_in_dim(value, 0, width, axis=dim)
        before = lax.ppermute(last, axis, up)
        after = lax.ppermute(leading, axis, down)
        value = jnp.concatenate([before, value, after], axis=dim)
    return value


def partner_2(block, axis, distance):
    count = lax.axis_size(axis)
    route = []
    for low in range(count):
        high = low | 1 << distance
        if high != low and high < count:
            route += [(low, high), (high, low)]
    return lax.ppermute(block, axis, route)


def flip_local(mixed, stride):
    rhs_count, blocks, width = mixed.shape
    grouped = mixed.reshape(rhs_count, blocks // (2 * stride), 2, stride, width)
    return grouped[:, :, ::-1].reshape(rhs_count, blocks, width)


def apply_level(mixed, partner, factor):
    own_term = jnp.einsum("rbw,bwv->rbv", mixed, factor[:, 0], preferred_element_type=jnp.float32)
    pair_term = jnp.einsum(
        "rbw,bwv->rbv", partner, factor[:, 1], preferred_element_type=jnp.float32
    )
    return (own_term + pair_term).astype(jnp.bfloat16)


def near_field(window, near_blocks, near_index, near_count):
    blocks, slots, width, _ = near_blocks.shape
    taken = window[:, near_index]
    usable = jnp.arange(slots, dtype=jnp.int32)[None, :] < near_count[:, None]
    taken = jnp.where(usable[None, :, :, None], taken, jnp.zeros_like(taken))
    return jnp.einsum("rbkw,bkwv->rbv", taken, near_blocks, preferred_element_type=jnp.float32)


def per_device(right_side, level_pairs, near_blocks, near_index, near_count):
    rhs_count = right_side.shape[0]
    blocks = near_index.shape[0]
    width = near_blocks.shape[-1]
    levels = level_pairs.shape[0]
    level_count = lax.axis_size("level")
    patch_count = lax.axis_size("patch")
    level_bits = level_count.bit_length() - 1
    patch_bits = patch_count.bit_length() - 1
    local_levels = levels - level_bits - patch_bits
    source = right_side.astype(jnp.float32).reshape(rhs_count, blocks, width)
    current = right_side.reshape(rhs_count, blocks, width)
    for sweep in range(ITERS):
        window = extended(current, (("patch", 1),), blocks)
        near = near_field(window, near_blocks, near_index, near_count)
        mixed = current
        for level_idx in range(local_levels):
            partner = flip_local(mixed, 2**level_idx)
            mixed = apply_level(mixed, partner, level_pairs[level_idx])
        for bit_index in range(level_bits):
            partner = partner_2(mixed, "level", bit_index)
            mixed = apply_level(mixed, partner, level_pairs[local_levels + bit_index])
        for bit_index in range(patch_bits):
            partner = partner_2(mixed, "patch", bit_index)
            mixed = apply_level(mixed, partner, level_pairs[local_levels + level_bits + bit_index])
        current = (source - coupling * (mixed.astype(jnp.float32) + near)).astype(jnp.bfloat16)
    return current.reshape(rhs_count, blocks * width)


def solution(mesh):
    in_specs = (
        P(None, ("patch", "level")),
        P(None, ("patch", "level"), None, None, None),
        P(("patch", "level"), None, None, None),
        P(("patch", "level"), None),
        P(("patch", "level")),
    )
    out_specs = P(None, ("patch", "level"))
    return jax.shard_map(
        per_device, mesh=mesh, in_specs=in_specs, out_specs=out_specs, check_vma=False
    )
```

profile of v0, /device:TPU:0, one launch (start us, length us, event | category | flops | bytes accessed | tf_op | source)
XLA Modules:
  0.0 228.1 jit_solution(3882574696344261691)
XLA Ops:
  0.0 7.6 %fusion.133 = (bf16[1,16,2,128,128]{4,3,2,1,0:T(8,128)(2,1)}, bf16[1,16,2,128,128]{4,3,2,1,0:T(8,128)(2,1)}, bf16[1,16,2,128,128]{4,3,2,1,0:T(8,128)(2,1)}, bf16...) fusion(bf16[10,16,2,128,128]{4,3,2,1,0:T(8,128)(2,1)} %param.6), kind=kLoop, calls=%fused_computation.198 | loop fusion | bytes 20971520 | tf_op jit(solution)/shard_map/slice | solution.py:81
  27.7 6.5 %collective-permute-start.8 = (bf16[64,16,128]{2,0,1:T(8,128)(2,1)}, bf16[64,16,128]{2,0,1:T(8,128)(2,1)}, u32[]{:S(2)}, u32[]{:S(2)}) collective-permute-start(bf16[64,16,128]{2,0,1:T(8,128)(2,1)} %copy_bitcast_fusion.11), channel_id=1, source_target_pairs={{8,0},{16,8},{24,16},{32,24},{40,32},{48,40},{56,48},{64,56},{72,6... | collective-permute-start | bytes 786440 | tf_op jit(solution)/shard_map/ppermute | solution.py:20
  34.8 2.8 %collective-permute-start.2 = (bf16[64,16,128]{2,0,1:T(8,128)(2,1)S(1)}, bf16[64,16,128]{2,0,1:T(8,128)(2,1)S(1)}, u32[]{:S(2)}, u32[]{:S(2)}) collective-permute-start(bf16[64,16,128]{2,0,1:T(8,128)(2,1)S(1)} %fusion.88), channel_id=1, source_target_pairs={{0,4},{4,0},{1,5},{5,1},{2,6},{6,2},{3,7},{7,3},{8,12},{12,8},{9,1... | collective-permute-start | bytes 786440 | tf_op jit(solution)/shard_map/ppermute | solution.py:32
  38.0 6.1 %collective-permute-done.2 = bf16[64,16,128]{2,0,1:T(8,128)(2,1)S(1)} collective-permute-done((bf16[64,16,128]{2,0,1:T(8,128)(2,1)S(1)}, bf16[64,16,128]{2,0,1:T(8,128)(2,1)S(1)}, u32[]{:S(2)}, u32[]{:S(2)}) %collective-permute-start.2) | collective-permute-done | bytes 262176 | tf_op jit(solution)/shard_map/ppermute | solution.py:32
  49.2 3.3 %collective-permute-done.3 = bf16[64,16,128]{2,0,1:T(8,128)(2,1)} collective-permute-done((bf16[64,16,128]{2,0,1:T(8,128)(2,1)}, bf16[64,16,128]{2,0,1:T(8,128)(2,1)}, u32[]{:S(2)}, u32[]{:S(2)}) %collective-permute-start.3) | collective-permute-done | bytes 262176 | tf_op jit(solution)/shard_map/ppermute | solution.py:32
  53.6 2.7 %collective-permute-start.4 = (bf16[64,16,128]{2,0,1:T(8,128)(2,1)S(1)}, bf16[64,16,128]{2,0,1:T(8,128)(2,1)S(1)}, u32[]{:S(2)}, u32[]{:S(2)}) collective-permute-start(bf16[64,16,128]{2,0,1:T(8,128)(2,1)S(1)} %fusion.86), channel_id=1, source_target_pairs={{0,16},{16,0},{8,24},{24,8},{32,48},{48,32},{40,56},{56,40},{64,80... | collective-permute-start | bytes 786440 | tf_op jit(solution)/shard_map/ppermute | solution.py:32
  59.3 2.3 collective-permute-done.4
  65.4 3.3 %gather_fusion = bf16[128,64,128]{2,1,0:T(8,128)(2,1)} fusion(bf16[64,48,128]{2,0,1:T(8,128)(2,1)} %pad_maximum_fusion, s32[1024]{0:T(1024)S(1)} %pad_clamp_fusion), kind=kCustom, calls=%fused_computation | custom fusion | bytes 4194816 | tf_op jit(solution)/shard_map/gather | solution.py:51
  71.3 3.0 %collective-permute-start.6 = (bf16[64,16,128]{2,0,1:T(8,128)(2,1)S(1)}, bf16[64,16,128]{2,0,1:T(8,128)(2,1)S(1)}, u32[]{:S(2)}, u32[]{:S(2)}) collective-permute-start(bf16[64,16,128]{2,0,1:T(8,128)(2,1)S(1)} %fusion.84), channel_id=1, source_target_pairs={{0,64},{64,0},{8,72},{72,8},{16,80},{80,16},{24,88},{88,24},{32,96... | collective-permute-start | bytes 786440 | tf_op jit(solution)/shard_map/ppermute | solution.py:32
  74.3 3.3 %fusion.12 = f32[16,64,128]{2,1,0:T(8,128)S(1)} fusion(bf16[16,8,128,128]{3,2,1,0:T(8,128)(2,1)} %param.7, bf16[16,8,64,128]{3,2,1,0:T(8,128)(2,1)S(1)} %bitcast.397, pred[16,8]{1,0:T(8,128)(4,1)S(1)} %iota_compare_fusion), kind=kOutput, calls=%fused_computation.15 | convolution fusion | flops 269484032 | bytes 6815872 | tf_op jit(solution)/shard_map/rbkw,bkwv->rbv/dot_general | solution.py:54
  85.2 2.2 fusion.98
  100.7 6.6 %collective-permute-done.10 = bf16[64,16,128]{2,0,1:T(8,128)(2,1)S(1)} collective-permute-done((bf16[64,16,128]{2,0,1:T(8,128)(2,1)S(1)}, bf16[64,16,128]{2,0,1:T(8,128)(2,1)S(1)}, u32[]{:S(2)}, u32[]{:S(2)}) %collective-permute-start.10) | collective-permute-done | bytes 262176 | tf_op jit(solution)/shard_map/ppermute | solution.py:32
  107.6 3.1 %collective-permute-start.11 = (bf16[64,16,128]{2,0,1:T(8,128)(2,1)S(1)}, bf16[64,16,128]{2,0,1:T(8,128)(2,1)S(1)}, u32[]{:S(2)}, u32[]{:S(2)}) collective-permute-start(bf16[64,16,128]{2,0,1:T(8,128)(2,1)S(1)} %fusion.81), channel_id=1, source_target_pairs={{0,4},{4,0},{1,5},{5,1},{2,6},{6,2},{3,7},{7,3},{8,12},{12,8},{9,1... | collective-permute-start | bytes 786440 | tf_op jit(solution)/shard_map/ppermute | solution.py:32
  111.0 5.7 %collective-permute-done.11 = bf16[64,16,128]{2,0,1:T(8,128)(2,1)S(1)} collective-permute-done((bf16[64,16,128]{2,0,1:T(8,128)(2,1)S(1)}, bf16[64,16,128]{2,0,1:T(8,128)(2,1)S(1)}, u32[]{:S(2)}, u32[]{:S(2)}) %collective-permute-start.11) | collective-permute-done | bytes 262176 | tf_op jit(solution)/shard_map/ppermute | solution.py:32
  118.9 4.7 %collective-permute-done.12 = bf16[64,16,128]{2,0,1:T(8,128)(2,1)S(1)} collective-permute-done((bf16[64,16,128]{2,0,1:T(8,128)(2,1)S(1)}, bf16[64,16,128]{2,0,1:T(8,128)(2,1)S(1)}, u32[]{:S(2)}, u32[]{:S(2)}) %collective-permute-start.12) | collective-permute-done | bytes 262176 | tf_op jit(solution)/shard_map/ppermute | solution.py:32
  123.9 3.6 %collective-permute-start.13 = (bf16[64,16,128]{2,0,1:T(8,128)(2,1)S(1)}, bf16[64,16,128]{2,0,1:T(8,128)(2,1)S(1)}, u32[]{:S(2)}, u32[]{:S(2)}) collective-permute-start(bf16[64,16,128]{2,0,1:T(8,128)(2,1)S(1)} %fusion.79), channel_id=1, source_target_pairs={{0,16},{16,0},{8,24},{24,8},{32,48},{48,32},{40,56},{56,40},{64,80... | collective-permute-start | bytes 786440 | tf_op jit(solution)/shard_map/ppermute | solution.py:32
  127.5 2.7 %collective-permute-start.17 = (bf16[64,16,128]{2,0,1:T(8,128)(2,1)S(1)}, bf16[64,16,128]{2,0,1:T(8,128)(2,1)S(1)}, u32[]{:S(2)}, u32[]{:S(2)}) collective-permute-start(bf16[64,16,128]{2,0,1:T(8,128)(2,1)S(1)} %copy-done.28), channel_id=1, source_target_pairs={{8,0},{16,8},{24,16},{32,24},{40,32},{48,40},{56,48},{64,56},{72,6... | collective-permute-start | bytes 786440 | tf_op jit(solution)/shard_map/ppermute | solution.py:20
  130.6 5.3 %collective-permute-done.13 = bf16[64,16,128]{2,0,1:T(8,128)(2,1)S(1)} collective-permute-done((bf16[64,16,128]{2,0,1:T(8,128)(2,1)S(1)}, bf16[64,16,128]{2,0,1:T(8,128)(2,1)S(1)}, u32[]{:S(2)}, u32[]{:S(2)}) %collective-permute-start.13) | collective-permute-done | bytes 262176 | tf_op jit(solution)/shard_map/ppermute | solution.py:32
  140.9 3.3 %gather_fusion.1 = bf16[128,64,128]{2,1,0:T(8,128)(2,1)} fusion(bf16[64,48,128]{2,0,1:T(8,128)(2,1)} %pad_maximum_fusion.1, s32[1024]{0:T(1024)S(1)} %pad_clamp_fusion), kind=kCustom, calls=%fused_computation.1 | custom fusion | bytes 4194816 | tf_op jit(solution)/shard_map/gather | solution.py:51
  146.9 2.4 %collective-permute-start.15 = (bf16[64,16,128]{2,0,1:T(8,128)(2,1)S(1)}, bf16[64,16,128]{2,0,1:T(8,128)(2,1)S(1)}, u32[]{:S(2)}, u32[]{:S(2)}) collective-permute-start(bf16[64,16,128]{2,0,1:T(8,128)(2,1)S(1)} %fusion.77), channel_id=1, source_target_pairs={{0,64},{64,0},{8,72},{72,8},{16,80},{80,16},{24,88},{88,24},{32,96... | collective-permute-start | bytes 786440 | tf_op jit(solution)/shard_map/ppermute | solution.py:32
  149.3 3.3 %fusion.15 = f32[16,64,128]{2,1,0:T(8,128)S(1)} fusion(bf16[16,8,128,128]{3,2,1,0:T(8,128)(2,1)} %param.7, bf16[16,8,64,128]{3,2,1,0:T(8,128)(2,1)S(1)} %bitcast.398, pred[16,8]{1,0:T(8,128)(4,1)S(1)} %iota_compare_fusion), kind=kOutput, calls=%fused_computation.16 | convolution fusion | flops 269484032 | bytes 6815872 | tf_op jit(solution)/shard_map/rbkw,bkwv->rbv/dot_general | solution.py:54
  160.8 2.2 fusion.97
  174.4 6.6 %collective-permute-done.19 = bf16[64,16,128]{2,0,1:T(8,128)(2,1)S(1)} collective-permute-done((bf16[64,16,128]{2,0,1:T(8,128)(2,1)S(1)}, bf16[64,16,128]{2,0,1:T(8,128)(2,1)S(1)}, u32[]{:S(2)}, u32[]{:S(2)}) %collective-permute-start.19) | collective-permute-done | bytes 262176 | tf_op jit(solution)/shard_map/ppermute | solution.py:32
  181.2 3.1 %collective-permute-start.20 = (bf16[64,16,128]{2,0,1:T(8,128)(2,1)S(1)}, bf16[64,16,128]{2,0,1:T(8,128)(2,1)S(1)}, u32[]{:S(2)}, u32[]{:S(2)}) collective-permute-start(bf16[64,16,128]{2,0,1:T(8,128)(2,1)S(1)} %fusion.74), channel_id=1, source_target_pairs={{0,4},{4,0},{1,5},{5,1},{2,6},{6,2},{3,7},{7,3},{8,12},{12,8},{9,1... | collective-permute-start | bytes 786440 | tf_op jit(solution)/shard_map/ppermute | solution.py:32
  184.6 5.7 %collective-permute-done.20 = bf16[64,16,128]{2,0,1:T(8,128)(2,1)S(1)} collective-permute-done((bf16[64,16,128]{2,0,1:T(8,128)(2,1)S(1)}, bf16[64,16,128]{2,0,1:T(8,128)(2,1)S(1)}, u32[]{:S(2)}, u32[]{:S(2)}) %collective-permute-start.20) | collective-permute-done | bytes 262176 | tf_op jit(solution)/shard_map/ppermute | solution.py:32
  191.0 6.3 %collective-permute-done.21 = bf16[64,16,128]{2,0,1:T(8,128)(2,1)S(1)} collective-permute-done((bf16[64,16,128]{2,0,1:T(8,128)(2,1)S(1)}, bf16[64,16,128]{2,0,1:T(8,128)(2,1)S(1)}, u32[]{:S(2)}, u32[]{:S(2)}) %collective-permute-start.21) | collective-permute-done | bytes 262176 | tf_op jit(solution)/shard_map/ppermute | solution.py:32
  197.6 3.4 %collective-permute-start.22 = (bf16[64,16,128]{2,0,1:T(8,128)(2,1)S(1)}, bf16[64,16,128]{2,0,1:T(8,128)(2,1)S(1)}, u32[]{:S(2)}, u32[]{:S(2)}) collective-permute-start(bf16[64,16,128]{2,0,1:T(8,128)(2,1)S(1)} %fusion.72), channel_id=1, source_target_pairs={{0,16},{16,0},{8,24},{24,8},{32,48},{48,32},{40,56},{56,40},{64,80... | collective-permute-start | bytes 786440 | tf_op jit(solution)/shard_map/ppermute | solution.py:32
  201.0 3.7 %collective-permute-start.26 = (bf16[64,16,128]{2,0,1:T(8,128)(2,1)S(1)}, bf16[64,16,128]{2,0,1:T(8,128)(2,1)S(1)}, u32[]{:S(2)}, u32[]{:S(2)}) collective-permute-start(bf16[64,16,128]{2,0,1:T(8,128)(2,1)S(1)} %copy-done.26), channel_id=1, source_target_pairs={{8,0},{16,8},{24,16},{32,24},{40,32},{48,40},{56,48},{64,56},{72,6... | collective-permute-start | bytes 786440 | tf_op jit(solution)/shard_map/ppermute | solution.py:20
  205.0 4.1 %collective-permute-done.22 = bf16[64,16,128]{2,0,1:T(8,128)(2,1)S(1)} collective-permute-done((bf16[64,16,128]{2,0,1:T(8,128)(2,1)S(1)}, bf16[64,16,128]{2,0,1:T(8,128)(2,1)S(1)}, u32[]{:S(2)}, u32[]{:S(2)}) %collective-permute-start.22) | collective-permute-done | bytes 262176 | tf_op jit(solution)/shard_map/ppermute | solution.py:32
  214.5 2.2 gather_fusion.2
  217.2 5.5 %collective-permute-start.24 = (bf16[64,16,128]{2,0,1:T(8,128)(2,1)S(1)}, bf16[64,16,128]{2,0,1:T(8,128)(2,1)S(1)}, u32[]{:S(2)}, u32[]{:S(2)}) collective-permute-start(bf16[64,16,128]{2,0,1:T(8,128)(2,1)S(1)} %fusion.70), channel_id=1, source_target_pairs={{0,64},{64,0},{8,72},{72,8},{16,80},{80,16},{24,88},{88,24},{32,96... | collective-permute-start | bytes 786440 | tf_op jit(solution)/shard_map/ppermute | solution.py:32
  222.7 3.3 %fusion.18 = f32[16,64,128]{2,1,0:T(8,128)S(1)} fusion(bf16[16,8,128,128]{3,2,1,0:T(8,128)(2,1)} %param.7, bf16[16,8,64,128]{3,2,1,0:T(8,128)(2,1)S(1)} %bitcast.396, pred[16,8]{1,0:T(8,128)(4,1)S(1)} %iota_compare_fusion), kind=kOutput, calls=%fused_computation.17 | convolution fusion | flops 269484032 | bytes 6815872 | tf_op jit(solution)/shard_map/rbkw,bkwv->rbv/dot_general | solution.py:54
  (201 shorter events, 97.6 us)
Async XLA Ops:
  23.3 1.6 collective-permute-start
  25.2 9.3 %collective-permute-start.1 = (bf16[64,16,128]{2,0,1:T(8,128)(2,1)S(1)}, bf16[64,16,128]{2,0,1:T(8,128)(2,1)S(1)}, u32[]{:S(2)}, u32[]{:S(2)}) collective-permute-start(bf16[64,16,128]{2,0,1:T(8,128)(2,1)S(1)} %fusion.89), channel_id=1, source_target_pairs={{0,2},{2,0},{1,3},{3,1},{4,6},{6,4},{5,7},{7,5},{8,10},{10,8},{9,1... | collective-permute-start | bytes 786440 | tf_op jit(solution)/shard_map/ppermute | solution.py:32
  27.7 35.7 %collective-permute-start.8 = (bf16[64,16,128]{2,0,1:T(8,128)(2,1)}, bf16[64,16,128]{2,0,1:T(8,128)(2,1)}, u32[]{:S(2)}, u32[]{:S(2)}) collective-permute-start(bf16[64,16,128]{2,0,1:T(8,128)(2,1)} %copy_bitcast_fusion.11), channel_id=1, source_target_pairs={{8,0},{16,8},{24,16},{32,24},{40,32},{48,40},{56,48},{64,56},{72,6... | collective-permute-start | bytes 786440 | tf_op jit(solution)/shard_map/ppermute | solution.py:20
  34.1 29.2 %collective-permute-start.7 = (bf16[64,16,128]{2,0,1:T(8,128)(2,1)}, bf16[64,16,128]{2,0,1:T(8,128)(2,1)}, u32[]{:S(2)}, u32[]{:S(2)}) collective-permute-start(bf16[64,16,128]{2,0,1:T(8,128)(2,1)} %copy_bitcast_fusion.11), channel_id=1, source_target_pairs={{0,8},{8,16},{16,24},{24,32},{32,40},{40,48},{48,56},{56,64},{64,7... | collective-permute-start | bytes 786440 | tf_op jit(solution)/shard_map/ppermute | solution.py:19
  34.8 9.4 %collective-permute-start.2 = (bf16[64,16,128]{2,0,1:T(8,128)(2,1)S(1)}, bf16[64,16,128]{2,0,1:T(8,128)(2,1)S(1)}, u32[]{:S(2)}, u32[]{:S(2)}) collective-permute-start(bf16[64,16,128]{2,0,1:T(8,128)(2,1)S(1)} %fusion.88), channel_id=1, source_target_pairs={{0,4},{4,0},{1,5},{5,1},{2,6},{6,2},{3,7},{7,3},{8,12},{12,8},{9,1... | collective-permute-start | bytes 786440 | tf_op jit(solution)/shard_map/ppermute | solution.py:32
  45.1 7.3 %collective-permute-start.3 = (bf16[64,16,128]{2,0,1:T(8,128)(2,1)}, bf16[64,16,128]{2,0,1:T(8,128)(2,1)}, u32[]{:S(2)}, u32[]{:S(2)}) collective-permute-start(bf16[64,16,128]{2,0,1:T(8,128)(2,1)} %fusion.87), channel_id=1, source_target_pairs={{0,8},{8,0},{16,24},{24,16},{32,40},{40,32},{48,56},{56,48},{64,72... | collective-permute-start | bytes 786440 | tf_op jit(solution)/shard_map/ppermute | solution.py:32
  53.6 8.0 %collective-permute-start.4 = (bf16[64,16,128]{2,0,1:T(8,128)(2,1)S(1)}, bf16[64,16,128]{2,0,1:T(8,128)(2,1)S(1)}, u32[]{:S(2)}, u32[]{:S(2)}) collective-permute-start(bf16[64,16,128]{2,0,1:T(8,128)(2,1)S(1)} %fusion.86), channel_id=1, source_target_pairs={{0,16},{16,0},{8,24},{24,8},{32,48},{48,32},{40,56},{56,40},{64,80... | collective-permute-start | bytes 786440 | tf_op jit(solution)/shard_map/ppermute | solution.py:32
  62.6 7.5 %collective-permute-start.5 = (bf16[64,16,128]{2,0,1:T(8,128)(2,1)}, bf16[64,16,128]{2,0,1:T(8,128)(2,1)}, u32[]{:S(2)}, u32[]{:S(2)}) collective-permute-start(bf16[64,16,128]{2,0,1:T(8,128)(2,1)} %fusion.85), channel_id=1, source_target_pairs={{0,32},{32,0},{8,40},{40,8},{16,48},{48,16},{24,56},{56,24},{64,96... | collective-permute-start | bytes 786440 | tf_op jit(solution)/shard_map/ppermute | solution.py:32
  71.3 8.0 %collective-permute-start.6 = (bf16[64,16,128]{2,0,1:T(8,128)(2,1)S(1)}, bf16[64,16,128]{2,0,1:T(8,128)(2,1)S(1)}, u32[]{:S(2)}, u32[]{:S(2)}) collective-permute-start(bf16[64,16,128]{2,0,1:T(8,128)(2,1)S(1)} %fusion.84), channel_id=1, source_target_pairs={{0,64},{64,0},{8,72},{72,8},{16,80},{80,16},{24,88},{88,24},{32,96... | collective-permute-start | bytes 786440 | tf_op jit(solution)/shard_map/ppermute | solution.py:32
  96.8 1.8 collective-permute-start.9
  98.9 8.4 %collective-permute-start.10 = (bf16[64,16,128]{2,0,1:T(8,128)(2,1)S(1)}, bf16[64,16,128]{2,0,1:T(8,128)(2,1)S(1)}, u32[]{:S(2)}, u32[]{:S(2)}) collective-permute-start(bf16[64,16,128]{2,0,1:T(8,128)(2,1)S(1)} %fusion.82), channel_id=1, source_target_pairs={{0,2},{2,0},{1,3},{3,1},{4,6},{6,4},{5,7},{7,5},{8,10},{10,8},{9,1... | collective-permute-start | bytes 786440 | tf_op jit(solution)/shard_map/ppermute | solution.py:32
  100.7 17.9 %copy-start.10 = (bf16[1,16,2,128,128]{4,3,1,2,0:T(8,128)(2,1)S(1)}, bf16[1,16,2,128,128]{4,3,1,2,0:T(8,128)(2,1)}, u32[]{:S(2)}) copy-start(bf16[1,16,2,128,128]{4,3,1,2,0:T(8,128)(2,1)} %copy-done.9) | copy-start | bytes 3145732
  107.6 9.1 %collective-permute-start.11 = (bf16[64,16,128]{2,0,1:T(8,128)(2,1)S(1)}, bf16[64,16,128]{2,0,1:T(8,128)(2,1)S(1)}, u32[]{:S(2)}, u32[]{:S(2)}) collective-permute-start(bf16[64,16,128]{2,0,1:T(8,128)(2,1)S(1)} %fusion.81), channel_id=1, source_target_pairs={{0,4},{4,0},{1,5},{5,1},{2,6},{6,2},{3,7},{7,3},{8,12},{12,8},{9,1... | collective-permute-start | bytes 786440 | tf_op jit(solution)/shard_map/ppermute | solution.py:32
  111.0 16.6 %copy-start.28 = (bf16[64,16,128]{2,0,1:T(8,128)(2,1)S(1)}, bf16[64,16,128]{2,0,1:T(8,128)(2,1)}, u32[]{:S(2)}) copy-start(bf16[64,16,128]{2,0,1:T(8,128)(2,1)} %copy-done.27) | copy-start | bytes 786436
  111.0 19.3 %copy-start.7 = (bf16[1,16,2,128,128]{4,3,1,2,0:T(8,128)(2,1)S(1)}, bf16[1,16,2,128,128]{4,3,1,2,0:T(8,128)(2,1)}, u32[]{:S(2)}) copy-start(bf16[1,16,2,128,128]{4,3,1,2,0:T(8,128)(2,1)} %copy-done.6) | copy-start | bytes 3145732
  117.0 6.7 %collective-permute-start.12 = (bf16[64,16,128]{2,0,1:T(8,128)(2,1)S(1)}, bf16[64,16,128]{2,0,1:T(8,128)(2,1)S(1)}, u32[]{:S(2)}, u32[]{:S(2)}) collective-permute-start(bf16[64,16,128]{2,0,1:T(8,128)(2,1)S(1)} %fusion.80), channel_id=1, source_target_pairs={{0,8},{8,0},{16,24},{24,16},{32,40},{40,32},{48,56},{56,48},{64,72... | collective-permute-start | bytes 786440 | tf_op jit(solution)/shard_map/ppermute | solution.py:32
  123.9 11.9 %collective-permute-start.13 = (bf16[64,16,128]{2,0,1:T(8,128)(2,1)S(1)}, bf16[64,16,128]{2,0,1:T(8,128)(2,1)S(1)}, u32[]{:S(2)}, u32[]{:S(2)}) collective-permute-start(bf16[64,16,128]{2,0,1:T(8,128)(2,1)S(1)} %fusion.79), channel_id=1, source_target_pairs={{0,16},{16,0},{8,24},{24,8},{32,48},{48,32},{40,56},{56,40},{64,80... | collective-permute-start | bytes 786440 | tf_op jit(solution)/shard_map/ppermute | solution.py:32
  127.5 11.8 %collective-permute-start.17 = (bf16[64,16,128]{2,0,1:T(8,128)(2,1)S(1)}, bf16[64,16,128]{2,0,1:T(8,128)(2,1)S(1)}, u32[]{:S(2)}, u32[]{:S(2)}) collective-permute-start(bf16[64,16,128]{2,0,1:T(8,128)(2,1)S(1)} %copy-done.28), channel_id=1, source_target_pairs={{8,0},{16,8},{24,16},{32,24},{40,32},{48,40},{56,48},{64,56},{72,6... | collective-permute-start | bytes 786440 | tf_op jit(solution)/shard_map/ppermute | solution.py:20
  130.3 9.7 %collective-permute-start.16 = (bf16[64,16,128]{2,0,1:T(8,128)(2,1)S(1)}, bf16[64,16,128]{2,0,1:T(8,128)(2,1)S(1)}, u32[]{:S(2)}, u32[]{:S(2)}) collective-permute-start(bf16[64,16,128]{2,0,1:T(8,128)(2,1)S(1)} %copy-done.28), channel_id=1, source_target_pairs={{0,8},{8,16},{16,24},{24,32},{32,40},{40,48},{48,56},{56,64},{64,7... | collective-permute-start | bytes 786440 | tf_op jit(solution)/shard_map/ppermute | solution.py:19
  136.8 8.9 %collective-permute-start.14 = (bf16[64,16,128]{2,0,1:T(8,128)(2,1)}, bf16[64,16,128]{2,0,1:T(8,128)(2,1)}, u32[]{:S(2)}, u32[]{:S(2)}) collective-permute-start(bf16[64,16,128]{2,0,1:T(8,128)(2,1)} %fusion.78), channel_id=1, source_target_pairs={{0,32},{32,0},{8,40},{40,8},{16,48},{48,16},{24,56},{56,24},{64,96... | collective-permute-start | bytes 786440 | tf_op jit(solution)/shard_map/ppermute | solution.py:32
  146.9 8.0 %collective-permute-start.15 = (bf16[64,16,128]{2,0,1:T(8,128)(2,1)S(1)}, bf16[64,16,128]{2,0,1:T(8,128)(2,1)S(1)}, u32[]{:S(2)}, u32[]{:S(2)}) collective-permute-start(bf16[64,16,128]{2,0,1:T(8,128)(2,1)S(1)} %fusion.77), channel_id=1, source_target_pairs={{0,64},{64,0},{8,72},{72,8},{16,80},{80,16},{24,88},{88,24},{32,96... | collective-permute-start | bytes 786440 | tf_op jit(solution)/shard_map/ppermute | solution.py:32
  170.7 1.6 collective-permute-start.18
  172.5 8.4 %collective-permute-start.19 = (bf16[64,16,128]{2,0,1:T(8,128)(2,1)S(1)}, bf16[64,16,128]{2,0,1:T(8,128)(2,1)S(1)}, u32[]{:S(2)}, u32[]{:S(2)}) collective-permute-start(bf16[64,16,128]{2,0,1:T(8,128)(2,1)S(1)} %fusion.75), channel_id=1, source_target_pairs={{0,2},{2,0},{1,3},{3,1},{4,6},{6,4},{5,7},{7,5},{8,10},{10,8},{9,1... | collective-permute-start | bytes 786440 | tf_op jit(solution)/shard_map/ppermute | solution.py:32
  181.2 9.1 %collective-permute-start.20 = (bf16[64,16,128]{2,0,1:T(8,128)(2,1)S(1)}, bf16[64,16,128]{2,0,1:T(8,128)(2,1)S(1)}, u32[]{:S(2)}, u32[]{:S(2)}) collective-permute-start(bf16[64,16,128]{2,0,1:T(8,128)(2,1)S(1)} %fusion.74), channel_id=1, source_target_pairs={{0,4},{4,0},{1,5},{5,1},{2,6},{6,2},{3,7},{7,3},{8,12},{12,8},{9,1... | collective-permute-start | bytes 786440 | tf_op jit(solution)/shard_map/ppermute | solution.py:32
  184.6 16.4 %copy-start.26 = (bf16[64,16,128]{2,0,1:T(8,128)(2,1)S(1)}, bf16[64,16,128]{2,0,1:T(8,128)(2,1)}, u32[]{:S(2)}) copy-start(bf16[64,16,128]{2,0,1:T(8,128)(2,1)} %copy-done.25) | copy-start | bytes 786436
  184.6 20.1 %copy-start.8 = (bf16[1,16,2,128,128]{4,3,1,2,0:T(8,128)(2,1)S(1)}, bf16[1,16,2,128,128]{4,3,1,2,0:T(8,128)(2,1)}, u32[]{:S(2)}) copy-start(bf16[1,16,2,128,128]{4,3,1,2,0:T(8,128)(2,1)} %copy-done.6) | copy-start | bytes 3145732
  190.6 6.7 %collective-permute-start.21 = (bf16[64,16,128]{2,0,1:T(8,128)(2,1)S(1)}, bf16[64,16,128]{2,0,1:T(8,128)(2,1)S(1)}, u32[]{:S(2)}, u32[]{:S(2)}) collective-permute-start(bf16[64,16,128]{2,0,1:T(8,128)(2,1)S(1)} %fusion.73), channel_id=1, source_target_pairs={{0,8},{8,0},{16,24},{24,16},{32,40},{40,32},{48,56},{56,48},{64,72... | collective-permute-start | bytes 786440 | tf_op jit(solution)/shard_map/ppermute | solution.py:32
  197.6 11.5 %collective-permute-start.22 = (bf16[64,16,128]{2,0,1:T(8,128)(2,1)S(1)}, bf16[64,16,128]{2,0,1:T(8,128)(2,1)S(1)}, u32[]{:S(2)}, u32[]{:S(2)}) collective-permute-start(bf16[64,16,128]{2,0,1:T(8,128)(2,1)S(1)} %fusion.72), channel_id=1, source_target_pairs={{0,16},{16,0},{8,24},{24,8},{32,48},{48,32},{40,56},{56,40},{64,80... | collective-permute-start | bytes 786440 | tf_op jit(solution)/shard_map/ppermute | solution.py:32
  201.0 11.8 %collective-permute-start.26 = (bf16[64,16,128]{2,0,1:T(8,128)(2,1)S(1)}, bf16[64,16,128]{2,0,1:T(8,128)(2,1)S(1)}, u32[]{:S(2)}, u32[]{:S(2)}) collective-permute-start(bf16[64,16,128]{2,0,1:T(8,128)(2,1)S(1)} %copy-done.26), channel_id=1, source_target_pairs={{8,0},{16,8},{24,16},{32,24},{40,32},{48,40},{56,48},{64,56},{72,6... | collective-permute-start | bytes 786440 | tf_op jit(solution)/shard_map/ppermute | solution.py:20
  204.7 9.7 %collective-permute-start.25 = (bf16[64,16,128]{2,0,1:T(8,128)(2,1)S(1)}, bf16[64,16,128]{2,0,1:T(8,128)(2,1)S(1)}, u32[]{:S(2)}, u32[]{:S(2)}) collective-permute-start(bf16[64,16,128]{2,0,1:T(8,128)(2,1)S(1)} %copy-done.26), channel_id=1, source_target_pairs={{0,8},{8,16},{16,24},{24,32},{32,40},{40,48},{48,56},{56,64},{64,7... | collective-permute-start | bytes 786440 | tf_op jit(solution)/shard_map/ppermute | solution.py:19
  209.3 7.6 %collective-permute-start.23 = (bf16[64,16,128]{2,0,1:T(8,128)(2,1)S(1)}, bf16[64,16,128]{2,0,1:T(8,128)(2,1)S(1)}, u32[]{:S(2)}, u32[]{:S(2)}) collective-permute-start(bf16[64,16,128]{2,0,1:T(8,128)(2,1)S(1)} %fusion.71), channel_id=1, source_target_pairs={{0,32},{32,0},{8,40},{40,8},{16,48},{48,16},{24,56},{56,24},{64,96... | collective-permute-start | bytes 786440 | tf_op jit(solution)/shard_map/ppermute | solution.py:32
  217.2 9.9 %collective-permute-start.24 = (bf16[64,16,128]{2,0,1:T(8,128)(2,1)S(1)}, bf16[64,16,128]{2,0,1:T(8,128)(2,1)S(1)}, u32[]{:S(2)}, u32[]{:S(2)}) collective-permute-start(bf16[64,16,128]{2,0,1:T(8,128)(2,1)S(1)} %fusion.70), channel_id=1, source_target_pairs={{0,64},{64,0},{8,72},{72,8},{16,80},{80,16},{24,88},{88,24},{32,96... | collective-permute-start | bytes 786440 | tf_op jit(solution)/shard_map/ppermute | solution.py:32
  (36 other events, 181.8 us)
where the time goes:
time: 230 us; the launch traced here: 228 us
  waiting for transfers between devices  70.7 us (31%)
  matrix products  54.7 us (24%)
  starting transfers between devices  53.3 us (23%)
  local copies, waits for them, and re-layouts  45.5 us (20%)
  other arithmetic  3.21 us (1%)
    ppermute x21, waiting for transfers between devices, partner_2(): return lax.ppermute(block, axis, route)  64.5 us
    ppermute x21, starting transfers between devices, partner_2(): return lax.ppermute(block, axis, route)  40.3 us
    dot_general x30, matrix products, apply_level(): jnp.einsum('rbw,bwv->rbv', partner, factor[:, 1], preferred_element_type=...  22.9 us
    dot_general x30, matrix products, apply_level(): jnp.einsum('rbw,bwv->rbv', mixed, factor[:, 0], preferred_element_type=jn...  22 us
    rev x10, local copies, waits for them, and re-layouts, flip_local(): return grouped[:, :, ::-1].reshape(rhs_count, blocks, width)  14.8 us
    ppermute x3, starting transfers between devices, extended(): after = lax.ppermute(leading, axis, down)  13 us
    unnamed x90, local copies, waits for them, and re-layouts  10.6 us
    dot_general x3, matrix products, near_field(): jnp.einsum('rbkw,bkwv->rbv', taken, near_blocks, preferred_element_type=j...  9.78 us
  transfers between devices with their start and end apart: 27, of which 21 were waited for; matrix products, arithmetic and copies ran while one was open for 17% of the time, Pallas kernels for 0%

commit v1 on v0

v1 whole, which is shorter than its diff:
```python
import functools

import jax
import jax.numpy as jnp
from jax import lax
from jax.experimental import pallas as pl
from jax.experimental.pallas import tpu as pltpu
from jax.sharding import PartitionSpec as P

ITERS = 3


coupling = 0.4


def exchange(block, axis, distance):
    count = lax.axis_size(axis)
    route = [(i, i ^ (1 << distance)) for i in range(count)]
    return lax.ppermute(block, axis, route)


def shifted(value, axis, step):
    count = lax.axis_size(axis)
    return lax.ppermute(value, axis, [(i, (i + step) % count) for i in range(count)])


def pair_product(own, partner, factor):
    both = jnp.concatenate([own, partner], axis=-1)
    weights = factor.reshape(2 * factor.shape[-2], factor.shape[-1])
    return jnp.dot(both, weights, preferred_element_type=jnp.float32)


def call(kernel, out_shape, operands, flops, scratch=()):
    in_specs = [
        pl.BlockSpec(memory_space=pltpu.SMEM if op.dtype == jnp.int32 else pltpu.VMEM)
        for op in operands
    ]
    size = sum(op.size * op.dtype.itemsize for op in operands)
    return pl.pallas_call(
        kernel,
        out_shape=out_shape,
        in_specs=in_specs,
        scratch_shapes=scratch,
        out_specs=jax.tree.map(lambda _: pl.BlockSpec(memory_space=pltpu.VMEM), out_shape),
        cost_estimate=pl.CostEstimate(flops=flops, bytes_accessed=size, transcendentals=0),
        compiler_params=pltpu.CompilerParams(vmem_limit_bytes=24 * 2**20),
    )(*operands)


def split_kernel(start, rows_ref, out_ref):
    blocks, _, width = out_ref.shape
    for b in range(blocks):
        out_ref[b] = rows_ref[:, (start + b) * width:(start + b + 1) * width]


def local_kernel(levels, z_ref, *refs):
    factors, out_ref = refs[:levels], refs[levels]
    blocks = z_ref.shape[0]
    mixed = [z_ref[b] for b in range(blocks)]
    for level, factor in enumerate(factors):
        stride = 1 << level
        mixed = [
            pair_product(mixed[b], mixed[b ^ stride], factor[b]).astype(jnp.bfloat16)
            for b in range(blocks)
        ]
    for b in range(blocks):
        out_ref[b] = mixed[b]


def level_kernel(own_ref, partner_ref, factor_ref, out_ref):
    for b in range(own_ref.shape[0]):
        out_ref[b] = pair_product(own_ref[b], partner_ref[b], factor_ref[b]).astype(jnp.bfloat16)


def near_kernel(start, index_ref, count_ref, *refs):
    pieces, near_ref, out_ref, window = refs[:-3], refs[-3], refs[-2], refs[-1]
    blocks, slots, width, _ = near_ref.shape
    half = pieces[0].shape[0]
    for i, piece in enumerate(pieces):
        window[i * half:(i + 1) * half] = piece[...]
    unused = len(pieces) * half
    window[unused] = jnp.zeros(window.shape[1:], window.dtype)
    for b in range(blocks):
        count = count_ref[start + b]
        taken = [
            window[jnp.where(k < count, index_ref[start + b, k], unused)] for k in range(slots)
        ]
        out_ref[b] = jnp.dot(
            jnp.concatenate(taken, axis=-1),
            near_ref[b].reshape(slots * width, width),
            preferred_element_type=jnp.float32,
        )


def last_kernel(own_ref, partner_ref, factor_ref, near_ref, source_ref, out_ref):
    for b in range(own_ref.shape[0]):
        mixed = pair_product(own_ref[b], partner_ref[b], factor_ref[b])
        mixed = mixed.astype(jnp.bfloat16).astype(jnp.float32)
        total = source_ref[b].astype(jnp.float32) - coupling * (mixed + near_ref[b])
        out_ref[b] = total.astype(jnp.bfloat16)


def join_kernel(*refs):
    parts, out_ref = refs[:-1], refs[-1]
    at = 0
    for part in parts:
        for b in range(part.shape[0]):
            width = part.shape[-1]
            out_ref[:, at:at + width] = part[b]
            at += width


def per_device(right_side, level_pairs, near_blocks, near_index, near_count):
    rhs_count = right_side.shape[0]
    blocks, slots, width, _ = near_blocks.shape
    levels = level_pairs.shape[0]
    level_bits = lax.axis_size("level").bit_length() - 1
    patch_bits = lax.axis_size("patch").bit_length() - 1
    local_levels = levels - level_bits - patch_bits
    half = 1 << local_levels
    chains = blocks // half
    piece = jax.ShapeDtypeStruct((half, rhs_count, width), jnp.bfloat16)
    near_shape = jax.ShapeDtypeStruct((half, rhs_count, width), jnp.float32)
    level_flops = 4 * half * rhs_count * width * width
    remote = [("level", i) for i in range(level_bits)] + [("patch", i) for i in range(patch_bits)]

    def factor(level, chain):
        return level_pairs[level, chain * half:(chain + 1) * half]

    near_parts = [near_blocks[c * half:(c + 1) * half] for c in range(chains)]
    source = [
        call(functools.partial(split_kernel, c * half), piece, (right_side,), 0)
        for c in range(chains)
    ]
    current = source
    window_shape = pltpu.VMEM((3 * blocks + 1, rhs_count, width), jnp.bfloat16)
    for sweep in range(ITERS):
        below = [shifted(current[c], "patch", 1) for c in range(chains)]
        above = [shifted(current[c], "patch", -1) for c in range(chains)]
        mixed = [
            call(
                functools.partial(local_kernel, local_levels),
                piece,
                (current[c], *[factor(i, c) for i in range(local_levels)]),
                local_levels * level_flops,
            )
            for c in range(chains)
        ]
        near = [
            call(
                functools.partial(near_kernel, c * half),
                near_shape,
                (near_index, near_count, *below, *current, *above, near_parts[c]),
                2 * half * slots * rhs_count * width * width,
                (window_shape,),
            )
            for c in range(chains)
        ]
        for i, (axis, bit) in enumerate(remote):
            partner = [exchange(mixed[c], axis, bit) for c in range(chains)]
            for c in range(chains):
                operands = (mixed[c], partner[c], factor(local_levels + i, c))
                if i < len(remote) - 1:
                    mixed[c] = call(level_kernel, piece, operands, level_flops)
                else:
                    mixed[c] = call(
                        last_kernel, piece, (*operands, near[c], source[c]), level_flops
                    )
        current = mixed
    return call(
        join_kernel,
        jax.ShapeDtypeStruct((rhs_count, blocks * width), jnp.bfloat16),
        current,
        0,
    )


def solution(mesh):
    in_specs = (
        P(None, ("patch", "level")),
        P(None, ("patch", "level"), None, None, None),
        P(("patch", "level"), None, None, None),
        P(("patch", "level"), None),
        P(("patch", "level")),
    )
    out_specs = P(None, ("patch", "level"))
    return jax.shard_map(
        per_device, mesh=mesh, in_specs=in_specs, out_specs=out_specs, check_vma=False
    )
```

time: 230 us -> 175 us (0.76)
  matrix products: 54.7 us -> 0 us
  local copies, waits for them, and re-layouts: 45.5 us -> 12.1 us
  starting transfers between devices: 53.3 us -> 84.1 us
  Pallas kernels: 0 us -> 24.5 us
  waiting for transfers between devices: 70.7 us -> 52.6 us
  other arithmetic: 3.21 us -> 0 us
    dot_general x63 -> x0, matrix products: 54.7 us -> none  [the longest x30 22.9 us: apply_level(): jnp.einsum('rbw,bwv->rbv', partner, factor[:, 1], preferred_element_type=...]
    ppermute x27 -> x54, starting transfers between devices: 53.3 us -> 84.1 us  [the longest x42 52.1 us: exchange(): return lax.ppermute(block, axis, route)]
    pallas_call x0 -> x57, Pallas kernels: none -> 24.5 us  [call(): pl.pallas_call(kernel, out_shape=out_shape, in_specs=in_specs, scratch_sh...]
    ppermute x27 -> x54, waiting for transfers between devices: 70.7 us -> 52.6 us  [the longest x42 52.4 us: exchange(): return lax.ppermute(block, axis, route)]
    rev x10 -> x0, local copies, waits for them, and re-layouts: 14.8 us -> none  [flip_local(): return grouped[:, :, ::-1].reshape(rhs_count, blocks, width)]
    gather x3 -> x0, local copies, waits for them, and re-layouts: 8.82 us -> none  [near_field(): taken = window[:, near_index]]
    unnamed x90 -> x85, local copies, waits for them, and re-layouts: 10.6 us -> 3.37 us
    slice x1, local copies, waits for them, and re-layouts: 7.57 us -> 1.72 us  [per_device(): near_parts = [near_blocks[c * half:(c + 1) * half] for c in range(chains)]]
  transfers between devices with their start and end apart: 27 -> 54, of which waited for: 21 -> 23; matrix products, arithmetic and copies ran while one was open for 17% -> 2% of each run, Pallas kernels for 0% -> 13%
where the time goes in v1:
time: 175 us; the launch traced here: 174 us
  starting transfers between devices  84.1 us (48%)
  waiting for transfers between devices  52.6 us (30%)
  Pallas kernels  24.5 us (14%)
  local copies, waits for them, and re-layouts  12.1 us (7%)
    ppermute x42, waiting for transfers between devices, exchange(): return lax.ppermute(block, axis, route)  52.4 us
    ppermute x42, starting transfers between devices, exchange(): return lax.ppermute(block, axis, route)  52.1 us
    ppermute x12, starting transfers between devices, shifted(): lax.ppermute(value, axis, [(i, (i + step) % count) for i in range(count)])  32 us
    pallas_call x57, Pallas kernels, call(): pl.pallas_call(kernel, out_shape=out_shape, in_specs=in_specs, scratch_sh...  24.5 us
    squeeze x2, local copies, waits for them, and re-layouts, factor(): return level_pairs[level, chain * half:(chain + 1) * half]  7.01 us
  transfers between devices with their start and end apart: 54, of which 23 were waited for; matrix products, arithmetic and copies ran while one was open for 2% of the time, Pallas kernels for 13%

profile of v1, /device:TPU:0, one launch (start us, length us, event | category | flops | bytes accessed | tf_op | source)
XLA Modules:
  0.0 174.4 jit_solution(230907740186492678)
XLA Ops:
  0.0 5.9 %slice_bitcast_fusion = (bf16[8,2,128,128]{3,2,1,0:T(8,128)(2,1)}, bf16[8,2,128,128]{3,2,1,0:T(8,128)(2,1)S(1)}, bf16[8,2,128,128]{3,2,1,0:T(8,128)(2,1)S(1)}, b...) fusion(bf16[10,16,2,128,128]{4,3,2,1,0:T(8,128)(2,1)} %param.6), kind=kLoop, calls=%fused_computation | loop fusion | bytes 19922944 | tf_op jit(solution)/shard_map/squeeze | solution.py:128
  10.8 3.9 %collective-permute-done.20.partner_ref = bf16[8,64,128]{2,1,0:T(8,128)(2,1)S(1)} collective-permute-done((bf16[8,64,128]{2,1,0:T(8,128)(2,1)S(1)}, bf16[8,64,128]{2,1,0:T(8,128)(2,1)S(1)}, u32[]{:S(2)}, u32[]{:S(2)}) %collective-permute-start.20) | collective-permute-done | bytes 131104 | tf_op jit(solution)/shard_map/ppermute | solution.py:19
  15.0 3.2 %collective-permute-start.21 = (bf16[8,64,128]{2,1,0:T(8,128)(2,1)S(1)}, bf16[8,64,128]{2,1,0:T(8,128)(2,1)S(1)}, u32[]{:S(2)}, u32[]{:S(2)}) collective-permute-start(bf16[8,64,128]{2,1,0:T(8,128)(2,1)S(1)} %shard_map.75.own_ref), channel_id=1, source_target_pairs={{0,4},{1,5},{2,6},{3,7},{4,0},{5,1},{6,2},{7,3},{8,12},{9,13},{10,... | collective-permute-start | bytes 393224 | tf_op jit(solution)/shard_map/ppermute | solution.py:19
  20.2 2.7 %collective-permute-done.21.partner_ref = bf16[8,64,128]{2,1,0:T(8,128)(2,1)S(1)} collective-permute-done((bf16[8,64,128]{2,1,0:T(8,128)(2,1)S(1)}, bf16[8,64,128]{2,1,0:T(8,128)(2,1)S(1)}, u32[]{:S(2)}, u32[]{:S(2)}) %collective-permute-start.21) | collective-permute-done | bytes 131104 | tf_op jit(solution)/shard_map/ppermute | solution.py:19
  29.2 4.4 %collective-permute-start.23 = (bf16[8,64,128]{2,1,0:T(8,128)(2,1)S(1)}, bf16[8,64,128]{2,1,0:T(8,128)(2,1)S(1)}, u32[]{:S(2)}, u32[]{:S(2)}) collective-permute-start(bf16[8,64,128]{2,1,0:T(8,128)(2,1)S(1)} %shard_map.77.own_ref), channel_id=1, source_target_pairs={{0,16},{8,24},{16,0},{24,8},{32,48},{40,56},{48,32},{56,40},{64,80... | collective-permute-start | bytes 393224 | tf_op jit(solution)/shard_map/ppermute | solution.py:19
  33.9 2.3 %collective-permute-start.4 = (bf16[8,64,128]{2,1,0:T(8,128)(2,1)S(1)}, bf16[8,64,128]{2,1,0:T(8,128)(2,1)S(1)}, u32[]{:S(2)}, u32[]{:S(2)}) collective-permute-start(bf16[8,64,128]{2,1,0:T(8,128)(2,1)S(1)} %shard_map.60.own_ref), channel_id=1, source_target_pairs={{0,16},{8,24},{16,0},{24,8},{32,48},{40,56},{48,32},{56,40},{64,80... | collective-permute-start | bytes 393224 | tf_op jit(solution)/shard_map/ppermute | solution.py:19
  36.2 4.1 %collective-permute-start.10 = (bf16[8,64,128]{2,1,0:T(8,128)(2,1)S(1)}, bf16[8,64,128]{2,1,0:T(8,128)(2,1)S(1)}, u32[]{:S(2)}, u32[]{:S(2)}) collective-permute-start(bf16[8,64,128]{2,1,0:T(8,128)(2,1)S(1)} %shard_map.63.refs_3_.z_ref.source_ref), channel_id=1, source_target_pairs={{0,120},{8,0},{16,8},{24,16},{32,24},{40,32},{48,40},{56,48},{64,5... | collective-permute-start | bytes 393224 | tf_op jit(solution)/shard_map/ppermute | solution.py:24
  46.8 6.4 %collective-permute-start.9 = (bf16[8,64,128]{2,1,0:T(8,128)(2,1)S(1)}, bf16[8,64,128]{2,1,0:T(8,128)(2,1)}, u32[]{:S(2)}, u32[]{:S(2)}) collective-permute-start(bf16[8,64,128]{2,1,0:T(8,128)(2,1)S(1)} %shard_map.55.z_ref.refs_2_.source_ref), channel_id=1, source_target_pairs={{0,120},{8,0},{16,8},{24,16},{32,24},{40,32},{48,40},{56,48},{64,5... | collective-permute-start | bytes 393224 | tf_op jit(solution)/shard_map/ppermute | solution.py:24
  55.0 3.5 %collective-permute-start.6 = (bf16[8,64,128]{2,1,0:T(8,128)(2,1)S(1)}, bf16[8,64,128]{2,1,0:T(8,128)(2,1)}, u32[]{:S(2)}, u32[]{:S(2)}) collective-permute-start(bf16[8,64,128]{2,1,0:T(8,128)(2,1)S(1)} %shard_map.62.own_ref), channel_id=1, source_target_pairs={{0,64},{8,72},{16,80},{24,88},{32,96},{40,104},{48,112},{56,120},{... | collective-permute-start | bytes 393224 | tf_op jit(solution)/shard_map/ppermute | solution.py:19
  73.9 3.7 %collective-permute-done.38.partner_ref = bf16[8,64,128]{2,1,0:T(8,128)(2,1)S(1)} collective-permute-done((bf16[8,64,128]{2,1,0:T(8,128)(2,1)S(1)}, bf16[8,64,128]{2,1,0:T(8,128)(2,1)S(1)}, u32[]{:S(2)}, u32[]{:S(2)}) %collective-permute-start.38) | collective-permute-done | bytes 131104 | tf_op jit(solution)/shard_map/ppermute | solution.py:19
  77.8 3.3 %collective-permute-start.39 = (bf16[8,64,128]{2,1,0:T(8,128)(2,1)S(1)}, bf16[8,64,128]{2,1,0:T(8,128)(2,1)S(1)}, u32[]{:S(2)}, u32[]{:S(2)}) collective-permute-start(bf16[8,64,128]{2,1,0:T(8,128)(2,1)S(1)} %shard_map.93.own_ref), channel_id=1, source_target_pairs={{0,4},{1,5},{2,6},{3,7},{4,0},{5,1},{6,2},{7,3},{8,12},{9,13},{10,... | collective-permute-start | bytes 393224 | tf_op jit(solution)/shard_map/ppermute | solution.py:19
  83.0 2.3 %collective-permute-done.39.partner_ref = bf16[8,64,128]{2,1,0:T(8,128)(2,1)S(1)} collective-permute-done((bf16[8,64,128]{2,1,0:T(8,128)(2,1)S(1)}, bf16[8,64,128]{2,1,0:T(8,128)(2,1)S(1)}, u32[]{:S(2)}, u32[]{:S(2)}) %collective-permute-start.39) | collective-permute-done | bytes 131104 | tf_op jit(solution)/shard_map/ppermute | solution.py:19
  85.7 2.2 %collective-permute-done.13.partner_ref = bf16[8,64,128]{2,1,0:T(8,128)(2,1)S(1)} collective-permute-done((bf16[8,64,128]{2,1,0:T(8,128)(2,1)S(1)}, bf16[8,64,128]{2,1,0:T(8,128)(2,1)S(1)}, u32[]{:S(2)}, u32[]{:S(2)}) %collective-permute-start.13) | collective-permute-done | bytes 131104 | tf_op jit(solution)/shard_map/ppermute | solution.py:19
  88.2 3.8 %collective-permute-done.40.partner_ref = bf16[8,64,128]{2,1,0:T(8,128)(2,1)S(1)} collective-permute-done((bf16[8,64,128]{2,1,0:T(8,128)(2,1)S(1)}, bf16[8,64,128]{2,1,0:T(8,128)(2,1)S(1)}, u32[]{:S(2)}, u32[]{:S(2)}) %collective-permute-start.40) | collective-permute-done | bytes 131104 | tf_op jit(solution)/shard_map/ppermute | solution.py:19
  92.3 2.5 %collective-permute-done.14.partner_ref = bf16[8,64,128]{2,1,0:T(8,128)(2,1)S(1)} collective-permute-done((bf16[8,64,128]{2,1,0:T(8,128)(2,1)S(1)}, bf16[8,64,128]{2,1,0:T(8,128)(2,1)S(1)}, u32[]{:S(2)}, u32[]{:S(2)}) %collective-permute-start.14) | collective-permute-done | bytes 131104 | tf_op jit(solution)/shard_map/ppermute | solution.py:19
  96.1 2.6 %collective-permute-done.41.partner_ref = bf16[8,64,128]{2,1,0:T(8,128)(2,1)S(1)} collective-permute-done((bf16[8,64,128]{2,1,0:T(8,128)(2,1)S(1)}, bf16[8,64,128]{2,1,0:T(8,128)(2,1)S(1)}, u32[]{:S(2)}, u32[]{:S(2)}) %collective-permute-start.41) | collective-permute-done | bytes 131104 | tf_op jit(solution)/shard_map/ppermute | solution.py:19
  99.1 2.5 %collective-permute-done.15.partner_ref = bf16[8,64,128]{2,1,0:T(8,128)(2,1)S(1)} collective-permute-done((bf16[8,64,128]{2,1,0:T(8,128)(2,1)S(1)}, bf16[8,64,128]{2,1,0:T(8,128)(2,1)S(1)}, u32[]{:S(2)}, u32[]{:S(2)}) %collective-permute-start.15) | collective-permute-done | bytes 131104 | tf_op jit(solution)/shard_map/ppermute | solution.py:19
  102.0 5.3 %collective-permute-start.28 = (bf16[8,64,128]{2,1,0:T(8,128)(2,1)S(1)}, bf16[8,64,128]{2,1,0:T(8,128)(2,1)S(1)}, u32[]{:S(2)}, u32[]{:S(2)}) collective-permute-start(bf16[8,64,128]{2,1,0:T(8,128)(2,1)S(1)} %shard_map.81.refs_3_.z_ref), channel_id=1, source_target_pairs={{0,120},{8,0},{16,8},{24,16},{32,24},{40,32},{48,40},{56,48},{64,5... | collective-permute-start | bytes 393224 | tf_op jit(solution)/shard_map/ppermute | solution.py:24
  107.4 5.3 %collective-permute-start.27 = (bf16[8,64,128]{2,1,0:T(8,128)(2,1)S(1)}, bf16[8,64,128]{2,1,0:T(8,128)(2,1)S(1)}, u32[]{:S(2)}, u32[]{:S(2)}) collective-permute-start(bf16[8,64,128]{2,1,0:T(8,128)(2,1)S(1)} %shard_map.65.z_ref.refs_2_), channel_id=1, source_target_pairs={{0,120},{8,0},{16,8},{24,16},{32,24},{40,32},{48,40},{56,48},{64,5... | collective-permute-start | bytes 393224 | tf_op jit(solution)/shard_map/ppermute | solution.py:24
  113.7 3.1 %collective-permute-start.17 = (bf16[8,64,128]{2,1,0:T(8,128)(2,1)S(1)}, bf16[8,64,128]{2,1,0:T(8,128)(2,1)S(1)}, u32[]{:S(2)}, u32[]{:S(2)}) collective-permute-start(bf16[8,64,128]{2,1,0:T(8,128)(2,1)S(1)} %shard_map.72.own_ref), channel_id=1, source_target_pairs={{0,64},{8,72},{16,80},{24,88},{32,96},{40,104},{48,112},{56,120},{... | collective-permute-start | bytes 393224 | tf_op jit(solution)/shard_map/ppermute | solution.py:19
  123.2 2.1 %collective-permute-start.48 = (bf16[8,64,128]{2,1,0:T(8,128)(2,1)S(1)}, bf16[8,64,128]{2,1,0:T(8,128)(2,1)S(1)}, u32[]{:S(2)}, u32[]{:S(2)}) collective-permute-start(bf16[8,64,128]{2,1,0:T(8,128)(2,1)S(1)} %shard_map.103.own_ref), channel_id=1, source_target_pairs={{0,2},{1,3},{2,0},{3,1},{4,6},{5,7},{6,4},{7,5},{8,10},{9,11},{10,... | collective-permute-start | bytes 393224 | tf_op jit(solution)/shard_map/ppermute | solution.py:19
  126.3 3.3 %collective-permute-done.48.partner_ref = bf16[8,64,128]{2,1,0:T(8,128)(2,1)S(1)} collective-permute-done((bf16[8,64,128]{2,1,0:T(8,128)(2,1)S(1)}, bf16[8,64,128]{2,1,0:T(8,128)(2,1)S(1)}, u32[]{:S(2)}, u32[]{:S(2)}) %collective-permute-start.48) | collective-permute-done | bytes 131104 | tf_op jit(solution)/shard_map/ppermute | solution.py:19
  129.9 3.6 %collective-permute-start.49 = (bf16[8,64,128]{2,1,0:T(8,128)(2,1)S(1)}, bf16[8,64,128]{2,1,0:T(8,128)(2,1)S(1)}, u32[]{:S(2)}, u32[]{:S(2)}) collective-permute-start(bf16[8,64,128]{2,1,0:T(8,128)(2,1)S(1)} %shard_map.104.own_ref), channel_id=1, source_target_pairs={{0,4},{1,5},{2,6},{3,7},{4,0},{5,1},{6,2},{7,3},{8,12},{9,13},{10,... | collective-permute-start | bytes 393224 | tf_op jit(solution)/shard_map/ppermute | solution.py:19
  135.7 2.2 %collective-permute-done.49.partner_ref = bf16[8,64,128]{2,1,0:T(8,128)(2,1)S(1)} collective-permute-done((bf16[8,64,128]{2,1,0:T(8,128)(2,1)S(1)}, bf16[8,64,128]{2,1,0:T(8,128)(2,1)S(1)}, u32[]{:S(2)}, u32[]{:S(2)}) %collective-permute-start.49) | collective-permute-done | bytes 131104 | tf_op jit(solution)/shard_map/ppermute | solution.py:19
  138.2 2.3 %collective-permute-done.31.partner_ref = bf16[8,64,128]{2,1,0:T(8,128)(2,1)S(1)} collective-permute-done((bf16[8,64,128]{2,1,0:T(8,128)(2,1)S(1)}, bf16[8,64,128]{2,1,0:T(8,128)(2,1)S(1)}, u32[]{:S(2)}, u32[]{:S(2)}) %collective-permute-start.31) | collective-permute-done | bytes 131104 | tf_op jit(solution)/shard_map/ppermute | solution.py:19
  140.8 3.7 %collective-permute-done.50.partner_ref = bf16[8,64,128]{2,1,0:T(8,128)(2,1)S(1)} collective-permute-done((bf16[8,64,128]{2,1,0:T(8,128)(2,1)S(1)}, bf16[8,64,128]{2,1,0:T(8,128)(2,1)S(1)}, u32[]{:S(2)}, u32[]{:S(2)}) %collective-permute-start.50) | collective-permute-done | bytes 131104 | tf_op jit(solution)/shard_map/ppermute | solution.py:19
  144.9 2.5 %collective-permute-done.32.partner_ref = bf16[8,64,128]{2,1,0:T(8,128)(2,1)S(1)} collective-permute-done((bf16[8,64,128]{2,1,0:T(8,128)(2,1)S(1)}, bf16[8,64,128]{2,1,0:T(8,128)(2,1)S(1)}, u32[]{:S(2)}, u32[]{:S(2)}) %collective-permute-start.32) | collective-permute-done | bytes 131104 | tf_op jit(solution)/shard_map/ppermute | solution.py:19
  148.7 2.6 %collective-permute-done.51.partner_ref = bf16[8,64,128]{2,1,0:T(8,128)(2,1)S(1)} collective-permute-done((bf16[8,64,128]{2,1,0:T(8,128)(2,1)S(1)}, bf16[8,64,128]{2,1,0:T(8,128)(2,1)S(1)}, u32[]{:S(2)}, u32[]{:S(2)}) %collective-permute-start.51) | collective-permute-done | bytes 131104 | tf_op jit(solution)/shard_map/ppermute | solution.py:19
  151.6 2.5 %collective-permute-done.33.partner_ref = bf16[8,64,128]{2,1,0:T(8,128)(2,1)S(1)} collective-permute-done((bf16[8,64,128]{2,1,0:T(8,128)(2,1)S(1)}, bf16[8,64,128]{2,1,0:T(8,128)(2,1)S(1)}, u32[]{:S(2)}, u32[]{:S(2)}) %collective-permute-start.33) | collective-permute-done | bytes 131104 | tf_op jit(solution)/shard_map/ppermute | solution.py:19
  154.5 5.3 %collective-permute-start.46 = (bf16[8,64,128]{2,1,0:T(8,128)(2,1)S(1)}, bf16[8,64,128]{2,1,0:T(8,128)(2,1)S(1)}, u32[]{:S(2)}, u32[]{:S(2)}) collective-permute-start(bf16[8,64,128]{2,1,0:T(8,128)(2,1)S(1)} %shard_map.99.refs_3_.z_ref), channel_id=1, source_target_pairs={{0,120},{8,0},{16,8},{24,16},{32,24},{40,32},{48,40},{56,48},{64,5... | collective-permute-start | bytes 393224 | tf_op jit(solution)/shard_map/ppermute | solution.py:24
  159.9 5.3 %collective-permute-start.45 = (bf16[8,64,128]{2,1,0:T(8,128)(2,1)S(1)}, bf16[8,64,128]{2,1,0:T(8,128)(2,1)S(1)}, u32[]{:S(2)}, u32[]{:S(2)}) collective-permute-start(bf16[8,64,128]{2,1,0:T(8,128)(2,1)S(1)} %shard_map.83.z_ref.refs_2_), channel_id=1, source_target_pairs={{0,120},{8,0},{16,8},{24,16},{32,24},{40,32},{48,40},{56,48},{64,5... | collective-permute-start | bytes 393224 | tf_op jit(solution)/shard_map/ppermute | solution.py:24
  166.4 3.0 %collective-permute-start.35 = (bf16[8,64,128]{2,1,0:T(8,128)(2,1)S(1)}, bf16[8,64,128]{2,1,0:T(8,128)(2,1)S(1)}, u32[]{:S(2)}, u32[]{:S(2)}) collective-permute-start(bf16[8,64,128]{2,1,0:T(8,128)(2,1)S(1)} %shard_map.90.own_ref), channel_id=1, source_target_pairs={{0,64},{8,72},{16,80},{24,88},{32,96},{40,104},{48,112},{56,120},{... | collective-permute-start | bytes 393224 | tf_op jit(solution)/shard_map/ppermute | solution.py:19
  (221 shorter events, 61.5 us)
Async XLA Ops:
  10.2 7.9 %collective-permute-start.1 = (bf16[8,64,128]{2,1,0:T(8,128)(2,1)S(1)}, bf16[8,64,128]{2,1,0:T(8,128)(2,1)S(1)}, u32[]{:S(2)}, u32[]{:S(2)}) collective-permute-start(bf16[8,64,128]{2,1,0:T(8,128)(2,1)S(1)} %shard_map.57.own_ref), channel_id=1, source_target_pairs={{0,2},{1,3},{2,0},{3,1},{4,6},{5,7},{6,4},{7,5},{8,10},{9,11},{10,... | collective-permute-start | bytes 393224 | tf_op jit(solution)/shard_map/ppermute | solution.py:19
  15.0 7.9 %collective-permute-start.21 = (bf16[8,64,128]{2,1,0:T(8,128)(2,1)S(1)}, bf16[8,64,128]{2,1,0:T(8,128)(2,1)S(1)}, u32[]{:S(2)}, u32[]{:S(2)}) collective-permute-start(bf16[8,64,128]{2,1,0:T(8,128)(2,1)S(1)} %shard_map.75.own_ref), channel_id=1, source_target_pairs={{0,4},{1,5},{2,6},{3,7},{4,0},{5,1},{6,2},{7,3},{8,12},{9,13},{10,... | collective-permute-start | bytes 393224 | tf_op jit(solution)/shard_map/ppermute | solution.py:19
  18.4 6.9 %collective-permute-start.2 = (bf16[8,64,128]{2,1,0:T(8,128)(2,1)S(1)}, bf16[8,64,128]{2,1,0:T(8,128)(2,1)S(1)}, u32[]{:S(2)}, u32[]{:S(2)}) collective-permute-start(bf16[8,64,128]{2,1,0:T(8,128)(2,1)S(1)} %shard_map.58.own_ref), channel_id=1, source_target_pairs={{0,4},{1,5},{2,6},{3,7},{4,0},{5,1},{6,2},{7,3},{8,12},{9,13},{10,... | collective-permute-start | bytes 393224 | tf_op jit(solution)/shard_map/ppermute | solution.py:19
  25.5 8.1 %collective-permute-start.3 = (bf16[8,64,128]{2,1,0:T(8,128)(2,1)S(1)}, bf16[8,64,128]{2,1,0:T(8,128)(2,1)S(1)}, u32[]{:S(2)}, u32[]{:S(2)}) collective-permute-start(bf16[8,64,128]{2,1,0:T(8,128)(2,1)S(1)} %shard_map.59.own_ref), channel_id=1, source_target_pairs={{0,8},{8,0},{16,24},{24,16},{32,40},{40,32},{48,56},{56,48},{64,72... | collective-permute-start | bytes 393224 | tf_op jit(solution)/shard_map/ppermute | solution.py:19
  29.2 11.1 %collective-permute-start.23 = (bf16[8,64,128]{2,1,0:T(8,128)(2,1)S(1)}, bf16[8,64,128]{2,1,0:T(8,128)(2,1)S(1)}, u32[]{:S(2)}, u32[]{:S(2)}) collective-permute-start(bf16[8,64,128]{2,1,0:T(8,128)(2,1)S(1)} %shard_map.77.own_ref), channel_id=1, source_target_pairs={{0,16},{8,24},{16,0},{24,8},{32,48},{40,56},{48,32},{56,40},{64,80... | collective-permute-start | bytes 393224 | tf_op jit(solution)/shard_map/ppermute | solution.py:19
  33.9 8.6 %collective-permute-start.4 = (bf16[8,64,128]{2,1,0:T(8,128)(2,1)S(1)}, bf16[8,64,128]{2,1,0:T(8,128)(2,1)S(1)}, u32[]{:S(2)}, u32[]{:S(2)}) collective-permute-start(bf16[8,64,128]{2,1,0:T(8,128)(2,1)S(1)} %shard_map.60.own_ref), channel_id=1, source_target_pairs={{0,16},{8,24},{16,0},{24,8},{32,48},{40,56},{48,32},{56,40},{64,80... | collective-permute-start | bytes 393224 | tf_op jit(solution)/shard_map/ppermute | solution.py:19
  36.2 18.1 %collective-permute-start.10 = (bf16[8,64,128]{2,1,0:T(8,128)(2,1)S(1)}, bf16[8,64,128]{2,1,0:T(8,128)(2,1)S(1)}, u32[]{:S(2)}, u32[]{:S(2)}) collective-permute-start(bf16[8,64,128]{2,1,0:T(8,128)(2,1)S(1)} %shard_map.63.refs_3_.z_ref.source_ref), channel_id=1, source_target_pairs={{0,120},{8,0},{16,8},{24,16},{32,24},{40,32},{48,40},{56,48},{64,5... | collective-permute-start | bytes 393224 | tf_op jit(solution)/shard_map/ppermute | solution.py:24
  40.3 20.0 %collective-permute-start.7 = (bf16[8,64,128]{2,1,0:T(8,128)(2,1)S(1)}, bf16[8,64,128]{2,1,0:T(8,128)(2,1)}, u32[]{:S(2)}, u32[]{:S(2)}) collective-permute-start(bf16[8,64,128]{2,1,0:T(8,128)(2,1)S(1)} %shard_map.55.z_ref.refs_2_.source_ref), channel_id=1, source_target_pairs={{0,8},{8,16},{16,24},{24,32},{32,40},{40,48},{48,56},{56,64},{64,7... | collective-permute-start | bytes 393224 | tf_op jit(solution)/shard_map/ppermute | solution.py:24
  40.3 20.0 %collective-permute-start.8 = (bf16[8,64,128]{2,1,0:T(8,128)(2,1)S(1)}, bf16[8,64,128]{2,1,0:T(8,128)(2,1)}, u32[]{:S(2)}, u32[]{:S(2)}) collective-permute-start(bf16[8,64,128]{2,1,0:T(8,128)(2,1)S(1)} %shard_map.63.refs_3_.z_ref.source_ref), channel_id=1, source_target_pairs={{0,8},{8,16},{16,24},{24,32},{32,40},{40,48},{48,56},{56,64},{64,7... | collective-permute-start | bytes 393224 | tf_op jit(solution)/shard_map/ppermute | solution.py:24
  42.7 11.4 %collective-permute-start.5 = (bf16[8,64,128]{2,1,0:T(8,128)(2,1)S(1)}, bf16[8,64,128]{2,1,0:T(8,128)(2,1)S(1)}, u32[]{:S(2)}, u32[]{:S(2)}) collective-permute-start(bf16[8,64,128]{2,1,0:T(8,128)(2,1)S(1)} %shard_map.61.own_ref), channel_id=1, source_target_pairs={{0,32},{8,40},{16,48},{24,56},{32,0},{40,8},{48,16},{56,24},{64,96... | collective-permute-start | bytes 393224 | tf_op jit(solution)/shard_map/ppermute | solution.py:19
  46.8 13.5 %collective-permute-start.9 = (bf16[8,64,128]{2,1,0:T(8,128)(2,1)S(1)}, bf16[8,64,128]{2,1,0:T(8,128)(2,1)}, u32[]{:S(2)}, u32[]{:S(2)}) collective-permute-start(bf16[8,64,128]{2,1,0:T(8,128)(2,1)S(1)} %shard_map.55.z_ref.refs_2_.source_ref), channel_id=1, source_target_pairs={{0,120},{8,0},{16,8},{24,16},{32,24},{40,32},{48,40},{56,48},{64,5... | collective-permute-start | bytes 393224 | tf_op jit(solution)/shard_map/ppermute | solution.py:24
  54.0 12.3 %collective-permute-start.25 = (bf16[8,64,128]{2,1,0:T(8,128)(2,1)}, bf16[8,64,128]{2,1,0:T(8,128)(2,1)}, u32[]{:S(2)}, u32[]{:S(2)}) collective-permute-start(bf16[8,64,128]{2,1,0:T(8,128)(2,1)} %shard_map.79.own_ref), channel_id=1, source_target_pairs={{0,64},{8,72},{16,80},{24,88},{32,96},{40,104},{48,112},{56,120},{... | collective-permute-start | bytes 393224 | tf_op jit(solution)/shard_map/ppermute | solution.py:19
  55.0 13.6 %collective-permute-start.6 = (bf16[8,64,128]{2,1,0:T(8,128)(2,1)S(1)}, bf16[8,64,128]{2,1,0:T(8,128)(2,1)}, u32[]{:S(2)}, u32[]{:S(2)}) collective-permute-start(bf16[8,64,128]{2,1,0:T(8,128)(2,1)S(1)} %shard_map.62.own_ref), channel_id=1, source_target_pairs={{0,64},{8,72},{16,80},{24,88},{32,96},{40,104},{48,112},{56,120},{... | collective-permute-start | bytes 393224 | tf_op jit(solution)/shard_map/ppermute | solution.py:19
  73.1 8.0 %collective-permute-start.12 = (bf16[8,64,128]{2,1,0:T(8,128)(2,1)S(1)}, bf16[8,64,128]{2,1,0:T(8,128)(2,1)S(1)}, u32[]{:S(2)}, u32[]{:S(2)}) collective-permute-start(bf16[8,64,128]{2,1,0:T(8,128)(2,1)S(1)} %shard_map.67.own_ref), channel_id=1, source_target_pairs={{0,2},{1,3},{2,0},{3,1},{4,6},{5,7},{6,4},{7,5},{8,10},{9,11},{10,... | collective-permute-start | bytes 393224 | tf_op jit(solution)/shard_map/ppermute | solution.py:19
  77.8 7.5 %collective-permute-start.39 = (bf16[8,64,128]{2,1,0:T(8,128)(2,1)S(1)}, bf16[8,64,128]{2,1,0:T(8,128)(2,1)S(1)}, u32[]{:S(2)}, u32[]{:S(2)}) collective-permute-start(bf16[8,64,128]{2,1,0:T(8,128)(2,1)S(1)} %shard_map.93.own_ref), channel_id=1, source_target_pairs={{0,4},{1,5},{2,6},{3,7},{4,0},{5,1},{6,2},{7,3},{8,12},{9,13},{10,... | collective-permute-start | bytes 393224 | tf_op jit(solution)/shard_map/ppermute | solution.py:19
  99.0 8.4 %collective-permute-start.42 = (bf16[8,64,128]{2,1,0:T(8,128)(2,1)S(1)}, bf16[8,64,128]{2,1,0:T(8,128)(2,1)S(1)}, u32[]{:S(2)}, u32[]{:S(2)}) collective-permute-start(bf16[8,64,128]{2,1,0:T(8,128)(2,1)S(1)} %shard_map.96.own_ref), channel_id=1, source_target_pairs={{0,32},{8,40},{16,48},{24,56},{32,0},{40,8},{48,16},{56,24},{64,96... | collective-permute-start | bytes 393224 | tf_op jit(solution)/shard_map/ppermute | solution.py:19
  101.8 11.1 %collective-permute-start.16 = (bf16[8,64,128]{2,1,0:T(8,128)(2,1)S(1)}, bf16[8,64,128]{2,1,0:T(8,128)(2,1)S(1)}, u32[]{:S(2)}, u32[]{:S(2)}) collective-permute-start(bf16[8,64,128]{2,1,0:T(8,128)(2,1)S(1)} %shard_map.71.own_ref), channel_id=1, source_target_pairs={{0,32},{8,40},{16,48},{24,56},{32,0},{40,8},{48,16},{56,24},{64,96... | collective-permute-start | bytes 393224 | tf_op jit(solution)/shard_map/ppermute | solution.py:19
  101.9 11.8 %collective-permute-start.26 = (bf16[8,64,128]{2,1,0:T(8,128)(2,1)S(1)}, bf16[8,64,128]{2,1,0:T(8,128)(2,1)S(1)}, u32[]{:S(2)}, u32[]{:S(2)}) collective-permute-start(bf16[8,64,128]{2,1,0:T(8,128)(2,1)S(1)} %shard_map.81.refs_3_.z_ref), channel_id=1, source_target_pairs={{0,8},{8,16},{16,24},{24,32},{32,40},{40,48},{48,56},{56,64},{64,7... | collective-permute-start | bytes 393224 | tf_op jit(solution)/shard_map/ppermute | solution.py:24
  102.0 14.9 %collective-permute-start.28 = (bf16[8,64,128]{2,1,0:T(8,128)(2,1)S(1)}, bf16[8,64,128]{2,1,0:T(8,128)(2,1)S(1)}, u32[]{:S(2)}, u32[]{:S(2)}) collective-permute-start(bf16[8,64,128]{2,1,0:T(8,128)(2,1)S(1)} %shard_map.81.refs_3_.z_ref), channel_id=1, source_target_pairs={{0,120},{8,0},{16,8},{24,16},{32,24},{40,32},{48,40},{56,48},{64,5... | collective-permute-start | bytes 393224 | tf_op jit(solution)/shard_map/ppermute | solution.py:24
  107.3 9.5 %collective-permute-start.18 = (bf16[8,64,128]{2,1,0:T(8,128)(2,1)S(1)}, bf16[8,64,128]{2,1,0:T(8,128)(2,1)S(1)}, u32[]{:S(2)}, u32[]{:S(2)}) collective-permute-start(bf16[8,64,128]{2,1,0:T(8,128)(2,1)S(1)} %shard_map.65.z_ref.refs_2_), channel_id=1, source_target_pairs={{0,8},{8,16},{16,24},{24,32},{32,40},{40,48},{48,56},{56,64},{64,7... | collective-permute-start | bytes 393224 | tf_op jit(solution)/shard_map/ppermute | solution.py:24
  107.4 9.5 %collective-permute-start.27 = (bf16[8,64,128]{2,1,0:T(8,128)(2,1)S(1)}, bf16[8,64,128]{2,1,0:T(8,128)(2,1)S(1)}, u32[]{:S(2)}, u32[]{:S(2)}) collective-permute-start(bf16[8,64,128]{2,1,0:T(8,128)(2,1)S(1)} %shard_map.65.z_ref.refs_2_), channel_id=1, source_target_pairs={{0,120},{8,0},{16,8},{24,16},{32,24},{40,32},{48,40},{56,48},{64,5... | collective-permute-start | bytes 393224 | tf_op jit(solution)/shard_map/ppermute | solution.py:24
  113.7 7.9 %collective-permute-start.17 = (bf16[8,64,128]{2,1,0:T(8,128)(2,1)S(1)}, bf16[8,64,128]{2,1,0:T(8,128)(2,1)S(1)}, u32[]{:S(2)}, u32[]{:S(2)}) collective-permute-start(bf16[8,64,128]{2,1,0:T(8,128)(2,1)S(1)} %shard_map.72.own_ref), channel_id=1, source_target_pairs={{0,64},{8,72},{16,80},{24,88},{32,96},{40,104},{48,112},{56,120},{... | collective-permute-start | bytes 393224 | tf_op jit(solution)/shard_map/ppermute | solution.py:19
  125.5 8.0 %collective-permute-start.30 = (bf16[8,64,128]{2,1,0:T(8,128)(2,1)S(1)}, bf16[8,64,128]{2,1,0:T(8,128)(2,1)S(1)}, u32[]{:S(2)}, u32[]{:S(2)}) collective-permute-start(bf16[8,64,128]{2,1,0:T(8,128)(2,1)S(1)} %shard_map.85.own_ref), channel_id=1, source_target_pairs={{0,2},{1,3},{2,0},{3,1},{4,6},{5,7},{6,4},{7,5},{8,10},{9,11},{10,... | collective-permute-start | bytes 393224 | tf_op jit(solution)/shard_map/ppermute | solution.py:19
  129.9 8.0 %collective-permute-start.49 = (bf16[8,64,128]{2,1,0:T(8,128)(2,1)S(1)}, bf16[8,64,128]{2,1,0:T(8,128)(2,1)S(1)}, u32[]{:S(2)}, u32[]{:S(2)}) collective-permute-start(bf16[8,64,128]{2,1,0:T(8,128)(2,1)S(1)} %shard_map.104.own_ref), channel_id=1, source_target_pairs={{0,4},{1,5},{2,6},{3,7},{4,0},{5,1},{6,2},{7,3},{8,12},{9,13},{10,... | collective-permute-start | bytes 393224 | tf_op jit(solution)/shard_map/ppermute | solution.py:19
  133.7 6.8 %collective-permute-start.31 = (bf16[8,64,128]{2,1,0:T(8,128)(2,1)S(1)}, bf16[8,64,128]{2,1,0:T(8,128)(2,1)S(1)}, u32[]{:S(2)}, u32[]{:S(2)}) collective-permute-start(bf16[8,64,128]{2,1,0:T(8,128)(2,1)S(1)} %shard_map.86.own_ref), channel_id=1, source_target_pairs={{0,4},{1,5},{2,6},{3,7},{4,0},{5,1},{6,2},{7,3},{8,12},{9,13},{10,... | collective-permute-start | bytes 393224 | tf_op jit(solution)/shard_map/ppermute | solution.py:19
  151.5 8.3 %collective-permute-start.52 = (bf16[8,64,128]{2,1,0:T(8,128)(2,1)S(1)}, bf16[8,64,128]{2,1,0:T(8,128)(2,1)S(1)}, u32[]{:S(2)}, u32[]{:S(2)}) collective-permute-start(bf16[8,64,128]{2,1,0:T(8,128)(2,1)S(1)} %shard_map.107.own_ref), channel_id=1, source_target_pairs={{0,32},{8,40},{16,48},{24,56},{32,0},{40,8},{48,16},{56,24},{64,96... | collective-permute-start | bytes 393224 | tf_op jit(solution)/shard_map/ppermute | solution.py:19
  154.4 11.1 %collective-permute-start.34 = (bf16[8,64,128]{2,1,0:T(8,128)(2,1)S(1)}, bf16[8,64,128]{2,1,0:T(8,128)(2,1)S(1)}, u32[]{:S(2)}, u32[]{:S(2)}) collective-permute-start(bf16[8,64,128]{2,1,0:T(8,128)(2,1)S(1)} %shard_map.89.own_ref), channel_id=1, source_target_pairs={{0,32},{8,40},{16,48},{24,56},{32,0},{40,8},{48,16},{56,24},{64,96... | collective-permute-start | bytes 393224 | tf_op jit(solution)/shard_map/ppermute | solution.py:19
  154.4 12.0 %collective-permute-start.44 = (bf16[8,64,128]{2,1,0:T(8,128)(2,1)S(1)}, bf16[8,64,128]{2,1,0:T(8,128)(2,1)S(1)}, u32[]{:S(2)}, u32[]{:S(2)}) collective-permute-start(bf16[8,64,128]{2,1,0:T(8,128)(2,1)S(1)} %shard_map.99.refs_3_.z_ref), channel_id=1, source_target_pairs={{0,8},{8,16},{16,24},{24,32},{32,40},{40,48},{48,56},{56,64},{64,7... | collective-permute-start | bytes 393224 | tf_op jit(solution)/shard_map/ppermute | solution.py:24
  154.5 14.9 %collective-permute-start.46 = (bf16[8,64,128]{2,1,0:T(8,128)(2,1)S(1)}, bf16[8,64,128]{2,1,0:T(8,128)(2,1)S(1)}, u32[]{:S(2)}, u32[]{:S(2)}) collective-permute-start(bf16[8,64,128]{2,1,0:T(8,128)(2,1)S(1)} %shard_map.99.refs_3_.z_ref), channel_id=1, source_target_pairs={{0,120},{8,0},{16,8},{24,16},{32,24},{40,32},{48,40},{56,48},{64,5... | collective-permute-start | bytes 393224 | tf_op jit(solution)/shard_map/ppermute | solution.py:24
  159.9 9.7 %collective-permute-start.36 = (bf16[8,64,128]{2,1,0:T(8,128)(2,1)S(1)}, bf16[8,64,128]{2,1,0:T(8,128)(2,1)S(1)}, u32[]{:S(2)}, u32[]{:S(2)}) collective-permute-start(bf16[8,64,128]{2,1,0:T(8,128)(2,1)S(1)} %shard_map.83.z_ref.refs_2_), channel_id=1, source_target_pairs={{0,8},{8,16},{16,24},{24,32},{32,40},{40,48},{48,56},{56,64},{64,7... | collective-permute-start | bytes 393224 | tf_op jit(solution)/shard_map/ppermute | solution.py:24
  159.9 9.7 %collective-permute-start.45 = (bf16[8,64,128]{2,1,0:T(8,128)(2,1)S(1)}, bf16[8,64,128]{2,1,0:T(8,128)(2,1)S(1)}, u32[]{:S(2)}, u32[]{:S(2)}) collective-permute-start(bf16[8,64,128]{2,1,0:T(8,128)(2,1)S(1)} %shard_map.83.z_ref.refs_2_), channel_id=1, source_target_pairs={{0,120},{8,0},{16,8},{24,16},{32,24},{40,32},{48,40},{56,48},{64,5... | collective-permute-start | bytes 393224 | tf_op jit(solution)/shard_map/ppermute | solution.py:24
  166.4 7.0 %collective-permute-start.35 = (bf16[8,64,128]{2,1,0:T(8,128)(2,1)S(1)}, bf16[8,64,128]{2,1,0:T(8,128)(2,1)S(1)}, u32[]{:S(2)}, u32[]{:S(2)}) collective-permute-start(bf16[8,64,128]{2,1,0:T(8,128)(2,1)S(1)} %shard_map.90.own_ref), channel_id=1, source_target_pairs={{0,64},{8,72},{16,80},{24,88},{32,96},{40,104},{48,112},{56,120},{... | collective-permute-start | bytes 393224 | tf_op jit(solution)/shard_map/ppermute | solution.py:19
  (64 other events, 860.7 us)

commit v2 on v1

v2 whole, which is shorter than its diff:
```python
import functools

import jax
import jax.numpy as jnp
from jax import lax
from jax.experimental import pallas as pl
from jax.experimental.pallas import tpu as pltpu
from jax.sharding import PartitionSpec as P

ITERS = 3
CHAINS = 2
NEAR_RING = 1


coupling = 0.4


def exchange(block, axis, flip):
    route = [(i, i ^ flip) for i in range(lax.axis_size(axis))]
    return lax.ppermute(block, axis, route)


def shifted(value, axis, step):
    count = lax.axis_size(axis)
    return lax.ppermute(value, axis, [(i, (i + step) % count) for i in range(count)])


def pair_product(own, partner, factor):
    both = jnp.concatenate([own, partner], axis=-1)
    weights = factor.reshape(2 * factor.shape[-2], factor.shape[-1])
    return jnp.dot(both, weights, preferred_element_type=jnp.float32)


def place(array):
    return pl.BlockSpec(memory_space=pltpu.SMEM if array.dtype == jnp.int32 else pltpu.VMEM)


def call(kernel, out_shape, operands, flops, scratch=()):
    size = sum(op.size * op.dtype.itemsize for op in operands)
    return pl.pallas_call(
        kernel,
        out_shape=out_shape,
        in_specs=[place(op) for op in operands],
        scratch_shapes=scratch,
        out_specs=jax.tree.map(place, out_shape),
        cost_estimate=pl.CostEstimate(flops=flops, bytes_accessed=size, transcendentals=0),
        compiler_params=pltpu.CompilerParams(vmem_limit_bytes=8 * 2**20),
    )(*operands)


def split_kernel(start, rows_ref, out_ref):
    blocks, _, width = out_ref.shape
    for b in range(blocks):
        out_ref[b] = rows_ref[:, (start + b) * width:(start + b + 1) * width]


def local_kernel(start, z_ref, *refs):
    factors, out_ref = refs[:-1], refs[-1]
    blocks = z_ref.shape[0]
    mixed = [z_ref[b] for b in range(blocks)]
    for level, factor in enumerate(factors):
        mixed = [
            pair_product(mixed[b], mixed[b ^ (1 << level)], factor[0, start + b]).astype(
                jnp.bfloat16
            )
            for b in range(blocks)
        ]
    for b in range(blocks):
        out_ref[b] = mixed[b]


def level_kernel(start, own_ref, partner_ref, factor_ref, *refs):
    out_ref = refs[-1]
    for b in range(own_ref.shape[0]):
        out_ref[b] = pair_product(own_ref[b], partner_ref[b], factor_ref[0, start + b]).astype(
            jnp.bfloat16
        )


def near_kernel(start, index_ref, count_ref, *refs):
    pieces, near_ref, out_ref, window = refs[:-3], *refs[-3:]
    blocks = out_ref.shape[0]
    slots, width = near_ref.shape[1:3]
    unused = 0
    for piece in pieces:
        window[unused:unused + piece.shape[0]] = piece[...]
        unused += piece.shape[0]
    window[unused] = jnp.zeros(window.shape[1:], window.dtype)
    for b in range(start, start + blocks):
        count = count_ref[b]
        taken = [window[jnp.where(k < count, index_ref[k, b], unused)] for k in range(slots)]
        out_ref[b - start] = jnp.dot(
            jnp.concatenate(taken, axis=-1),
            near_ref[b].reshape(slots * width, width),
            preferred_element_type=jnp.float32,
        )


def take_kernel(*refs):
    refs[-1][...] = refs[-2][...]


def last_kernel(start, own_ref, partner_ref, factor_ref, near_ref, source_ref, out_ref):
    for b in range(own_ref.shape[0]):
        mixed = pair_product(own_ref[b], partner_ref[b], factor_ref[0, start + b])
        mixed = mixed.astype(jnp.bfloat16).astype(jnp.float32)
        total = source_ref[b].astype(jnp.float32) - coupling * (mixed + near_ref[b])
        out_ref[b] = total.astype(jnp.bfloat16)


def stack_kernel(*refs):
    at = 0
    for part in refs[:-1]:
        refs[-1][at:at + part.shape[0]] = part[...]
        at += part.shape[0]


def join_kernel(*refs):
    at = 0
    for part in refs[:-1]:
        for b in range(part.shape[0]):
            width = part.shape[-1]
            refs[-1][:, at:at + width] = part[b]
            at += width


def per_device(right_side, level_pairs, near_blocks, near_index, near_count):
    rhs_count = right_side.shape[0]
    blocks, slots, width, _ = near_blocks.shape
    levels = level_pairs.shape[0]
    level_bits = lax.axis_size("level").bit_length() - 1
    patch_bits = lax.axis_size("patch").bit_length() - 1
    core = levels - level_bits - patch_bits
    half = blocks // CHAINS
    chains = range(CHAINS)
    piece = jax.ShapeDtypeStruct((half, rhs_count, width), jnp.bfloat16)
    whole = jax.ShapeDtypeStruct((blocks, rhs_count, width), jnp.bfloat16)
    near_shape = jax.ShapeDtypeStruct((half, rhs_count, width), jnp.float32)
    one_level = jax.ShapeDtypeStruct((1, *level_pairs.shape[1:]), jnp.bfloat16)
    level_flops = 4 * half * rhs_count * width * width
    window_shape = pltpu.VMEM((3 * blocks + 1, rhs_count, width), jnp.bfloat16)

    rings = [
        (core + 1 + i, "level", 1 << (1 + i)) for i in range(0, level_bits - 1, 2)
    ] + [(core + level_bits + i, "patch", 1 << i) for i in range(0, patch_bits, 2)]
    factors = [level_pairs[level:level + 1] for level in range(levels)]
    partner_factors = {
        level: exchange(factors[level], axis, flip) for level, axis, flip in rings[1:]
    }

    def product(kernel, c, own, partner, factor, *more, shape=piece):
        return call(
            functools.partial(kernel, c * half), shape, (own, partner, factor, *more), level_flops
        )

    source = [
        call(functools.partial(split_kernel, c * half), piece, (right_side,), 0) for c in chains
    ]
    current = list(source)
    for sweep in range(ITERS):
        joined = call(stack_kernel, whole, current, 0)
        below = shifted(joined, "patch", 1)
        above = shifted(joined, "patch", -1)
        mixed = [
            call(
                functools.partial(local_kernel, c * half),
                piece,
                (current[c], *factors[:core]),
                core * level_flops,
            )
            for c in chains
        ]
        near = [
            call(
                functools.partial(near_kernel, c * half),
                near_shape,
                (near_index.T, near_count, below, joined, above, near_blocks),
                2 * half * slots * rhs_count * width * width,
                (window_shape,),
            )
            for c in chains
        ]
        for c in chains:
            partner = exchange(mixed[c], "level", 1)
            mixed[c] = product(level_kernel, c, mixed[c], partner, factors[core])
        for ring, (level, axis, flip) in enumerate(rings):
            for c in chains:
                partner = exchange(mixed[c], axis, flip)
                own = product(level_kernel, c, mixed[c], partner, factors[level])
                extra = (near[c],) if ring == NEAR_RING and sweep > 0 else ()
                if level in partner_factors:
                    theirs = product(
                        level_kernel, c, partner, mixed[c], partner_factors[level], *extra
                    )
                    partner = exchange(theirs, axis, 3 * flip)
                else:
                    partner = exchange(own, axis, 2 * flip)
                second = factors[level + 1]
                if ring == len(rings) - 1:
                    mixed[c] = product(last_kernel, c, own, partner, second, near[c], source[c])
                else:
                    mixed[c] = product(level_kernel, c, own, partner, second)
            if level not in partner_factors:
                partner_factors[level] = exchange(
                    call(take_kernel, one_level, (*mixed, factors[level]), 0), axis, flip
                )
        current = mixed
    return call(
        join_kernel,
        jax.ShapeDtypeStruct((rhs_count, blocks * width), jnp.bfloat16),
        current,
        0,
    )


def solution(mesh):
    in_specs = (
        P(None, ("patch", "level")),
        P(None, ("patch", "level"), None, None, None),
        P(("patch", "level"), None, None, None),
        P(("patch", "level"), None),
        P(("patch", "level")),
    )
    out_specs = P(None, ("patch", "level"))
    return jax.shard_map(
        per_device, mesh=mesh, in_specs=in_specs, out_specs=out_specs, check_vma=False
    )
```

time: 175 us -> 156 us (0.89)
  starting transfers between devices: 84.1 us -> 66.6 us
  local copies, waits for them, and re-layouts: 12.1 us -> 5.16 us
  waiting for transfers between devices: 52.6 us -> 58.7 us
    ppermute x12 -> x6, starting transfers between devices: 32 us -> 13 us  [shifted(): lax.ppermute(value, axis, [(i, (i + step) % count) for i in range(count)])]
    squeeze x2 -> x0, local copies, waits for them, and re-layouts: 7.01 us -> none  [factor(): return level_pairs[level, chain * half:(chain + 1) * half]]
    ppermute x42 -> x45, waiting for transfers between devices: 52.4 us -> 57.7 us  [exchange(): return lax.ppermute(block, axis, route)]
    slice x1, local copies, waits for them, and re-layouts: 1.72 us -> 5.14 us  [per_device(): factors = [level_pairs[level:level + 1] for level in range(levels)]]
    unnamed x85 -> x8, local copies, waits for them, and re-layouts: 3.37 us -> 0.02 us
    ppermute x42 -> x45, starting transfers between devices: 52.1 us -> 53.7 us  [exchange(): return lax.ppermute(block, axis, route)]
    pallas_call x57 -> x77, Pallas kernels: 24.5 us -> 24.3 us  [call(): pl.pallas_call(kernel, out_shape=out_shape, in_specs=[place(op) for op in...]
  transfers between devices with their start and end apart: 54 -> 51, of which waited for: 23 -> 29; matrix products, arithmetic and copies ran while one was open for 2% -> 0% of each run, Pallas kernels for 13% -> 15%
where the time goes in v2:
time: 156 us
  starting transfers between devices  66.6 us (43%)
  waiting for transfers between devices  58.7 us (38%)
  Pallas kernels  24.3 us (16%)
  local copies, waits for them, and re-layouts  5.16 us (3%)
    ppermute x45, waiting for transfers between devices, exchange(): return lax.ppermute(block, axis, route)  57.7 us
    ppermute x45, starting transfers between devices, exchange(): return lax.ppermute(block, axis, route)  53.7 us
    pallas_call x77, Pallas kernels, call(): pl.pallas_call(kernel, out_shape=out_shape, in_specs=[place(op) for op in...  24.3 us
    ppermute x6, starting transfers between devices, shifted(): lax.ppermute(value, axis, [(i, (i + step) % count) for i in range(count)])  13 us
    slice x1, local copies, waits for them, and re-layouts, per_device(): factors = [level_pairs[level:level + 1] for level in range(levels)]  5.14 us
  transfers between devices with their start and end apart: 51, of which 29 were waited for; matrix products, arithmetic and copies ran while one was open for 0% of the time, Pallas kernels for 15%

profile of v2, /device:TPU:0, one launch (start us, length us, event | category | flops | bytes accessed | tf_op | source)
XLA Modules:
  0.0 155.6 jit_solution(874705094830196650)
XLA Ops:
  0.0 5.1 %fusion = (bf16[1,16,2,128,128]{4,3,2,1,0:T(8,128)(2,1)S(1)}, bf16[1,16,2,128,128]{4,3,2,1,0:T(8,128)(2,1)S(1)}, bf16[1,16,2,128,128]{4,3,2,1,0:T(8,128)(2,1)S(1...) fusion(bf16[10,16,2,128,128]{4,3,2,1,0:T(8,128)(2,1)} %param.6), kind=kLoop, calls=%fused_computation | loop fusion | bytes 20971520 | tf_op jit(solution)/shard_map/slice | solution.py:146
  5.1 2.1 %collective-permute-start.4 = (bf16[1,16,2,128,128]{4,3,2,1,0:T(8,128)(2,1)S(1)}, bf16[1,16,2,128,128]{4,3,2,1,0:T(8,128)(2,1)S(1)}, u32[]{:S(2)}, u32[]{:S(2)}) collective-permute-start(bf16[1,16,2,128,128]{4,3,2,1,0:T(8,128)(2,1)S(1)} %get-tuple-element.7.factor_ref), channel_id=1, source_target_pairs={{0,8},{8,0},{16,24},{24,16},{32,40},{40,32},{48,56},{56,48},{64,72... | collective-permute-start | bytes 3145736 | tf_op jit(solution)/shard_map/ppermute | solution.py:20
  13.5 4.0 %collective-permute-done.1.partner_ref = bf16[8,64,128]{2,1,0:T(8,128)(2,1)S(1)} collective-permute-done((bf16[8,64,128]{2,1,0:T(8,128)(2,1)S(1)}, bf16[8,64,128]{2,1,0:T(8,128)(2,1)S(1)}, u32[]{:S(2)}, u32[]{:S(2)}) %collective-permute-start.1) | collective-permute-done | bytes 131104 | tf_op jit(solution)/shard_map/ppermute | solution.py:20
  17.7 3.1 %collective-permute-start.2 = (bf16[8,64,128]{2,1,0:T(8,128)(2,1)S(1)}, bf16[8,64,128]{2,1,0:T(8,128)(2,1)S(1)}, u32[]{:S(2)}, u32[]{:S(2)}) collective-permute-start(bf16[8,64,128]{2,1,0:T(8,128)(2,1)S(1)} %shard_map.58.own_ref), channel_id=1, source_target_pairs={{0,4},{1,5},{2,6},{3,7},{4,0},{5,1},{6,2},{7,3},{8,12},{9,13},{10,... | collective-permute-start | bytes 393224 | tf_op jit(solution)/shard_map/ppermute | solution.py:20
  22.9 2.7 %collective-permute-done.2.partner_ref = bf16[8,64,128]{2,1,0:T(8,128)(2,1)S(1)} collective-permute-done((bf16[8,64,128]{2,1,0:T(8,128)(2,1)S(1)}, bf16[8,64,128]{2,1,0:T(8,128)(2,1)S(1)}, u32[]{:S(2)}, u32[]{:S(2)}) %collective-permute-start.2) | collective-permute-done | bytes 131104 | tf_op jit(solution)/shard_map/ppermute | solution.py:20
  25.8 1.8 %collective-permute-done.15.partner_ref = bf16[8,64,128]{2,1,0:T(8,128)(2,1)S(1)} collective-permute-done((bf16[8,64,128]{2,1,0:T(8,128)(2,1)S(1)}, bf16[8,64,128]{2,1,0:T(8,128)(2,1)S(1)}, u32[]{:S(2)}, u32[]{:S(2)}) %collective-permute-start.15) | collective-permute-done | bytes 131104 | tf_op jit(solution)/shard_map/ppermute | solution.py:20
  29.1 1.9 %collective-permute-start.3 = (bf16[8,64,128]{2,1,0:T(8,128)(2,1)S(1)}, bf16[8,64,128]{2,1,0:T(8,128)(2,1)S(1)}, u32[]{:S(2)}, u32[]{:S(2)}) collective-permute-start(bf16[8,64,128]{2,1,0:T(8,128)(2,1)S(1)} %shard_map.59.own_ref.partner_ref.refs_0_), channel_id=1, source_target_pairs={{0,8},{8,0},{16,24},{24,16},{32,40},{40,32},{48,56},{56,48},{64,72... | collective-permute-start | bytes 393224 | tf_op jit(solution)/shard_map/ppermute | solution.py:20
  31.0 3.6 %collective-permute-done.19.partner_ref.own_ref = bf16[8,64,128]{2,1,0:T(8,128)(2,1)S(1)} collective-permute-done((bf16[8,64,128]{2,1,0:T(8,128)(2,1)S(1)}, bf16[8,64,128]{2,1,0:T(8,128)(2,1)S(1)}, u32[]{:S(2)}, u32[]{:S(2)}) %collective-permute-start.19) | collective-permute-done | bytes 131104 | tf_op jit(solution)/shard_map/ppermute | solution.py:20
  34.8 3.7 %collective-permute-start.20 = (bf16[8,64,128]{2,1,0:T(8,128)(2,1)S(1)}, bf16[8,64,128]{2,1,0:T(8,128)(2,1)S(1)}, u32[]{:S(2)}, u32[]{:S(2)}) collective-permute-start(bf16[8,64,128]{2,1,0:T(8,128)(2,1)S(1)} %shard_map.81), channel_id=1, source_target_pairs={{0,24},{8,16},{16,8},{24,0},{32,56},{40,48},{48,40},{56,32},{64,88... | collective-permute-start | bytes 393224 | tf_op jit(solution)/shard_map/ppermute | solution.py:20
  40.2 4.4 %collective-permute-start.10 = (bf16[16,64,128]{2,1,0:T(8,128)(2,1)S(1)}, bf16[16,64,128]{2,1,0:T(8,128)(2,1)S(1)}, u32[]{:S(2)}, u32[]{:S(2)}) collective-permute-start(bf16[16,64,128]{2,1,0:T(8,128)(2,1)S(1)} %shard_map.66.refs_1_), channel_id=1, source_target_pairs={{0,120},{8,0},{16,8},{24,16},{32,24},{40,32},{48,40},{56,48},{64,5... | collective-permute-start | bytes 786440 | tf_op jit(solution)/shard_map/ppermute | solution.py:25
  44.6 3.1 %collective-permute-done.20.partner_ref = bf16[8,64,128]{2,1,0:T(8,128)(2,1)S(1)} collective-permute-done((bf16[8,64,128]{2,1,0:T(8,128)(2,1)S(1)}, bf16[8,64,128]{2,1,0:T(8,128)(2,1)S(1)}, u32[]{:S(2)}, u32[]{:S(2)}) %collective-permute-start.20) | collective-permute-done | bytes 131104 | tf_op jit(solution)/shard_map/ppermute | solution.py:20
  51.7 3.0 %collective-permute-done.21.partner_ref.own_ref = bf16[8,64,128]{2,1,0:T(8,128)(2,1)S(1)} collective-permute-done((bf16[8,64,128]{2,1,0:T(8,128)(2,1)S(1)}, bf16[8,64,128]{2,1,0:T(8,128)(2,1)S(1)}, u32[]{:S(2)}, u32[]{:S(2)}) %collective-permute-start.21) | collective-permute-done | bytes 131104 | tf_op jit(solution)/shard_map/ppermute | solution.py:20
  54.9 2.5 %collective-permute-start.22 = (bf16[8,64,128]{2,1,0:T(8,128)(2,1)S(1)}, bf16[8,64,128]{2,1,0:T(8,128)(2,1)S(1)}, u32[]{:S(2)}, u32[]{:S(2)}) collective-permute-start(bf16[8,64,128]{2,1,0:T(8,128)(2,1)S(1)} %shard_map.84), channel_id=1, source_target_pairs={{0,96},{8,104},{16,112},{24,120},{32,64},{40,72},{48,80},{56,88},{... | collective-permute-start | bytes 393224 | tf_op jit(solution)/shard_map/ppermute | solution.py:20
  67.9 6.4 %collective-permute-start.24 = (bf16[16,64,128]{2,1,0:T(8,128)(2,1)S(1)}, bf16[16,64,128]{2,1,0:T(8,128)(2,1)S(1)}, u32[]{:S(2)}, u32[]{:S(2)}) collective-permute-start(bf16[16,64,128]{2,1,0:T(8,128)(2,1)S(1)} %shard_map.87.refs_1_), channel_id=1, source_target_pairs={{0,120},{8,0},{16,8},{24,16},{32,24},{40,32},{48,40},{56,48},{64,5... | collective-permute-start | bytes 786440 | tf_op jit(solution)/shard_map/ppermute | solution.py:25
  74.6 2.4 %collective-permute-start.34 = (bf16[8,64,128]{2,1,0:T(8,128)(2,1)S(1)}, bf16[8,64,128]{2,1,0:T(8,128)(2,1)S(1)}, u32[]{:S(2)}, u32[]{:S(2)}) collective-permute-start(bf16[8,64,128]{2,1,0:T(8,128)(2,1)S(1)} %shard_map.103), channel_id=1, source_target_pairs={{0,6},{1,7},{2,4},{3,5},{4,2},{5,3},{6,0},{7,1},{8,14},{9,15},{10,... | collective-permute-start | bytes 393224 | tf_op jit(solution)/shard_map/ppermute | solution.py:20
  78.5 3.3 %collective-permute-done.34.partner_ref = bf16[8,64,128]{2,1,0:T(8,128)(2,1)S(1)} collective-permute-done((bf16[8,64,128]{2,1,0:T(8,128)(2,1)S(1)}, bf16[8,64,128]{2,1,0:T(8,128)(2,1)S(1)}, u32[]{:S(2)}, u32[]{:S(2)}) %collective-permute-start.34) | collective-permute-done | bytes 131104 | tf_op jit(solution)/shard_map/ppermute | solution.py:20
  88.6 3.8 %collective-permute-start.36 = (bf16[8,64,128]{2,1,0:T(8,128)(2,1)S(1)}, bf16[8,64,128]{2,1,0:T(8,128)(2,1)S(1)}, u32[]{:S(2)}, u32[]{:S(2)}) collective-permute-start(bf16[8,64,128]{2,1,0:T(8,128)(2,1)S(1)} %shard_map.107), channel_id=1, source_target_pairs={{0,24},{8,16},{16,8},{24,0},{32,56},{40,48},{48,40},{56,32},{64,88... | collective-permute-start | bytes 393224 | tf_op jit(solution)/shard_map/ppermute | solution.py:20
  94.1 1.9 %collective-permute-done.36.partner_ref = bf16[8,64,128]{2,1,0:T(8,128)(2,1)S(1)} collective-permute-done((bf16[8,64,128]{2,1,0:T(8,128)(2,1)S(1)}, bf16[8,64,128]{2,1,0:T(8,128)(2,1)S(1)}, u32[]{:S(2)}, u32[]{:S(2)}) %collective-permute-start.36) | collective-permute-done | bytes 131104 | tf_op jit(solution)/shard_map/ppermute | solution.py:20
  96.9 3.1 %collective-permute-done.25.partner_ref = bf16[8,64,128]{2,1,0:T(8,128)(2,1)S(1)} collective-permute-done((bf16[8,64,128]{2,1,0:T(8,128)(2,1)S(1)}, bf16[8,64,128]{2,1,0:T(8,128)(2,1)S(1)}, u32[]{:S(2)}, u32[]{:S(2)}) %collective-permute-start.25) | collective-permute-done | bytes 131104 | tf_op jit(solution)/shard_map/ppermute | solution.py:20
  101.5 2.2 %collective-permute-start.38 = (bf16[8,64,128]{2,1,0:T(8,128)(2,1)S(1)}, bf16[8,64,128]{2,1,0:T(8,128)(2,1)S(1)}, u32[]{:S(2)}, u32[]{:S(2)}) collective-permute-start(bf16[8,64,128]{2,1,0:T(8,128)(2,1)S(1)} %shard_map.110), channel_id=1, source_target_pairs={{0,96},{8,104},{16,112},{24,120},{32,64},{40,72},{48,80},{56,88},{... | collective-permute-start | bytes 393224 | tf_op jit(solution)/shard_map/ppermute | solution.py:20
  105.5 2.2 %collective-permute-start.27 = (bf16[8,64,128]{2,1,0:T(8,128)(2,1)S(1)}, bf16[8,64,128]{2,1,0:T(8,128)(2,1)S(1)}, u32[]{:S(2)}, u32[]{:S(2)}) collective-permute-start(bf16[8,64,128]{2,1,0:T(8,128)(2,1)S(1)} %shard_map.92), channel_id=1, source_target_pairs={{0,96},{8,104},{16,112},{24,120},{32,64},{40,72},{48,80},{56,88},{... | collective-permute-start | bytes 393224 | tf_op jit(solution)/shard_map/ppermute | solution.py:20
  109.1 2.7 %collective-permute-done.27.partner_ref = bf16[8,64,128]{2,1,0:T(8,128)(2,1)S(1)} collective-permute-done((bf16[8,64,128]{2,1,0:T(8,128)(2,1)S(1)}, bf16[8,64,128]{2,1,0:T(8,128)(2,1)S(1)}, u32[]{:S(2)}, u32[]{:S(2)}) %collective-permute-start.27) | collective-permute-done | bytes 131104 | tf_op jit(solution)/shard_map/ppermute | solution.py:20
  115.4 2.0 %collective-permute-start.40 = (bf16[16,64,128]{2,1,0:T(8,128)(2,1)S(1)}, bf16[16,64,128]{2,1,0:T(8,128)(2,1)S(1)}, u32[]{:S(2)}, u32[]{:S(2)}) collective-permute-start(bf16[16,64,128]{2,1,0:T(8,128)(2,1)S(1)} %shard_map.112.refs_1_), channel_id=1, source_target_pairs={{0,120},{8,0},{16,8},{24,16},{32,24},{40,32},{48,40},{56,48},{64,5... | collective-permute-start | bytes 786440 | tf_op jit(solution)/shard_map/ppermute | solution.py:25
  117.5 1.8 %collective-permute-done.45.partner_ref.own_ref = bf16[8,64,128]{2,1,0:T(8,128)(2,1)S(1)} collective-permute-done((bf16[8,64,128]{2,1,0:T(8,128)(2,1)S(1)}, bf16[8,64,128]{2,1,0:T(8,128)(2,1)S(1)}, u32[]{:S(2)}, u32[]{:S(2)}) %collective-permute-start.45) | collective-permute-done | bytes 131104 | tf_op jit(solution)/shard_map/ppermute | solution.py:20
  123.7 2.3 %collective-permute-done.46.partner_ref = bf16[8,64,128]{2,1,0:T(8,128)(2,1)S(1)} collective-permute-done((bf16[8,64,128]{2,1,0:T(8,128)(2,1)S(1)}, bf16[8,64,128]{2,1,0:T(8,128)(2,1)S(1)}, u32[]{:S(2)}, u32[]{:S(2)}) %collective-permute-start.46) | collective-permute-done | bytes 131104 | tf_op jit(solution)/shard_map/ppermute | solution.py:20
  126.3 2.3 %collective-permute-done.30.partner_ref = bf16[8,64,128]{2,1,0:T(8,128)(2,1)S(1)} collective-permute-done((bf16[8,64,128]{2,1,0:T(8,128)(2,1)S(1)}, bf16[8,64,128]{2,1,0:T(8,128)(2,1)S(1)}, u32[]{:S(2)}, u32[]{:S(2)}) %collective-permute-start.30) | collective-permute-done | bytes 131104 | tf_op jit(solution)/shard_map/ppermute | solution.py:20
  132.3 2.5 %collective-permute-start.48 = (bf16[8,64,128]{2,1,0:T(8,128)(2,1)S(1)}, bf16[8,64,128]{2,1,0:T(8,128)(2,1)S(1)}, u32[]{:S(2)}, u32[]{:S(2)}) collective-permute-start(bf16[8,64,128]{2,1,0:T(8,128)(2,1)S(1)} %shard_map.126), channel_id=1, source_target_pairs={{0,24},{8,16},{16,8},{24,0},{32,56},{40,48},{48,40},{56,32},{64,88... | collective-permute-start | bytes 393224 | tf_op jit(solution)/shard_map/ppermute | solution.py:20
  136.8 3.1 %collective-permute-done.48.partner_ref = bf16[8,64,128]{2,1,0:T(8,128)(2,1)S(1)} collective-permute-done((bf16[8,64,128]{2,1,0:T(8,128)(2,1)S(1)}, bf16[8,64,128]{2,1,0:T(8,128)(2,1)S(1)}, u32[]{:S(2)}, u32[]{:S(2)}) %collective-permute-start.48) | collective-permute-done | bytes 131104 | tf_op jit(solution)/shard_map/ppermute | solution.py:20
  142.5 3.1 %collective-permute-done.49.partner_ref.own_ref = bf16[8,64,128]{2,1,0:T(8,128)(2,1)S(1)} collective-permute-done((bf16[8,64,128]{2,1,0:T(8,128)(2,1)S(1)}, bf16[8,64,128]{2,1,0:T(8,128)(2,1)S(1)}, u32[]{:S(2)}, u32[]{:S(2)}) %collective-permute-start.49) | collective-permute-done | bytes 131104 | tf_op jit(solution)/shard_map/ppermute | solution.py:20
  145.9 2.2 %collective-permute-start.50 = (bf16[8,64,128]{2,1,0:T(8,128)(2,1)S(1)}, bf16[8,64,128]{2,1,0:T(8,128)(2,1)S(1)}, u32[]{:S(2)}, u32[]{:S(2)}) collective-permute-start(bf16[8,64,128]{2,1,0:T(8,128)(2,1)S(1)} %shard_map.129), channel_id=1, source_target_pairs={{0,96},{8,104},{16,112},{24,120},{32,64},{40,72},{48,80},{56,88},{... | collective-permute-start | bytes 393224 | tf_op jit(solution)/shard_map/ppermute | solution.py:20
  150.0 2.2 %collective-permute-done.50.partner_ref = bf16[8,64,128]{2,1,0:T(8,128)(2,1)S(1)} collective-permute-done((bf16[8,64,128]{2,1,0:T(8,128)(2,1)S(1)}, bf16[8,64,128]{2,1,0:T(8,128)(2,1)S(1)}, u32[]{:S(2)}, u32[]{:S(2)}) %collective-permute-start.50) | collective-permute-done | bytes 131104 | tf_op jit(solution)/shard_map/ppermute | solution.py:20
  152.4 2.2 %collective-permute-done.43.partner_ref = bf16[8,64,128]{2,1,0:T(8,128)(2,1)S(1)} collective-permute-done((bf16[8,64,128]{2,1,0:T(8,128)(2,1)S(1)}, bf16[8,64,128]{2,1,0:T(8,128)(2,1)S(1)}, u32[]{:S(2)}, u32[]{:S(2)}) %collective-permute-start.43) | collective-permute-done | bytes 131104 | tf_op jit(solution)/shard_map/ppermute | solution.py:20
  (156 shorter events, 61.9 us)
Async XLA Ops:
  5.1 29.5 %collective-permute-start.4 = (bf16[1,16,2,128,128]{4,3,2,1,0:T(8,128)(2,1)S(1)}, bf16[1,16,2,128,128]{4,3,2,1,0:T(8,128)(2,1)S(1)}, u32[]{:S(2)}, u32[]{:S(2)}) collective-permute-start(bf16[1,16,2,128,128]{4,3,2,1,0:T(8,128)(2,1)S(1)} %get-tuple-element.7.factor_ref), channel_id=1, source_target_pairs={{0,8},{8,0},{16,24},{24,16},{32,40},{40,32},{48,56},{56,48},{64,72... | collective-permute-start | bytes 3145736 | tf_op jit(solution)/shard_map/ppermute | solution.py:20
  7.2 43.9 %collective-permute-start.7 = (bf16[1,16,2,128,128]{4,3,2,1,0:T(8,128)(2,1)S(1)}, bf16[1,16,2,128,128]{4,3,2,1,0:T(8,128)(2,1)S(1)}, u32[]{:S(2)}, u32[]{:S(2)}) collective-permute-start(bf16[1,16,2,128,128]{4,3,2,1,0:T(8,128)(2,1)S(1)} %get-tuple-element.14.factor_ref), channel_id=1, source_target_pairs={{0,32},{8,40},{16,48},{24,56},{32,0},{40,8},{48,16},{56,24},{64,96... | collective-permute-start | bytes 3145736 | tf_op jit(solution)/shard_map/ppermute | solution.py:20
  11.1 6.4 %collective-permute-start.1 = (bf16[8,64,128]{2,1,0:T(8,128)(2,1)S(1)}, bf16[8,64,128]{2,1,0:T(8,128)(2,1)S(1)}, u32[]{:S(2)}, u32[]{:S(2)}) collective-permute-start(bf16[8,64,128]{2,1,0:T(8,128)(2,1)S(1)} %shard_map.57.own_ref), channel_id=1, source_target_pairs={{0,2},{1,3},{2,0},{3,1},{4,6},{5,7},{6,4},{7,5},{8,10},{9,11},{10,... | collective-permute-start | bytes 393224 | tf_op jit(solution)/shard_map/ppermute | solution.py:20
  12.9 8.0 %collective-permute-start.14 = (bf16[8,64,128]{2,1,0:T(8,128)(2,1)S(1)}, bf16[8,64,128]{2,1,0:T(8,128)(2,1)S(1)}, u32[]{:S(2)}, u32[]{:S(2)}) collective-permute-start(bf16[8,64,128]{2,1,0:T(8,128)(2,1)S(1)} %shard_map.73.own_ref), channel_id=1, source_target_pairs={{0,2},{1,3},{2,0},{3,1},{4,6},{5,7},{6,4},{7,5},{8,10},{9,11},{10,... | collective-permute-start | bytes 393224 | tf_op jit(solution)/shard_map/ppermute | solution.py:20
  17.7 7.9 %collective-permute-start.2 = (bf16[8,64,128]{2,1,0:T(8,128)(2,1)S(1)}, bf16[8,64,128]{2,1,0:T(8,128)(2,1)S(1)}, u32[]{:S(2)}, u32[]{:S(2)}) collective-permute-start(bf16[8,64,128]{2,1,0:T(8,128)(2,1)S(1)} %shard_map.58.own_ref), channel_id=1, source_target_pairs={{0,4},{1,5},{2,6},{3,7},{4,0},{5,1},{6,2},{7,3},{8,12},{9,13},{10,... | collective-permute-start | bytes 393224 | tf_op jit(solution)/shard_map/ppermute | solution.py:20
  21.1 6.6 %collective-permute-start.15 = (bf16[8,64,128]{2,1,0:T(8,128)(2,1)S(1)}, bf16[8,64,128]{2,1,0:T(8,128)(2,1)S(1)}, u32[]{:S(2)}, u32[]{:S(2)}) collective-permute-start(bf16[8,64,128]{2,1,0:T(8,128)(2,1)S(1)} %shard_map.74.own_ref), channel_id=1, source_target_pairs={{0,4},{1,5},{2,6},{3,7},{4,0},{5,1},{6,2},{7,3},{8,12},{9,13},{10,... | collective-permute-start | bytes 393224 | tf_op jit(solution)/shard_map/ppermute | solution.py:20
  27.9 46.5 %collective-permute-start.16 = (bf16[1,16,2,128,128]{4,3,2,1,0:T(8,128)(2,1)S(1)}, bf16[1,16,2,128,128]{4,3,2,1,0:T(8,128)(2,1)S(1)}, u32[]{:S(2)}, u32[]{:S(2)}) collective-permute-start(bf16[1,16,2,128,128]{4,3,2,1,0:T(8,128)(2,1)S(1)} %shard_map.76), channel_id=1, source_target_pairs={{0,2},{1,3},{2,0},{3,1},{4,6},{5,7},{6,4},{7,5},{8,10},{9,11},{10,... | collective-permute-start | bytes 3145736 | tf_op jit(solution)/shard_map/ppermute | solution.py:20
  29.1 9.4 %collective-permute-start.3 = (bf16[8,64,128]{2,1,0:T(8,128)(2,1)S(1)}, bf16[8,64,128]{2,1,0:T(8,128)(2,1)S(1)}, u32[]{:S(2)}, u32[]{:S(2)}) collective-permute-start(bf16[8,64,128]{2,1,0:T(8,128)(2,1)S(1)} %shard_map.59.own_ref.partner_ref.refs_0_), channel_id=1, source_target_pairs={{0,8},{8,0},{16,24},{24,16},{32,40},{40,32},{48,56},{56,48},{64,72... | collective-permute-start | bytes 393224 | tf_op jit(solution)/shard_map/ppermute | solution.py:20
  34.8 12.9 %collective-permute-start.20 = (bf16[8,64,128]{2,1,0:T(8,128)(2,1)S(1)}, bf16[8,64,128]{2,1,0:T(8,128)(2,1)S(1)}, u32[]{:S(2)}, u32[]{:S(2)}) collective-permute-start(bf16[8,64,128]{2,1,0:T(8,128)(2,1)S(1)} %shard_map.81), channel_id=1, source_target_pairs={{0,24},{8,16},{16,8},{24,0},{32,56},{40,48},{48,40},{56,32},{64,88... | collective-permute-start | bytes 393224 | tf_op jit(solution)/shard_map/ppermute | solution.py:20
  38.8 10.3 %collective-permute-start.5 = (bf16[8,64,128]{2,1,0:T(8,128)(2,1)S(1)}, bf16[8,64,128]{2,1,0:T(8,128)(2,1)S(1)}, u32[]{:S(2)}, u32[]{:S(2)}) collective-permute-start(bf16[8,64,128]{2,1,0:T(8,128)(2,1)S(1)} %shard_map.61), channel_id=1, source_target_pairs={{0,24},{8,16},{16,8},{24,0},{32,56},{40,48},{48,40},{56,32},{64,88... | collective-permute-start | bytes 393224 | tf_op jit(solution)/shard_map/ppermute | solution.py:20
  40.2 18.6 %collective-permute-start.10 = (bf16[16,64,128]{2,1,0:T(8,128)(2,1)S(1)}, bf16[16,64,128]{2,1,0:T(8,128)(2,1)S(1)}, u32[]{:S(2)}, u32[]{:S(2)}) collective-permute-start(bf16[16,64,128]{2,1,0:T(8,128)(2,1)S(1)} %shard_map.66.refs_1_), channel_id=1, source_target_pairs={{0,120},{8,0},{16,8},{24,16},{32,24},{40,32},{48,40},{56,48},{64,5... | collective-permute-start | bytes 786440 | tf_op jit(solution)/shard_map/ppermute | solution.py:25
  47.7 11.1 %collective-permute-start.9 = (bf16[16,64,128]{2,1,0:T(8,128)(2,1)S(1)}, bf16[16,64,128]{2,1,0:T(8,128)(2,1)S(1)}, u32[]{:S(2)}, u32[]{:S(2)}) collective-permute-start(bf16[16,64,128]{2,1,0:T(8,128)(2,1)S(1)} %shard_map.66.refs_1_), channel_id=1, source_target_pairs={{0,8},{8,16},{16,24},{24,32},{32,40},{40,48},{48,56},{56,64},{64,7... | collective-permute-start | bytes 786440 | tf_op jit(solution)/shard_map/ppermute | solution.py:25
  51.1 6.3 %collective-permute-start.6 = (bf16[8,64,128]{2,1,0:T(8,128)(2,1)S(1)}, bf16[8,64,128]{2,1,0:T(8,128)(2,1)S(1)}, u32[]{:S(2)}, u32[]{:S(2)}) collective-permute-start(bf16[8,64,128]{2,1,0:T(8,128)(2,1)S(1)} %shard_map.62.own_ref.partner_ref), channel_id=1, source_target_pairs={{0,32},{8,40},{16,48},{24,56},{32,0},{40,8},{48,16},{56,24},{64,96... | collective-permute-start | bytes 393224 | tf_op jit(solution)/shard_map/ppermute | solution.py:20
  54.9 6.6 %collective-permute-start.22 = (bf16[8,64,128]{2,1,0:T(8,128)(2,1)S(1)}, bf16[8,64,128]{2,1,0:T(8,128)(2,1)S(1)}, u32[]{:S(2)}, u32[]{:S(2)}) collective-permute-start(bf16[8,64,128]{2,1,0:T(8,128)(2,1)S(1)} %shard_map.84), channel_id=1, source_target_pairs={{0,96},{8,104},{16,112},{24,120},{32,64},{40,72},{48,80},{56,88},{... | collective-permute-start | bytes 393224 | tf_op jit(solution)/shard_map/ppermute | solution.py:20
  65.0 9.4 %collective-permute-start.33 = (bf16[8,64,128]{2,1,0:T(8,128)(2,1)S(1)}, bf16[8,64,128]{2,1,0:T(8,128)(2,1)S(1)}, u32[]{:S(2)}, u32[]{:S(2)}) collective-permute-start(bf16[8,64,128]{2,1,0:T(8,128)(2,1)S(1)} %shard_map.101.own_ref.partner_ref), channel_id=1, source_target_pairs={{0,2},{1,3},{2,0},{3,1},{4,6},{5,7},{6,4},{7,5},{8,10},{9,11},{10,... | collective-permute-start | bytes 393224 | tf_op jit(solution)/shard_map/ppermute | solution.py:20
  66.8 10.2 %collective-permute-start.12 = (bf16[8,64,128]{2,1,0:T(8,128)(2,1)S(1)}, bf16[8,64,128]{2,1,0:T(8,128)(2,1)S(1)}, u32[]{:S(2)}, u32[]{:S(2)}) collective-permute-start(bf16[8,64,128]{2,1,0:T(8,128)(2,1)S(1)} %shard_map.70.own_ref.partner_ref), channel_id=1, source_target_pairs={{0,2},{1,3},{2,0},{3,1},{4,6},{5,7},{6,4},{7,5},{8,10},{9,11},{10,... | collective-permute-start | bytes 393224 | tf_op jit(solution)/shard_map/ppermute | solution.py:20
  67.9 16.8 %collective-permute-start.24 = (bf16[16,64,128]{2,1,0:T(8,128)(2,1)S(1)}, bf16[16,64,128]{2,1,0:T(8,128)(2,1)S(1)}, u32[]{:S(2)}, u32[]{:S(2)}) collective-permute-start(bf16[16,64,128]{2,1,0:T(8,128)(2,1)S(1)} %shard_map.87.refs_1_), channel_id=1, source_target_pairs={{0,120},{8,0},{16,8},{24,16},{32,24},{40,32},{48,40},{56,48},{64,5... | collective-permute-start | bytes 786440 | tf_op jit(solution)/shard_map/ppermute | solution.py:25
  74.4 11.3 %collective-permute-start.23 = (bf16[16,64,128]{2,1,0:T(8,128)(2,1)S(1)}, bf16[16,64,128]{2,1,0:T(8,128)(2,1)S(1)}, u32[]{:S(2)}, u32[]{:S(2)}) collective-permute-start(bf16[16,64,128]{2,1,0:T(8,128)(2,1)S(1)} %shard_map.87.refs_1_), channel_id=1, source_target_pairs={{0,8},{8,16},{16,24},{24,32},{32,40},{40,48},{48,56},{56,64},{64,7... | collective-permute-start | bytes 786440 | tf_op jit(solution)/shard_map/ppermute | solution.py:25
  74.6 7.2 %collective-permute-start.34 = (bf16[8,64,128]{2,1,0:T(8,128)(2,1)S(1)}, bf16[8,64,128]{2,1,0:T(8,128)(2,1)S(1)}, u32[]{:S(2)}, u32[]{:S(2)}) collective-permute-start(bf16[8,64,128]{2,1,0:T(8,128)(2,1)S(1)} %shard_map.103), channel_id=1, source_target_pairs={{0,6},{1,7},{2,4},{3,5},{4,2},{5,3},{6,0},{7,1},{8,14},{9,15},{10,... | collective-permute-start | bytes 393224 | tf_op jit(solution)/shard_map/ppermute | solution.py:20
  77.3 6.7 %collective-permute-start.17 = (bf16[8,64,128]{2,1,0:T(8,128)(2,1)S(1)}, bf16[8,64,128]{2,1,0:T(8,128)(2,1)S(1)}, u32[]{:S(2)}, u32[]{:S(2)}) collective-permute-start(bf16[8,64,128]{2,1,0:T(8,128)(2,1)S(1)} %shard_map.77), channel_id=1, source_target_pairs={{0,6},{1,7},{2,4},{3,5},{4,2},{5,3},{6,0},{7,1},{8,14},{9,15},{10,... | collective-permute-start | bytes 393224 | tf_op jit(solution)/shard_map/ppermute | solution.py:20
  82.1 6.3 %collective-permute-start.35 = (bf16[8,64,128]{2,1,0:T(8,128)(2,1)S(1)}, bf16[8,64,128]{2,1,0:T(8,128)(2,1)S(1)}, u32[]{:S(2)}, u32[]{:S(2)}) collective-permute-start(bf16[8,64,128]{2,1,0:T(8,128)(2,1)S(1)} %shard_map.104.own_ref.partner_ref), channel_id=1, source_target_pairs={{0,8},{8,0},{16,24},{24,16},{32,40},{40,32},{48,56},{56,48},{64,72... | collective-permute-start | bytes 393224 | tf_op jit(solution)/shard_map/ppermute | solution.py:20
  84.2 9.4 %collective-permute-start.18 = (bf16[8,64,128]{2,1,0:T(8,128)(2,1)S(1)}, bf16[8,64,128]{2,1,0:T(8,128)(2,1)S(1)}, u32[]{:S(2)}, u32[]{:S(2)}) collective-permute-start(bf16[8,64,128]{2,1,0:T(8,128)(2,1)S(1)} %shard_map.78.own_ref.partner_ref), channel_id=1, source_target_pairs={{0,8},{8,0},{16,24},{24,16},{32,40},{40,32},{48,56},{56,48},{64,72... | collective-permute-start | bytes 393224 | tf_op jit(solution)/shard_map/ppermute | solution.py:20
  88.6 7.5 %collective-permute-start.36 = (bf16[8,64,128]{2,1,0:T(8,128)(2,1)S(1)}, bf16[8,64,128]{2,1,0:T(8,128)(2,1)S(1)}, u32[]{:S(2)}, u32[]{:S(2)}) collective-permute-start(bf16[8,64,128]{2,1,0:T(8,128)(2,1)S(1)} %shard_map.107), channel_id=1, source_target_pairs={{0,24},{8,16},{16,8},{24,0},{32,56},{40,48},{48,40},{56,32},{64,88... | collective-permute-start | bytes 393224 | tf_op jit(solution)/shard_map/ppermute | solution.py:20
  101.5 6.6 %collective-permute-start.38 = (bf16[8,64,128]{2,1,0:T(8,128)(2,1)S(1)}, bf16[8,64,128]{2,1,0:T(8,128)(2,1)S(1)}, u32[]{:S(2)}, u32[]{:S(2)}) collective-permute-start(bf16[8,64,128]{2,1,0:T(8,128)(2,1)S(1)} %shard_map.110), channel_id=1, source_target_pairs={{0,96},{8,104},{16,112},{24,120},{32,64},{40,72},{48,80},{56,88},{... | collective-permute-start | bytes 393224 | tf_op jit(solution)/shard_map/ppermute | solution.py:20
  112.9 6.4 %collective-permute-start.45 = (bf16[8,64,128]{2,1,0:T(8,128)(2,1)S(1)}, bf16[8,64,128]{2,1,0:T(8,128)(2,1)S(1)}, u32[]{:S(2)}, u32[]{:S(2)}) collective-permute-start(bf16[8,64,128]{2,1,0:T(8,128)(2,1)S(1)} %shard_map.120.own_ref.partner_ref), channel_id=1, source_target_pairs={{0,2},{1,3},{2,0},{3,1},{4,6},{5,7},{6,4},{7,5},{8,10},{9,11},{10,... | collective-permute-start | bytes 393224 | tf_op jit(solution)/shard_map/ppermute | solution.py:20
  114.2 7.5 %collective-permute-start.29 = (bf16[8,64,128]{2,1,0:T(8,128)(2,1)S(1)}, bf16[8,64,128]{2,1,0:T(8,128)(2,1)S(1)}, u32[]{:S(2)}, u32[]{:S(2)}) collective-permute-start(bf16[8,64,128]{2,1,0:T(8,128)(2,1)S(1)} %shard_map.95.own_ref.partner_ref), channel_id=1, source_target_pairs={{0,2},{1,3},{2,0},{3,1},{4,6},{5,7},{6,4},{7,5},{8,10},{9,11},{10,... | collective-permute-start | bytes 393224 | tf_op jit(solution)/shard_map/ppermute | solution.py:20
  115.4 13.6 %collective-permute-start.40 = (bf16[16,64,128]{2,1,0:T(8,128)(2,1)S(1)}, bf16[16,64,128]{2,1,0:T(8,128)(2,1)S(1)}, u32[]{:S(2)}, u32[]{:S(2)}) collective-permute-start(bf16[16,64,128]{2,1,0:T(8,128)(2,1)S(1)} %shard_map.112.refs_1_), channel_id=1, source_target_pairs={{0,120},{8,0},{16,8},{24,16},{32,24},{40,32},{48,40},{56,48},{64,5... | collective-permute-start | bytes 786440 | tf_op jit(solution)/shard_map/ppermute | solution.py:25
  117.4 11.5 %collective-permute-start.39 = (bf16[16,64,128]{2,1,0:T(8,128)(2,1)S(1)}, bf16[16,64,128]{2,1,0:T(8,128)(2,1)S(1)}, u32[]{:S(2)}, u32[]{:S(2)}) collective-permute-start(bf16[16,64,128]{2,1,0:T(8,128)(2,1)S(1)} %shard_map.112.refs_1_), channel_id=1, source_target_pairs={{0,8},{8,16},{16,24},{24,32},{32,40},{40,48},{48,56},{56,64},{64,7... | collective-permute-start | bytes 786440 | tf_op jit(solution)/shard_map/ppermute | solution.py:25
  119.5 6.5 %collective-permute-start.46 = (bf16[8,64,128]{2,1,0:T(8,128)(2,1)S(1)}, bf16[8,64,128]{2,1,0:T(8,128)(2,1)S(1)}, u32[]{:S(2)}, u32[]{:S(2)}) collective-permute-start(bf16[8,64,128]{2,1,0:T(8,128)(2,1)S(1)} %shard_map.122), channel_id=1, source_target_pairs={{0,6},{1,7},{2,4},{3,5},{4,2},{5,3},{6,0},{7,1},{8,14},{9,15},{10,... | collective-permute-start | bytes 393224 | tf_op jit(solution)/shard_map/ppermute | solution.py:20
  121.9 6.7 %collective-permute-start.30 = (bf16[8,64,128]{2,1,0:T(8,128)(2,1)S(1)}, bf16[8,64,128]{2,1,0:T(8,128)(2,1)S(1)}, u32[]{:S(2)}, u32[]{:S(2)}) collective-permute-start(bf16[8,64,128]{2,1,0:T(8,128)(2,1)S(1)} %shard_map.97), channel_id=1, source_target_pairs={{0,6},{1,7},{2,4},{3,5},{4,2},{5,3},{6,0},{7,1},{8,14},{9,15},{10,... | collective-permute-start | bytes 393224 | tf_op jit(solution)/shard_map/ppermute | solution.py:20
  132.3 7.6 %collective-permute-start.48 = (bf16[8,64,128]{2,1,0:T(8,128)(2,1)S(1)}, bf16[8,64,128]{2,1,0:T(8,128)(2,1)S(1)}, u32[]{:S(2)}, u32[]{:S(2)}) collective-permute-start(bf16[8,64,128]{2,1,0:T(8,128)(2,1)S(1)} %shard_map.126), channel_id=1, source_target_pairs={{0,24},{8,16},{16,8},{24,0},{32,56},{40,48},{48,40},{56,32},{64,88... | collective-permute-start | bytes 393224 | tf_op jit(solution)/shard_map/ppermute | solution.py:20
  141.5 6.6 %collective-permute-start.42 = (bf16[8,64,128]{2,1,0:T(8,128)(2,1)S(1)}, bf16[8,64,128]{2,1,0:T(8,128)(2,1)S(1)}, u32[]{:S(2)}, u32[]{:S(2)}) collective-permute-start(bf16[8,64,128]{2,1,0:T(8,128)(2,1)S(1)} %shard_map.115.own_ref.partner_ref), channel_id=1, source_target_pairs={{0,32},{8,40},{16,48},{24,56},{32,0},{40,8},{48,16},{56,24},{64,96... | collective-permute-start | bytes 393224 | tf_op jit(solution)/shard_map/ppermute | solution.py:20
  (23 other events, 241.9 us)

commit v3 on v2

--- a/solution.py
+++ b/solution.py
@@ -9,7 +9,7 @@
 
 ITERS = 3
 CHAINS = 2
-NEAR_RING = 1
+NEAR_TIES = ((1, 0, 0), (2, 0, 0))
 
 
 coupling = 0.4
@@ -54,25 +54,24 @@
         out_ref[b] = rows_ref[:, (start + b) * width:(start + b + 1) * width]
 
 
-def local_kernel(start, z_ref, *refs):
-    factors, out_ref = refs[:-1], refs[-1]
+def local_kernel(levels, start, z_ref, factor_ref, out_ref):
     blocks = z_ref.shape[0]
     mixed = [z_ref[b] for b in range(blocks)]
-    for level, factor in enumerate(factors):
+    for level in range(levels):
         mixed = [
-            pair_product(mixed[b], mixed[b ^ (1 << level)], factor[0, start + b]).astype(
-                jnp.bfloat16
-            )
+            pair_product(
+                mixed[b], mixed[b ^ (1 << level)], factor_ref[level, start + b]
+            ).astype(jnp.bfloat16)
             for b in range(blocks)
         ]
     for b in range(blocks):
         out_ref[b] = mixed[b]
 
 
-def level_kernel(start, own_ref, partner_ref, factor_ref, *refs):
+def level_kernel(level, start, own_ref, partner_ref, factor_ref, *refs):
     out_ref = refs[-1]
     for b in range(own_ref.shape[0]):
-        out_ref[b] = pair_product(own_ref[b], partner_ref[b], factor_ref[0, start + b]).astype(
+        out_ref[b] = pair_product(own_ref[b], partner_ref[b], factor_ref[level, start + b]).astype(
             jnp.bfloat16
         )
 
@@ -96,32 +95,37 @@
         )
 
 
-def take_kernel(*refs):
-    refs[-1][...] = refs[-2][...]
-
-
-def last_kernel(start, own_ref, partner_ref, factor_ref, near_ref, source_ref, out_ref):
+def take_kernel(level, *refs):
+    refs[-1][0] = refs[-2][level]
+
+
+def last_kernel(level, start, own_ref, partner_ref, factor_ref, near_ref, source_ref, out_ref):
     for b in range(own_ref.shape[0]):
-        mixed = pair_product(own_ref[b], partner_ref[b], factor_ref[0, start + b])
+        mixed = pair_product(own_ref[b], partner_ref[b], factor_ref[level, start + b])
         mixed = mixed.astype(jnp.bfloat16).astype(jnp.float32)
         total = source_ref[b].astype(jnp.float32) - coupling * (mixed + near_ref[b])
         out_ref[b] = total.astype(jnp.bfloat16)
 
 
-def stack_kernel(*refs):
+def stack_kernel(count, *refs):
     at = 0
-    for part in refs[:-1]:
+    for part in refs[:count]:
         refs[-1][at:at + part.shape[0]] = part[...]
         at += part.shape[0]
 
 
-def join_kernel(*refs):
-    at = 0
-    for part in refs[:-1]:
-        for b in range(part.shape[0]):
-            width = part.shape[-1]
-            refs[-1][:, at:at + width] = part[b]
-            at += width
+def final_kernel(
+    level, start, own_ref, partner_ref, factor_ref, near_ref, source_ref, before_ref, out_ref
+):
+    width = own_ref.shape[-1]
+    for b in range(start):
+        out_ref[:, b * width:(b + 1) * width] = before_ref[b]
+    for b in range(own_ref.shape[0]):
+        mixed = pair_product(own_ref[b], partner_ref[b], factor_ref[level, start + b])
+        mixed = mixed.astype(jnp.bfloat16).astype(jnp.float32)
+        total = source_ref[b].astype(jnp.float32) - coupling * (mixed + near_ref[b])
+        at = (start + b) * width
+        out_ref[:, at:at + width] = total.astype(jnp.bfloat16)
 
 
 def per_device(right_side, level_pairs, near_blocks, near_index, near_count):
@@ -137,20 +141,31 @@
     whole = jax.ShapeDtypeStruct((blocks, rhs_count, width), jnp.bfloat16)
     near_shape = jax.ShapeDtypeStruct((half, rhs_count, width), jnp.float32)
     one_level = jax.ShapeDtypeStruct((1, *level_pairs.shape[1:]), jnp.bfloat16)
+    flat = jax.ShapeDtypeStruct(right_side.shape, jnp.bfloat16)
     level_flops = 4 * half * rhs_count * width * width
     window_shape = pltpu.VMEM((3 * blocks + 1, rhs_count, width), jnp.bfloat16)
 
     rings = [
         (core + 1 + i, "level", 1 << (1 + i)) for i in range(0, level_bits - 1, 2)
     ] + [(core + level_bits + i, "patch", 1 << i) for i in range(0, patch_bits, 2)]
-    factors = [level_pairs[level:level + 1] for level in range(levels)]
-    partner_factors = {
-        level: exchange(factors[level], axis, flip) for level, axis, flip in rings[1:]
-    }
+    early = level_pairs[:core + 1]
+    factors = [(early, level) for level in range(core + 1)]
+    factors += [(level_pairs, level) for level in range(core + 1, levels)]
+
+    def sent(level, axis, flip, after):
+        taken = call(functools.partial(take_kernel, level), one_level, (*after, level_pairs), 0)
+        return exchange(taken, axis, flip)
+
+    level, axis, flip = rings[1]
+    partner_factors = {level: exchange(level_pairs[level:level + 1], axis, flip)}
 
     def product(kernel, c, own, partner, factor, *more, shape=piece):
+        pairs, level = factor
         return call(
-            functools.partial(kernel, c * half), shape, (own, partner, factor, *more), level_flops
+            functools.partial(kernel, level, c * half),
+            shape,
+            (own, partner, pairs, *more),
+            level_flops,
         )
 
     source = [
@@ -158,59 +173,72 @@
     ]
     current = list(source)
     for sweep in range(ITERS):
-        joined = call(stack_kernel, whole, current, 0)
-        below = shifted(joined, "patch", 1)
-        above = shifted(joined, "patch", -1)
         mixed = [
             call(
-                functools.partial(local_kernel, c * half),
+                functools.partial(local_kernel, core, c * half),
                 piece,
-                (current[c], *factors[:core]),
+                (current[c], early),
                 core * level_flops,
             )
             for c in chains
         ]
-        near = [
-            call(
+        def window_of(*after):
+            joined = call(functools.partial(stack_kernel, CHAINS), whole, (*current, *after), 0)
+            return shifted(joined, "patch", 1), joined, shifted(joined, "patch", -1)
+
+        def near_of(c):
+            return call(
                 functools.partial(near_kernel, c * half),
                 near_shape,
-                (near_index.T, near_count, below, joined, above, near_blocks),
+                (near_index.T, near_count, *window, near_blocks),
                 2 * half * slots * rhs_count * width * width,
                 (window_shape,),
             )
-            for c in chains
-        ]
+
+        ties = {(2, 0, 0): near_blocks}
+        if sweep > 0:
+            ties = {}
+            window = window_of()
+            near = [near_of(c) for c in chains]
+            ties[0, 1, 0] = window[0]
+            for c in chains:
+                ties[NEAR_TIES[c]] = near[c]
         for c in chains:
             partner = exchange(mixed[c], "level", 1)
             mixed[c] = product(level_kernel, c, mixed[c], partner, factors[core])
+        if sweep == 0:
+            for level, axis, flip in rings[2:]:
+                partner_factors[level] = sent(level, axis, flip, mixed)
         for ring, (level, axis, flip) in enumerate(rings):
             for c in chains:
                 partner = exchange(mixed[c], axis, flip)
                 own = product(level_kernel, c, mixed[c], partner, factors[level])
-                extra = (near[c],) if ring == NEAR_RING and sweep > 0 else ()
+                extra = [ties[ring, 0, c]] if (ring, 0, c) in ties else []
+                more = [ties[ring, 1, c]] if (ring, 1, c) in ties else []
                 if level in partner_factors:
                     theirs = product(
-                        level_kernel, c, partner, mixed[c], partner_factors[level], *extra
+                        level_kernel, c, partner, mixed[c], (partner_factors[level], 0), *extra
                     )
                     partner = exchange(theirs, axis, 3 * flip)
                 else:
                     partner = exchange(own, axis, 2 * flip)
                 second = factors[level + 1]
-                if ring == len(rings) - 1:
+                if ring == len(rings) - 1 and sweep == ITERS - 1 and c == CHAINS - 1:
+                    mixed[c] = product(
+                        final_kernel, c, own, partner, second, near[c], source[c], mixed[0],
+                        shape=flat,
+                    )
+                elif ring == len(rings) - 1:
                     mixed[c] = product(last_kernel, c, own, partner, second, near[c], source[c])
                 else:
-                    mixed[c] = product(level_kernel, c, own, partner, second)
+                    mixed[c] = product(level_kernel, c, own, partner, second, *more)
+            if sweep == 0 and ring == 1:
+                window = window_of(mixed[0])
+                near = [near_of(c) for c in chains]
             if level not in partner_factors:
-                partner_factors[level] = exchange(
-                    call(take_kernel, one_level, (*mixed, factors[level]), 0), axis, flip
-                )
+                partner_factors[level] = sent(level, axis, flip, mixed)
         current = mixed
-    return call(
-        join_kernel,
-        jax.ShapeDtypeStruct((rhs_count, blocks * width), jnp.bfloat16),
-        current,
-        0,
-    )
+    return current[-1]
 
 
 def solution(mesh):

time: 156 us -> 148 us (0.949)
  waiting for transfers between devices: 58.7 us -> 51 us
    ppermute x45, waiting for transfers between devices: 57.7 us -> 51 us  [exchange(): return lax.ppermute(block, axis, route)]
    ppermute x45, starting transfers between devices: 53.7 us -> 50.4 us  [exchange(): return lax.ppermute(block, axis, route)]
    ppermute x6, starting transfers between devices: 13 us -> 16.2 us  [shifted(): lax.ppermute(value, axis, [(i, (i + step) % count) for i in range(count)])]
    slice x1 -> x2, local copies, waits for them, and re-layouts: 5.14 us -> 3.94 us  [the longest x1 2.64 us: per_device(): early = level_pairs[:core + 1]]
  transfers between devices with their start and end apart: 51 -> 51, of which waited for: 29 -> 30; matrix products, arithmetic and copies ran while one was open for 0% -> 2% of each run, Pallas kernels for 15% -> 16%
where the time goes in v3:
time: 148 us
  starting transfers between devices  66.6 us (45%)
  waiting for transfers between devices  51 us (34%)
  Pallas kernels  24.2 us (16%)
  local copies, waits for them, and re-layouts  5.01 us (3%)
    ppermute x45, waiting for transfers between devices, exchange(): return lax.ppermute(block, axis, route)  51 us
    ppermute x45, starting transfers between devices, exchange(): return lax.ppermute(block, axis, route)  50.4 us
    pallas_call x77, Pallas kernels, call(): pl.pallas_call(kernel, out_shape=out_shape, in_specs=[place(op) for op in...  24.2 us
    ppermute x6, starting transfers between devices, shifted(): lax.ppermute(value, axis, [(i, (i + step) % count) for i in range(count)])  16.2 us
  transfers between devices with their start and end apart: 51, of which 30 were waited for; matrix products, arithmetic and copies ran while one was open for 2% of the time, Pallas kernels for 16%

profile of v3, /device:TPU:0, one launch (start us, length us, event | category | flops | bytes accessed | tf_op | source)
XLA Modules:
  0.0 147.7 jit_solution(1289955536454456095)
XLA Ops:
  1.3 2.1 %collective-permute-start.4 = (bf16[1,16,2,128,128]{4,3,2,1,0:T(8,128)(2,1)S(1)}, bf16[1,16,2,128,128]{4,3,2,1,0:T(8,128)(2,1)S(1)}, u32[]{:S(2)}, u32[]{:S(2)}) collective-permute-start(bf16[1,16,2,128,128]{4,3,2,1,0:T(8,128)(2,1)S(1)} %slice.7), channel_id=1, source_target_pairs={{0,8},{8,0},{16,24},{24,16},{32,40},{40,32},{48,56},{56,48},{64,72... | collective-permute-start | bytes 3145736 | tf_op jit(solution)/shard_map/ppermute | solution.py:20
  3.4 2.6 %slice.6.factor_ref = bf16[4,16,2,128,128]{4,3,2,1,0:T(8,128)(2,1)S(1)} slice(bf16[10,16,2,128,128]{4,3,2,1,0:T(8,128)(2,1)} %factor_ref.71), slice={[0:4], [0:16], [0:2], [0:128], [0:128]} | slice | bytes 8388608 | tf_op jit(solution)/shard_map/slice | solution.py:151
  13.5 4.3 %collective-permute-done.10.partner_ref = bf16[8,64,128]{2,1,0:T(8,128)(2,1)S(1)} collective-permute-done((bf16[8,64,128]{2,1,0:T(8,128)(2,1)S(1)}, bf16[8,64,128]{2,1,0:T(8,128)(2,1)S(1)}, u32[]{:S(2)}, u32[]{:S(2)}) %collective-permute-start.10) | collective-permute-done | bytes 131104 | tf_op jit(solution)/shard_map/ppermute | solution.py:20
  18.1 3.1 %collective-permute-start.11 = (bf16[8,64,128]{2,1,0:T(8,128)(2,1)S(1)}, bf16[8,64,128]{2,1,0:T(8,128)(2,1)S(1)}, u32[]{:S(2)}, u32[]{:S(2)}) collective-permute-start(bf16[8,64,128]{2,1,0:T(8,128)(2,1)S(1)} %shard_map.69.own_ref), channel_id=1, source_target_pairs={{0,4},{1,5},{2,6},{3,7},{4,0},{5,1},{6,2},{7,3},{8,12},{9,13},{10,... | collective-permute-start | bytes 393224 | tf_op jit(solution)/shard_map/ppermute | solution.py:20
  21.4 1.7 %collective-permute-start.2 = (bf16[8,64,128]{2,1,0:T(8,128)(2,1)S(1)}, bf16[8,64,128]{2,1,0:T(8,128)(2,1)S(1)}, u32[]{:S(2)}, u32[]{:S(2)}) collective-permute-start(bf16[8,64,128]{2,1,0:T(8,128)(2,1)S(1)} %shard_map.58.own_ref), channel_id=1, source_target_pairs={{0,4},{1,5},{2,6},{3,7},{4,0},{5,1},{6,2},{7,3},{8,12},{9,13},{10,... | collective-permute-start | bytes 393224 | tf_op jit(solution)/shard_map/ppermute | solution.py:20
  23.1 2.7 %collective-permute-done.11.partner_ref = bf16[8,64,128]{2,1,0:T(8,128)(2,1)S(1)} collective-permute-done((bf16[8,64,128]{2,1,0:T(8,128)(2,1)S(1)}, bf16[8,64,128]{2,1,0:T(8,128)(2,1)S(1)}, u32[]{:S(2)}, u32[]{:S(2)}) %collective-permute-start.11) | collective-permute-done | bytes 131104 | tf_op jit(solution)/shard_map/ppermute | solution.py:20
  26.1 1.9 %collective-permute-done.2.partner_ref = bf16[8,64,128]{2,1,0:T(8,128)(2,1)S(1)} collective-permute-done((bf16[8,64,128]{2,1,0:T(8,128)(2,1)S(1)}, bf16[8,64,128]{2,1,0:T(8,128)(2,1)S(1)}, u32[]{:S(2)}, u32[]{:S(2)}) %collective-permute-start.2) | collective-permute-done | bytes 131104 | tf_op jit(solution)/shard_map/ppermute | solution.py:20
  29.4 1.9 %collective-permute-start.3 = (bf16[8,64,128]{2,1,0:T(8,128)(2,1)S(1)}, bf16[8,64,128]{2,1,0:T(8,128)(2,1)S(1)}, u32[]{:S(2)}, u32[]{:S(2)}) collective-permute-start(bf16[8,64,128]{2,1,0:T(8,128)(2,1)S(1)} %shard_map.59.own_ref.partner_ref.refs_1_), channel_id=1, source_target_pairs={{0,8},{8,0},{16,24},{24,16},{32,40},{40,32},{48,56},{56,48},{64,72... | collective-permute-start | bytes 393224 | tf_op jit(solution)/shard_map/ppermute | solution.py:20
  31.3 3.2 %collective-permute-done.12.partner_ref.own_ref = bf16[8,64,128]{2,1,0:T(8,128)(2,1)S(1)} collective-permute-done((bf16[8,64,128]{2,1,0:T(8,128)(2,1)S(1)}, bf16[8,64,128]{2,1,0:T(8,128)(2,1)S(1)}, u32[]{:S(2)}, u32[]{:S(2)}) %collective-permute-start.12) | collective-permute-done | bytes 131104 | tf_op jit(solution)/shard_map/ppermute | solution.py:20
  34.8 2.6 %collective-permute-start.13 = (bf16[8,64,128]{2,1,0:T(8,128)(2,1)S(1)}, bf16[8,64,128]{2,1,0:T(8,128)(2,1)S(1)}, u32[]{:S(2)}, u32[]{:S(2)}) collective-permute-start(bf16[8,64,128]{2,1,0:T(8,128)(2,1)S(1)} %shard_map.72), channel_id=1, source_target_pairs={{0,24},{8,16},{16,8},{24,0},{32,56},{40,48},{48,40},{56,32},{64,88... | collective-permute-start | bytes 393224 | tf_op jit(solution)/shard_map/ppermute | solution.py:20
  39.0 2.3 %collective-permute-done.13.partner_ref = bf16[8,64,128]{2,1,0:T(8,128)(2,1)S(1)} collective-permute-done((bf16[8,64,128]{2,1,0:T(8,128)(2,1)S(1)}, bf16[8,64,128]{2,1,0:T(8,128)(2,1)S(1)}, u32[]{:S(2)}, u32[]{:S(2)}) %collective-permute-start.13) | collective-permute-done | bytes 131104 | tf_op jit(solution)/shard_map/ppermute | solution.py:20
  41.8 5.2 %collective-permute-start.15 = (bf16[16,64,128]{2,1,0:T(8,128)(2,1)S(1)}, bf16[16,64,128]{2,1,0:T(8,128)(2,1)S(1)}, u32[]{:S(2)}, u32[]{:S(2)}) collective-permute-start(bf16[16,64,128]{2,1,0:T(8,128)(2,1)S(1)} %shard_map.74.refs_1_), channel_id=1, source_target_pairs={{0,120},{8,0},{16,8},{24,16},{32,24},{40,32},{48,40},{56,48},{64,5... | collective-permute-start | bytes 786440 | tf_op jit(solution)/shard_map/ppermute | solution.py:25
  47.5 2.1 %collective-permute-start.6 = (bf16[8,64,128]{2,1,0:T(8,128)(2,1)S(1)}, bf16[8,64,128]{2,1,0:T(8,128)(2,1)S(1)}, u32[]{:S(2)}, u32[]{:S(2)}) collective-permute-start(bf16[8,64,128]{2,1,0:T(8,128)(2,1)S(1)} %shard_map.62.own_ref.partner_ref), channel_id=1, source_target_pairs={{0,32},{8,40},{16,48},{24,56},{32,0},{40,8},{48,16},{56,24},{64,96... | collective-permute-start | bytes 393224 | tf_op jit(solution)/shard_map/ppermute | solution.py:20
  49.6 2.6 %collective-permute-done.24.partner_ref.own_ref = bf16[8,64,128]{2,1,0:T(8,128)(2,1)S(1)} collective-permute-done((bf16[8,64,128]{2,1,0:T(8,128)(2,1)S(1)}, bf16[8,64,128]{2,1,0:T(8,128)(2,1)S(1)}, u32[]{:S(2)}, u32[]{:S(2)}) %collective-permute-start.24) | collective-permute-done | bytes 131104 | tf_op jit(solution)/shard_map/ppermute | solution.py:20
  54.1 1.9 %collective-permute-start.9 = (bf16[8,64,128]{2,1,0:T(8,128)(2,1)S(1)}, bf16[8,64,128]{2,1,0:T(8,128)(2,1)S(1)}, u32[]{:S(2)}, u32[]{:S(2)}) collective-permute-start(bf16[8,64,128]{2,1,0:T(8,128)(2,1)S(1)} %shard_map.68), channel_id=1, source_target_pairs={{0,96},{8,104},{16,112},{24,120},{32,64},{40,72},{48,80},{56,88},{... | collective-permute-start | bytes 393224 | tf_op jit(solution)/shard_map/ppermute | solution.py:20
  65.1 5.3 %collective-permute-start.27 = (bf16[16,64,128]{2,1,0:T(8,128)(2,1)S(1)}, bf16[16,64,128]{2,1,0:T(8,128)(2,1)S(1)}, u32[]{:S(2)}, u32[]{:S(2)}) collective-permute-start(bf16[16,64,128]{2,1,0:T(8,128)(2,1)S(1)} %shard_map.92.refs_1_), channel_id=1, source_target_pairs={{0,120},{8,0},{16,8},{24,16},{32,24},{40,32},{48,40},{56,48},{64,5... | collective-permute-start | bytes 786440 | tf_op jit(solution)/shard_map/ppermute | solution.py:25
  70.6 2.2 %collective-permute-start.37 = (bf16[8,64,128]{2,1,0:T(8,128)(2,1)S(1)}, bf16[8,64,128]{2,1,0:T(8,128)(2,1)S(1)}, u32[]{:S(2)}, u32[]{:S(2)}) collective-permute-start(bf16[8,64,128]{2,1,0:T(8,128)(2,1)S(1)} %shard_map.108), channel_id=1, source_target_pairs={{0,6},{1,7},{2,4},{3,5},{4,2},{5,3},{6,0},{7,1},{8,14},{9,15},{10,... | collective-permute-start | bytes 393224 | tf_op jit(solution)/shard_map/ppermute | solution.py:20
  74.5 3.7 %collective-permute-done.37.partner_ref = bf16[8,64,128]{2,1,0:T(8,128)(2,1)S(1)} collective-permute-done((bf16[8,64,128]{2,1,0:T(8,128)(2,1)S(1)}, bf16[8,64,128]{2,1,0:T(8,128)(2,1)S(1)}, u32[]{:S(2)}, u32[]{:S(2)}) %collective-permute-start.37) | collective-permute-done | bytes 131104 | tf_op jit(solution)/shard_map/ppermute | solution.py:20
  82.3 1.9 %collective-permute-done.38.partner_ref.own_ref = bf16[8,64,128]{2,1,0:T(8,128)(2,1)S(1)} collective-permute-done((bf16[8,64,128]{2,1,0:T(8,128)(2,1)S(1)}, bf16[8,64,128]{2,1,0:T(8,128)(2,1)S(1)}, u32[]{:S(2)}, u32[]{:S(2)}) %collective-permute-start.38) | collective-permute-done | bytes 131104 | tf_op jit(solution)/shard_map/ppermute | solution.py:20
  85.8 2.2 %collective-permute-start.21 = (bf16[8,64,128]{2,1,0:T(8,128)(2,1)S(1)}, bf16[8,64,128]{2,1,0:T(8,128)(2,1)S(1)}, u32[]{:S(2)}, u32[]{:S(2)}) collective-permute-start(bf16[8,64,128]{2,1,0:T(8,128)(2,1)S(1)} %shard_map.84), channel_id=1, source_target_pairs={{0,24},{8,16},{16,8},{24,0},{32,56},{40,48},{48,40},{56,32},{64,88... | collective-permute-start | bytes 393224 | tf_op jit(solution)/shard_map/ppermute | solution.py:20
  88.3 2.4 %collective-permute-done.39.partner_ref = bf16[8,64,128]{2,1,0:T(8,128)(2,1)S(1)} collective-permute-done((bf16[8,64,128]{2,1,0:T(8,128)(2,1)S(1)}, bf16[8,64,128]{2,1,0:T(8,128)(2,1)S(1)}, u32[]{:S(2)}, u32[]{:S(2)}) %collective-permute-start.39) | collective-permute-done | bytes 131104 | tf_op jit(solution)/shard_map/ppermute | solution.py:20
  97.6 2.2 %collective-permute-start.23 = (bf16[8,64,128]{2,1,0:T(8,128)(2,1)S(1)}, bf16[8,64,128]{2,1,0:T(8,128)(2,1)S(1)}, u32[]{:S(2)}, u32[]{:S(2)}) collective-permute-start(bf16[8,64,128]{2,1,0:T(8,128)(2,1)S(1)} %shard_map.87), channel_id=1, source_target_pairs={{0,96},{8,104},{16,112},{24,120},{32,64},{40,72},{48,80},{56,88},{... | collective-permute-start | bytes 393224 | tf_op jit(solution)/shard_map/ppermute | solution.py:20
  100.3 2.2 %collective-permute-done.41.partner_ref = bf16[8,64,128]{2,1,0:T(8,128)(2,1)S(1)} collective-permute-done((bf16[8,64,128]{2,1,0:T(8,128)(2,1)S(1)}, bf16[8,64,128]{2,1,0:T(8,128)(2,1)S(1)}, u32[]{:S(2)}, u32[]{:S(2)}) %collective-permute-start.41) | collective-permute-done | bytes 131104 | tf_op jit(solution)/shard_map/ppermute | solution.py:20
  107.4 5.3 %collective-permute-start.43 = (bf16[16,64,128]{2,1,0:T(8,128)(2,1)S(1)}, bf16[16,64,128]{2,1,0:T(8,128)(2,1)S(1)}, u32[]{:S(2)}, u32[]{:S(2)}) collective-permute-start(bf16[16,64,128]{2,1,0:T(8,128)(2,1)S(1)} %shard_map.117.refs_1_), channel_id=1, source_target_pairs={{0,120},{8,0},{16,8},{24,16},{32,24},{40,32},{48,40},{56,48},{64,5... | collective-permute-start | bytes 786440 | tf_op jit(solution)/shard_map/ppermute | solution.py:25
  114.5 2.3 %collective-permute-start.30 = (bf16[8,64,128]{2,1,0:T(8,128)(2,1)S(1)}, bf16[8,64,128]{2,1,0:T(8,128)(2,1)S(1)}, u32[]{:S(2)}, u32[]{:S(2)}) collective-permute-start(bf16[8,64,128]{2,1,0:T(8,128)(2,1)S(1)} %shard_map.98), channel_id=1, source_target_pairs={{0,6},{1,7},{2,4},{3,5},{4,2},{5,3},{6,0},{7,1},{8,14},{9,15},{10,... | collective-permute-start | bytes 393224 | tf_op jit(solution)/shard_map/ppermute | solution.py:20
  117.3 3.3 %collective-permute-done.46.partner_ref = bf16[8,64,128]{2,1,0:T(8,128)(2,1)S(1)} collective-permute-done((bf16[8,64,128]{2,1,0:T(8,128)(2,1)S(1)}, bf16[8,64,128]{2,1,0:T(8,128)(2,1)S(1)}, u32[]{:S(2)}, u32[]{:S(2)}) %collective-permute-start.46) | collective-permute-done | bytes 131104 | tf_op jit(solution)/shard_map/ppermute | solution.py:20
  124.4 2.0 %collective-permute-done.47.partner_ref.own_ref = bf16[8,64,128]{2,1,0:T(8,128)(2,1)S(1)} collective-permute-done((bf16[8,64,128]{2,1,0:T(8,128)(2,1)S(1)}, bf16[8,64,128]{2,1,0:T(8,128)(2,1)S(1)}, u32[]{:S(2)}, u32[]{:S(2)}) %collective-permute-start.47) | collective-permute-done | bytes 131104 | tf_op jit(solution)/shard_map/ppermute | solution.py:20
  128.0 2.2 %collective-permute-start.32 = (bf16[8,64,128]{2,1,0:T(8,128)(2,1)S(1)}, bf16[8,64,128]{2,1,0:T(8,128)(2,1)S(1)}, u32[]{:S(2)}, u32[]{:S(2)}) collective-permute-start(bf16[8,64,128]{2,1,0:T(8,128)(2,1)S(1)} %shard_map.101), channel_id=1, source_target_pairs={{0,24},{8,16},{16,8},{24,0},{32,56},{40,48},{48,40},{56,32},{64,88... | collective-permute-start | bytes 393224 | tf_op jit(solution)/shard_map/ppermute | solution.py:20
  130.7 2.2 %collective-permute-done.48.partner_ref = bf16[8,64,128]{2,1,0:T(8,128)(2,1)S(1)} collective-permute-done((bf16[8,64,128]{2,1,0:T(8,128)(2,1)S(1)}, bf16[8,64,128]{2,1,0:T(8,128)(2,1)S(1)}, u32[]{:S(2)}, u32[]{:S(2)}) %collective-permute-start.48) | collective-permute-done | bytes 131104 | tf_op jit(solution)/shard_map/ppermute | solution.py:20
  138.4 1.9 %collective-permute-start.50 = (bf16[8,64,128]{2,1,0:T(8,128)(2,1)S(1)}, bf16[8,64,128]{2,1,0:T(8,128)(2,1)S(1)}, u32[]{:S(2)}, u32[]{:S(2)}) collective-permute-start(bf16[8,64,128]{2,1,0:T(8,128)(2,1)S(1)} %shard_map.129), channel_id=1, source_target_pairs={{0,96},{8,104},{16,112},{24,120},{32,64},{40,72},{48,80},{56,88},{... | collective-permute-start | bytes 393224 | tf_op jit(solution)/shard_map/ppermute | solution.py:20
  142.5 2.2 %collective-permute-done.50.partner_ref = bf16[8,64,128]{2,1,0:T(8,128)(2,1)S(1)} collective-permute-done((bf16[8,64,128]{2,1,0:T(8,128)(2,1)S(1)}, bf16[8,64,128]{2,1,0:T(8,128)(2,1)S(1)}, u32[]{:S(2)}, u32[]{:S(2)}) %collective-permute-start.50) | collective-permute-done | bytes 131104 | tf_op jit(solution)/shard_map/ppermute | solution.py:20
  144.9 1.9 %collective-permute-done.34.partner_ref = bf16[8,64,128]{2,1,0:T(8,128)(2,1)S(1)} collective-permute-done((bf16[8,64,128]{2,1,0:T(8,128)(2,1)S(1)}, bf16[8,64,128]{2,1,0:T(8,128)(2,1)S(1)}, u32[]{:S(2)}, u32[]{:S(2)}) %collective-permute-start.34) | collective-permute-done | bytes 131104 | tf_op jit(solution)/shard_map/ppermute | solution.py:20
  (164 shorter events, 61.2 us)
Async XLA Ops:
  1.3 33.2 %collective-permute-start.4 = (bf16[1,16,2,128,128]{4,3,2,1,0:T(8,128)(2,1)S(1)}, bf16[1,16,2,128,128]{4,3,2,1,0:T(8,128)(2,1)S(1)}, u32[]{:S(2)}, u32[]{:S(2)}) collective-permute-start(bf16[1,16,2,128,128]{4,3,2,1,0:T(8,128)(2,1)S(1)} %slice.7), channel_id=1, source_target_pairs={{0,8},{8,0},{16,24},{24,16},{32,40},{40,32},{48,56},{56,48},{64,72... | collective-permute-start | bytes 3145736 | tf_op jit(solution)/shard_map/ppermute | solution.py:20
  9.8 37.7 %collective-permute-start.8 = (bf16[1,16,2,128,128]{4,3,2,1,0:T(8,128)(2,1)S(1)}, bf16[1,16,2,128,128]{4,3,2,1,0:T(8,128)(2,1)S(1)}, u32[]{:S(2)}, u32[]{:S(2)}) collective-permute-start(bf16[1,16,2,128,128]{4,3,2,1,0:T(8,128)(2,1)S(1)} %shard_map.67), channel_id=1, source_target_pairs={{0,32},{8,40},{16,48},{24,56},{32,0},{40,8},{48,16},{56,24},{64,96... | collective-permute-start | bytes 3145736 | tf_op jit(solution)/shard_map/ppermute | solution.py:20
  11.5 6.4 %collective-permute-start.10 = (bf16[8,64,128]{2,1,0:T(8,128)(2,1)S(1)}, bf16[8,64,128]{2,1,0:T(8,128)(2,1)S(1)}, u32[]{:S(2)}, u32[]{:S(2)}) collective-permute-start(bf16[8,64,128]{2,1,0:T(8,128)(2,1)S(1)} %shard_map.66.refs_0_.own_ref), channel_id=1, source_target_pairs={{0,2},{1,3},{2,0},{3,1},{4,6},{5,7},{6,4},{7,5},{8,10},{9,11},{10,... | collective-permute-start | bytes 393224 | tf_op jit(solution)/shard_map/ppermute | solution.py:20
  13.0 8.2 %collective-permute-start.1 = (bf16[8,64,128]{2,1,0:T(8,128)(2,1)S(1)}, bf16[8,64,128]{2,1,0:T(8,128)(2,1)S(1)}, u32[]{:S(2)}, u32[]{:S(2)}) collective-permute-start(bf16[8,64,128]{2,1,0:T(8,128)(2,1)S(1)} %shard_map.57.own_ref.refs_1_), channel_id=1, source_target_pairs={{0,2},{1,3},{2,0},{3,1},{4,6},{5,7},{6,4},{7,5},{8,10},{9,11},{10,... | collective-permute-start | bytes 393224 | tf_op jit(solution)/shard_map/ppermute | solution.py:20
  18.1 7.8 %collective-permute-start.11 = (bf16[8,64,128]{2,1,0:T(8,128)(2,1)S(1)}, bf16[8,64,128]{2,1,0:T(8,128)(2,1)S(1)}, u32[]{:S(2)}, u32[]{:S(2)}) collective-permute-start(bf16[8,64,128]{2,1,0:T(8,128)(2,1)S(1)} %shard_map.69.own_ref), channel_id=1, source_target_pairs={{0,4},{1,5},{2,6},{3,7},{4,0},{5,1},{6,2},{7,3},{8,12},{9,13},{10,... | collective-permute-start | bytes 393224 | tf_op jit(solution)/shard_map/ppermute | solution.py:20
  21.4 6.6 %collective-permute-start.2 = (bf16[8,64,128]{2,1,0:T(8,128)(2,1)S(1)}, bf16[8,64,128]{2,1,0:T(8,128)(2,1)S(1)}, u32[]{:S(2)}, u32[]{:S(2)}) collective-permute-start(bf16[8,64,128]{2,1,0:T(8,128)(2,1)S(1)} %shard_map.58.own_ref), channel_id=1, source_target_pairs={{0,4},{1,5},{2,6},{3,7},{4,0},{5,1},{6,2},{7,3},{8,12},{9,13},{10,... | collective-permute-start | bytes 393224 | tf_op jit(solution)/shard_map/ppermute | solution.py:20
  28.3 42.1 %collective-permute-start.18 = (bf16[1,16,2,128,128]{4,3,2,1,0:T(8,128)(2,1)S(1)}, bf16[1,16,2,128,128]{4,3,2,1,0:T(8,128)(2,1)S(1)}, u32[]{:S(2)}, u32[]{:S(2)}) collective-permute-start(bf16[1,16,2,128,128]{4,3,2,1,0:T(8,128)(2,1)S(1)} %shard_map.80), channel_id=1, source_target_pairs={{0,2},{1,3},{2,0},{3,1},{4,6},{5,7},{6,4},{7,5},{8,10},{9,11},{10,... | collective-permute-start | bytes 3145736 | tf_op jit(solution)/shard_map/ppermute | solution.py:20
  29.4 7.9 %collective-permute-start.3 = (bf16[8,64,128]{2,1,0:T(8,128)(2,1)S(1)}, bf16[8,64,128]{2,1,0:T(8,128)(2,1)S(1)}, u32[]{:S(2)}, u32[]{:S(2)}) collective-permute-start(bf16[8,64,128]{2,1,0:T(8,128)(2,1)S(1)} %shard_map.59.own_ref.partner_ref.refs_1_), channel_id=1, source_target_pairs={{0,8},{8,0},{16,24},{24,16},{32,40},{40,32},{48,56},{56,48},{64,72... | collective-permute-start | bytes 393224 | tf_op jit(solution)/shard_map/ppermute | solution.py:20
  34.8 6.6 %collective-permute-start.13 = (bf16[8,64,128]{2,1,0:T(8,128)(2,1)S(1)}, bf16[8,64,128]{2,1,0:T(8,128)(2,1)S(1)}, u32[]{:S(2)}, u32[]{:S(2)}) collective-permute-start(bf16[8,64,128]{2,1,0:T(8,128)(2,1)S(1)} %shard_map.72), channel_id=1, source_target_pairs={{0,24},{8,16},{16,8},{24,0},{32,56},{40,48},{48,40},{56,32},{64,88... | collective-permute-start | bytes 393224 | tf_op jit(solution)/shard_map/ppermute | solution.py:20
  37.6 9.4 %collective-permute-start.5 = (bf16[8,64,128]{2,1,0:T(8,128)(2,1)S(1)}, bf16[8,64,128]{2,1,0:T(8,128)(2,1)S(1)}, u32[]{:S(2)}, u32[]{:S(2)}) collective-permute-start(bf16[8,64,128]{2,1,0:T(8,128)(2,1)S(1)} %shard_map.61), channel_id=1, source_target_pairs={{0,24},{8,16},{16,8},{24,0},{32,56},{40,48},{48,40},{56,32},{64,88... | collective-permute-start | bytes 393224 | tf_op jit(solution)/shard_map/ppermute | solution.py:20
  41.6 15.0 %collective-permute-start.14 = (bf16[16,64,128]{2,1,0:T(8,128)(2,1)S(1)}, bf16[16,64,128]{2,1,0:T(8,128)(2,1)S(1)}, u32[]{:S(2)}, u32[]{:S(2)}) collective-permute-start(bf16[16,64,128]{2,1,0:T(8,128)(2,1)S(1)} %shard_map.74.refs_1_), channel_id=1, source_target_pairs={{0,8},{8,16},{16,24},{24,32},{32,40},{40,48},{48,56},{56,64},{64,7... | collective-permute-start | bytes 786440 | tf_op jit(solution)/shard_map/ppermute | solution.py:25
  41.8 14.7 %collective-permute-start.15 = (bf16[16,64,128]{2,1,0:T(8,128)(2,1)S(1)}, bf16[16,64,128]{2,1,0:T(8,128)(2,1)S(1)}, u32[]{:S(2)}, u32[]{:S(2)}) collective-permute-start(bf16[16,64,128]{2,1,0:T(8,128)(2,1)S(1)} %shard_map.74.refs_1_), channel_id=1, source_target_pairs={{0,120},{8,0},{16,8},{24,16},{32,24},{40,32},{48,40},{56,48},{64,5... | collective-permute-start | bytes 786440 | tf_op jit(solution)/shard_map/ppermute | solution.py:25
  47.5 6.4 %collective-permute-start.6 = (bf16[8,64,128]{2,1,0:T(8,128)(2,1)S(1)}, bf16[8,64,128]{2,1,0:T(8,128)(2,1)S(1)}, u32[]{:S(2)}, u32[]{:S(2)}) collective-permute-start(bf16[8,64,128]{2,1,0:T(8,128)(2,1)S(1)} %shard_map.62.own_ref.partner_ref), channel_id=1, source_target_pairs={{0,32},{8,40},{16,48},{24,56},{32,0},{40,8},{48,16},{56,24},{64,96... | collective-permute-start | bytes 393224 | tf_op jit(solution)/shard_map/ppermute | solution.py:20
  54.1 6.6 %collective-permute-start.9 = (bf16[8,64,128]{2,1,0:T(8,128)(2,1)S(1)}, bf16[8,64,128]{2,1,0:T(8,128)(2,1)S(1)}, u32[]{:S(2)}, u32[]{:S(2)}) collective-permute-start(bf16[8,64,128]{2,1,0:T(8,128)(2,1)S(1)} %shard_map.68), channel_id=1, source_target_pairs={{0,96},{8,104},{16,112},{24,120},{32,64},{40,72},{48,80},{56,88},{... | collective-permute-start | bytes 393224 | tf_op jit(solution)/shard_map/ppermute | solution.py:20
  62.5 7.9 %collective-permute-start.36 = (bf16[8,64,128]{2,1,0:T(8,128)(2,1)S(1)}, bf16[8,64,128]{2,1,0:T(8,128)(2,1)S(1)}, u32[]{:S(2)}, u32[]{:S(2)}) collective-permute-start(bf16[8,64,128]{2,1,0:T(8,128)(2,1)S(1)} %shard_map.106.own_ref.partner_ref), channel_id=1, source_target_pairs={{0,2},{1,3},{2,0},{3,1},{4,6},{5,7},{6,4},{7,5},{8,10},{9,11},{10,... | collective-permute-start | bytes 393224 | tf_op jit(solution)/shard_map/ppermute | solution.py:20
  63.1 11.4 %collective-permute-start.26 = (bf16[16,64,128]{2,1,0:T(8,128)(2,1)S(1)}, bf16[16,64,128]{2,1,0:T(8,128)(2,1)S(1)}, u32[]{:S(2)}, u32[]{:S(2)}) collective-permute-start(bf16[16,64,128]{2,1,0:T(8,128)(2,1)S(1)} %shard_map.92.refs_1_), channel_id=1, source_target_pairs={{0,8},{8,16},{16,24},{24,32},{32,40},{40,48},{48,56},{56,64},{64,7... | collective-permute-start | bytes 786440 | tf_op jit(solution)/shard_map/ppermute | solution.py:25
  63.5 9.3 %collective-permute-start.17 = (bf16[8,64,128]{2,1,0:T(8,128)(2,1)S(1)}, bf16[8,64,128]{2,1,0:T(8,128)(2,1)S(1)}, u32[]{:S(2)}, u32[]{:S(2)}) collective-permute-start(bf16[8,64,128]{2,1,0:T(8,128)(2,1)S(1)} %shard_map.78.own_ref.partner_ref), channel_id=1, source_target_pairs={{0,2},{1,3},{2,0},{3,1},{4,6},{5,7},{6,4},{7,5},{8,10},{9,11},{10,... | collective-permute-start | bytes 393224 | tf_op jit(solution)/shard_map/ppermute | solution.py:20
  65.1 16.0 %collective-permute-start.27 = (bf16[16,64,128]{2,1,0:T(8,128)(2,1)S(1)}, bf16[16,64,128]{2,1,0:T(8,128)(2,1)S(1)}, u32[]{:S(2)}, u32[]{:S(2)}) collective-permute-start(bf16[16,64,128]{2,1,0:T(8,128)(2,1)S(1)} %shard_map.92.refs_1_), channel_id=1, source_target_pairs={{0,120},{8,0},{16,8},{24,16},{32,24},{40,32},{48,40},{56,48},{64,5... | collective-permute-start | bytes 786440 | tf_op jit(solution)/shard_map/ppermute | solution.py:25
  70.6 7.6 %collective-permute-start.37 = (bf16[8,64,128]{2,1,0:T(8,128)(2,1)S(1)}, bf16[8,64,128]{2,1,0:T(8,128)(2,1)S(1)}, u32[]{:S(2)}, u32[]{:S(2)}) collective-permute-start(bf16[8,64,128]{2,1,0:T(8,128)(2,1)S(1)} %shard_map.108), channel_id=1, source_target_pairs={{0,6},{1,7},{2,4},{3,5},{4,2},{5,3},{6,0},{7,1},{8,14},{9,15},{10,... | collective-permute-start | bytes 393224 | tf_op jit(solution)/shard_map/ppermute | solution.py:20
  73.0 6.6 %collective-permute-start.19 = (bf16[8,64,128]{2,1,0:T(8,128)(2,1)S(1)}, bf16[8,64,128]{2,1,0:T(8,128)(2,1)S(1)}, u32[]{:S(2)}, u32[]{:S(2)}) collective-permute-start(bf16[8,64,128]{2,1,0:T(8,128)(2,1)S(1)} %shard_map.81), channel_id=1, source_target_pairs={{0,6},{1,7},{2,4},{3,5},{4,2},{5,3},{6,0},{7,1},{8,14},{9,15},{10,... | collective-permute-start | bytes 393224 | tf_op jit(solution)/shard_map/ppermute | solution.py:20
  84.4 6.3 %collective-permute-start.39 = (bf16[8,64,128]{2,1,0:T(8,128)(2,1)S(1)}, bf16[8,64,128]{2,1,0:T(8,128)(2,1)S(1)}, u32[]{:S(2)}, u32[]{:S(2)}) collective-permute-start(bf16[8,64,128]{2,1,0:T(8,128)(2,1)S(1)} %shard_map.112), channel_id=1, source_target_pairs={{0,24},{8,16},{16,8},{24,0},{32,56},{40,48},{48,40},{56,32},{64,88... | collective-permute-start | bytes 393224 | tf_op jit(solution)/shard_map/ppermute | solution.py:20
  85.8 6.3 %collective-permute-start.21 = (bf16[8,64,128]{2,1,0:T(8,128)(2,1)S(1)}, bf16[8,64,128]{2,1,0:T(8,128)(2,1)S(1)}, u32[]{:S(2)}, u32[]{:S(2)}) collective-permute-start(bf16[8,64,128]{2,1,0:T(8,128)(2,1)S(1)} %shard_map.84), channel_id=1, source_target_pairs={{0,24},{8,16},{16,8},{24,0},{32,56},{40,48},{48,40},{56,32},{64,88... | collective-permute-start | bytes 393224 | tf_op jit(solution)/shard_map/ppermute | solution.py:20
  96.2 6.3 %collective-permute-start.41 = (bf16[8,64,128]{2,1,0:T(8,128)(2,1)S(1)}, bf16[8,64,128]{2,1,0:T(8,128)(2,1)S(1)}, u32[]{:S(2)}, u32[]{:S(2)}) collective-permute-start(bf16[8,64,128]{2,1,0:T(8,128)(2,1)S(1)} %shard_map.115), channel_id=1, source_target_pairs={{0,96},{8,104},{16,112},{24,120},{32,64},{40,72},{48,80},{56,88},{... | collective-permute-start | bytes 393224 | tf_op jit(solution)/shard_map/ppermute | solution.py:20
  97.6 6.3 %collective-permute-start.23 = (bf16[8,64,128]{2,1,0:T(8,128)(2,1)S(1)}, bf16[8,64,128]{2,1,0:T(8,128)(2,1)S(1)}, u32[]{:S(2)}, u32[]{:S(2)}) collective-permute-start(bf16[8,64,128]{2,1,0:T(8,128)(2,1)S(1)} %shard_map.87), channel_id=1, source_target_pairs={{0,96},{8,104},{16,112},{24,120},{32,64},{40,72},{48,80},{56,88},{... | collective-permute-start | bytes 393224 | tf_op jit(solution)/shard_map/ppermute | solution.py:20
  105.0 7.8 %collective-permute-start.45 = (bf16[8,64,128]{2,1,0:T(8,128)(2,1)S(1)}, bf16[8,64,128]{2,1,0:T(8,128)(2,1)S(1)}, u32[]{:S(2)}, u32[]{:S(2)}) collective-permute-start(bf16[8,64,128]{2,1,0:T(8,128)(2,1)S(1)} %shard_map.120.own_ref.partner_ref), channel_id=1, source_target_pairs={{0,2},{1,3},{2,0},{3,1},{4,6},{5,7},{6,4},{7,5},{8,10},{9,11},{10,... | collective-permute-start | bytes 393224 | tf_op jit(solution)/shard_map/ppermute | solution.py:20
  105.1 12.2 %collective-permute-start.42 = (bf16[16,64,128]{2,1,0:T(8,128)(2,1)S(1)}, bf16[16,64,128]{2,1,0:T(8,128)(2,1)S(1)}, u32[]{:S(2)}, u32[]{:S(2)}) collective-permute-start(bf16[16,64,128]{2,1,0:T(8,128)(2,1)S(1)} %shard_map.117.refs_1_), channel_id=1, source_target_pairs={{0,8},{8,16},{16,24},{24,32},{32,40},{40,48},{48,56},{56,64},{64,7... | collective-permute-start | bytes 786440 | tf_op jit(solution)/shard_map/ppermute | solution.py:25
  106.3 8.0 %collective-permute-start.29 = (bf16[8,64,128]{2,1,0:T(8,128)(2,1)S(1)}, bf16[8,64,128]{2,1,0:T(8,128)(2,1)S(1)}, u32[]{:S(2)}, u32[]{:S(2)}) collective-permute-start(bf16[8,64,128]{2,1,0:T(8,128)(2,1)S(1)} %shard_map.96.own_ref.partner_ref), channel_id=1, source_target_pairs={{0,2},{1,3},{2,0},{3,1},{4,6},{5,7},{6,4},{7,5},{8,10},{9,11},{10,... | collective-permute-start | bytes 393224 | tf_op jit(solution)/shard_map/ppermute | solution.py:20
  107.4 15.9 %collective-permute-start.43 = (bf16[16,64,128]{2,1,0:T(8,128)(2,1)S(1)}, bf16[16,64,128]{2,1,0:T(8,128)(2,1)S(1)}, u32[]{:S(2)}, u32[]{:S(2)}) collective-permute-start(bf16[16,64,128]{2,1,0:T(8,128)(2,1)S(1)} %shard_map.117.refs_1_), channel_id=1, source_target_pairs={{0,120},{8,0},{16,8},{24,16},{32,24},{40,32},{48,40},{56,48},{64,5... | collective-permute-start | bytes 786440 | tf_op jit(solution)/shard_map/ppermute | solution.py:25
  113.0 7.6 %collective-permute-start.46 = (bf16[8,64,128]{2,1,0:T(8,128)(2,1)S(1)}, bf16[8,64,128]{2,1,0:T(8,128)(2,1)S(1)}, u32[]{:S(2)}, u32[]{:S(2)}) collective-permute-start(bf16[8,64,128]{2,1,0:T(8,128)(2,1)S(1)} %shard_map.122), channel_id=1, source_target_pairs={{0,6},{1,7},{2,4},{3,5},{4,2},{5,3},{6,0},{7,1},{8,14},{9,15},{10,... | collective-permute-start | bytes 393224 | tf_op jit(solution)/shard_map/ppermute | solution.py:20
  114.5 7.5 %collective-permute-start.30 = (bf16[8,64,128]{2,1,0:T(8,128)(2,1)S(1)}, bf16[8,64,128]{2,1,0:T(8,128)(2,1)S(1)}, u32[]{:S(2)}, u32[]{:S(2)}) collective-permute-start(bf16[8,64,128]{2,1,0:T(8,128)(2,1)S(1)} %shard_map.98), channel_id=1, source_target_pairs={{0,6},{1,7},{2,4},{3,5},{4,2},{5,3},{6,0},{7,1},{8,14},{9,15},{10,... | collective-permute-start | bytes 393224 | tf_op jit(solution)/shard_map/ppermute | solution.py:20
  126.6 6.3 %collective-permute-start.48 = (bf16[8,64,128]{2,1,0:T(8,128)(2,1)S(1)}, bf16[8,64,128]{2,1,0:T(8,128)(2,1)S(1)}, u32[]{:S(2)}, u32[]{:S(2)}) collective-permute-start(bf16[8,64,128]{2,1,0:T(8,128)(2,1)S(1)} %shard_map.126), channel_id=1, source_target_pairs={{0,24},{8,16},{16,8},{24,0},{32,56},{40,48},{48,40},{56,32},{64,88... | collective-permute-start | bytes 393224 | tf_op jit(solution)/shard_map/ppermute | solution.py:20
  128.0 6.3 %collective-permute-start.32 = (bf16[8,64,128]{2,1,0:T(8,128)(2,1)S(1)}, bf16[8,64,128]{2,1,0:T(8,128)(2,1)S(1)}, u32[]{:S(2)}, u32[]{:S(2)}) collective-permute-start(bf16[8,64,128]{2,1,0:T(8,128)(2,1)S(1)} %shard_map.101), channel_id=1, source_target_pairs={{0,24},{8,16},{16,8},{24,0},{32,56},{40,48},{48,40},{56,32},{64,88... | collective-permute-start | bytes 393224 | tf_op jit(solution)/shard_map/ppermute | solution.py:20
  (26 other events, 105.4 us)

commit v4 on v3

--- a/solution.py
+++ b/solution.py
@@ -20,9 +20,12 @@
     return lax.ppermute(block, axis, route)
 
 
-def shifted(value, axis, step):
+def exchange_next(block, axis):
     count = lax.axis_size(axis)
-    return lax.ppermute(value, axis, [(i, (i + step) % count) for i in range(count)])
+    route = []
+    for i in range(1, count, 2):
+        route += [(i, (i + 1) % count), ((i + 1) % count, i)]
+    return lax.ppermute(block, axis, route)
 
 
 def pair_product(own, partner, factor):
@@ -85,9 +88,17 @@
         window[unused:unused + piece.shape[0]] = piece[...]
         unused += piece.shape[0]
     window[unused] = jnp.zeros(window.shape[1:], window.dtype)
+    last = 2 * near_ref.shape[0]
+    even = lax.axis_index("patch") % 2 == 0
+    below, above = jnp.where(even, last, 0), jnp.where(even, -last, 0)
+
+    def place_of(k, b):
+        at = index_ref[k, b]
+        shift = jnp.where(at < last // 2, below, jnp.where(at < last, 0, above))
+        return jnp.where(k < count_ref[b], at + shift, unused)
+
     for b in range(start, start + blocks):
-        count = count_ref[b]
-        taken = [window[jnp.where(k < count, index_ref[k, b], unused)] for k in range(slots)]
+        taken = [window[place_of(k, b)] for k in range(slots)]
         out_ref[b - start] = jnp.dot(
             jnp.concatenate(taken, axis=-1),
             near_ref[b].reshape(slots * width, width),
@@ -156,8 +167,9 @@
         taken = call(functools.partial(take_kernel, level), one_level, (*after, level_pairs), 0)
         return exchange(taken, axis, flip)
 
-    level, axis, flip = rings[1]
-    partner_factors = {level: exchange(level_pairs[level:level + 1], axis, flip)}
+    partner_factors = {
+        level: exchange(level_pairs[level:level + 1], axis, flip) for level, axis, flip in rings[1:]
+    }
 
     def product(kernel, c, own, partner, factor, *more, shape=piece):
         pairs, level = factor
@@ -184,7 +196,7 @@
         ]
         def window_of(*after):
             joined = call(functools.partial(stack_kernel, CHAINS), whole, (*current, *after), 0)
-            return shifted(joined, "patch", 1), joined, shifted(joined, "patch", -1)
+            return exchange(joined, "patch", 1), joined, exchange_next(joined, "patch")
 
         def near_of(c):
             return call(
@@ -206,9 +218,6 @@
         for c in chains:
             partner = exchange(mixed[c], "level", 1)
             mixed[c] = product(level_kernel, c, mixed[c], partner, factors[core])
-        if sweep == 0:
-            for level, axis, flip in rings[2:]:
-                partner_factors[level] = sent(level, axis, flip, mixed)
         for ring, (level, axis, flip) in enumerate(rings):
             for c in chains:
                 partner = exchange(mixed[c], axis, flip)

time: 148 us -> 145 us (0.980)
  starting transfers between devices: 66.6 us -> 62.4 us
  waiting for transfers between devices: 51 us -> 52.5 us
    ppermute x6 -> x3, starting transfers between devices: 16.2 us -> 9.47 us  [exchange_next(): return lax.ppermute(block, axis, route)]
    ppermute x45 -> x48, starting transfers between devices: 50.4 us -> 53 us  [exchange(): return lax.ppermute(block, axis, route)]
    ppermute x45 -> x48, waiting for transfers between devices: 51 us -> 52.5 us  [exchange(): return lax.ppermute(block, axis, route)]
    pallas_call x77 -> x76, Pallas kernels: 24.2 us -> 24.2 us  [call(): pl.pallas_call(kernel, out_shape=out_shape, in_specs=[place(op) for op in...]
  transfers between devices with their start and end apart: 51 -> 51, of which waited for: 30 -> 29; matrix products, arithmetic and copies ran while one was open for 2% -> 2% of each run, Pallas kernels for 16% -> 16%
where the time goes in v4:
time: 145 us; the launch traced here: 144 us
  starting transfers between devices  62.4 us (43%)
  waiting for transfers between devices  52.5 us (36%)
  Pallas kernels  24.2 us (17%)
  local copies, waits for them, and re-layouts  4.41 us (3%)
    ppermute x48, starting transfers between devices, exchange(): return lax.ppermute(block, axis, route)  53 us
    ppermute x48, waiting for transfers between devices, exchange(): return lax.ppermute(block, axis, route)  52.5 us
    pallas_call x76, Pallas kernels, call(): pl.pallas_call(kernel, out_shape=out_shape, in_specs=[place(op) for op in...  24.2 us
    ppermute x3, starting transfers between devices, exchange_next(): return lax.ppermute(block, axis, route)  9.47 us
  transfers between devices with their start and end apart: 51, of which 29 were waited for; matrix products, arithmetic and copies ran while one was open for 2% of the time, Pallas kernels for 16%

profile of v4, /device:TPU:0, one launch (start us, length us, event | category | flops | bytes accessed | tf_op | source)
XLA Modules:
  0.0 144.4 jit_solution(6027045799998553883)
XLA Ops:
  1.7 2.1 %collective-permute-start.4 = (bf16[1,16,2,128,128]{4,3,2,1,0:T(8,128)(2,1)S(1)}, bf16[1,16,2,128,128]{4,3,2,1,0:T(8,128)(2,1)S(1)}, u32[]{:S(2)}, u32[]{:S(2)}) collective-permute-start(bf16[1,16,2,128,128]{4,3,2,1,0:T(8,128)(2,1)S(1)} %get-tuple-element.6), channel_id=1, source_target_pairs={{0,8},{8,0},{16,24},{24,16},{32,40},{40,32},{48,56},{56,48},{64,72... | collective-permute-start | bytes 3145736 | tf_op jit(solution)/shard_map/ppermute | solution.py:20
  5.4 2.6 %slice.9.factor_ref = bf16[4,16,2,128,128]{4,3,2,1,0:T(8,128)(2,1)S(1)} slice(bf16[10,16,2,128,128]{4,3,2,1,0:T(8,128)(2,1)} %factor_ref.71), slice={[0:4], [0:16], [0:2], [0:128], [0:128]} | slice | bytes 8388608 | tf_op jit(solution)/shard_map/slice | solution.py:162
  12.7 4.0 %collective-permute-done.10.partner_ref = bf16[8,64,128]{2,1,0:T(8,128)(2,1)S(1)} collective-permute-done((bf16[8,64,128]{2,1,0:T(8,128)(2,1)S(1)}, bf16[8,64,128]{2,1,0:T(8,128)(2,1)S(1)}, u32[]{:S(2)}, u32[]{:S(2)}) %collective-permute-start.10) | collective-permute-done | bytes 131104 | tf_op jit(solution)/shard_map/ppermute | solution.py:20
  17.0 3.1 %collective-permute-start.11 = (bf16[8,64,128]{2,1,0:T(8,128)(2,1)S(1)}, bf16[8,64,128]{2,1,0:T(8,128)(2,1)S(1)}, u32[]{:S(2)}, u32[]{:S(2)}) collective-permute-start(bf16[8,64,128]{2,1,0:T(8,128)(2,1)S(1)} %shard_map.68.own_ref), channel_id=1, source_target_pairs={{0,4},{1,5},{2,6},{3,7},{4,0},{5,1},{6,2},{7,3},{8,12},{9,13},{10,... | collective-permute-start | bytes 393224 | tf_op jit(solution)/shard_map/ppermute | solution.py:20
  20.3 1.8 %collective-permute-start.2 = (bf16[8,64,128]{2,1,0:T(8,128)(2,1)S(1)}, bf16[8,64,128]{2,1,0:T(8,128)(2,1)S(1)}, u32[]{:S(2)}, u32[]{:S(2)}) collective-permute-start(bf16[8,64,128]{2,1,0:T(8,128)(2,1)S(1)} %shard_map.58.own_ref), channel_id=1, source_target_pairs={{0,4},{1,5},{2,6},{3,7},{4,0},{5,1},{6,2},{7,3},{8,12},{9,13},{10,... | collective-permute-start | bytes 393224 | tf_op jit(solution)/shard_map/ppermute | solution.py:20
  22.1 2.7 %collective-permute-done.11.partner_ref = bf16[8,64,128]{2,1,0:T(8,128)(2,1)S(1)} collective-permute-done((bf16[8,64,128]{2,1,0:T(8,128)(2,1)S(1)}, bf16[8,64,128]{2,1,0:T(8,128)(2,1)S(1)}, u32[]{:S(2)}, u32[]{:S(2)}) %collective-permute-start.11) | collective-permute-done | bytes 131104 | tf_op jit(solution)/shard_map/ppermute | solution.py:20
  25.0 1.8 %collective-permute-done.2.partner_ref = bf16[8,64,128]{2,1,0:T(8,128)(2,1)S(1)} collective-permute-done((bf16[8,64,128]{2,1,0:T(8,128)(2,1)S(1)}, bf16[8,64,128]{2,1,0:T(8,128)(2,1)S(1)}, u32[]{:S(2)}, u32[]{:S(2)}) %collective-permute-start.2) | collective-permute-done | bytes 131104 | tf_op jit(solution)/shard_map/ppermute | solution.py:20
  28.3 1.9 %collective-permute-start.3 = (bf16[8,64,128]{2,1,0:T(8,128)(2,1)S(1)}, bf16[8,64,128]{2,1,0:T(8,128)(2,1)S(1)}, u32[]{:S(2)}, u32[]{:S(2)}) collective-permute-start(bf16[8,64,128]{2,1,0:T(8,128)(2,1)S(1)} %shard_map.59.own_ref.partner_ref.refs_1_), channel_id=1, source_target_pairs={{0,8},{8,0},{16,24},{24,16},{32,40},{40,32},{48,56},{56,48},{64,72... | collective-permute-start | bytes 393224 | tf_op jit(solution)/shard_map/ppermute | solution.py:20
  30.2 3.5 %collective-permute-done.12.partner_ref.own_ref = bf16[8,64,128]{2,1,0:T(8,128)(2,1)S(1)} collective-permute-done((bf16[8,64,128]{2,1,0:T(8,128)(2,1)S(1)}, bf16[8,64,128]{2,1,0:T(8,128)(2,1)S(1)}, u32[]{:S(2)}, u32[]{:S(2)}) %collective-permute-start.12) | collective-permute-done | bytes 131104 | tf_op jit(solution)/shard_map/ppermute | solution.py:20
  34.0 2.6 %collective-permute-start.13 = (bf16[8,64,128]{2,1,0:T(8,128)(2,1)S(1)}, bf16[8,64,128]{2,1,0:T(8,128)(2,1)S(1)}, u32[]{:S(2)}, u32[]{:S(2)}) collective-permute-start(bf16[8,64,128]{2,1,0:T(8,128)(2,1)S(1)} %shard_map.71), channel_id=1, source_target_pairs={{0,24},{8,16},{16,8},{24,0},{32,56},{40,48},{48,40},{56,32},{64,88... | collective-permute-start | bytes 393224 | tf_op jit(solution)/shard_map/ppermute | solution.py:20
  38.2 2.3 %collective-permute-done.13.partner_ref = bf16[8,64,128]{2,1,0:T(8,128)(2,1)S(1)} collective-permute-done((bf16[8,64,128]{2,1,0:T(8,128)(2,1)S(1)}, bf16[8,64,128]{2,1,0:T(8,128)(2,1)S(1)}, u32[]{:S(2)}, u32[]{:S(2)}) %collective-permute-start.13) | collective-permute-done | bytes 131104 | tf_op jit(solution)/shard_map/ppermute | solution.py:20
  40.9 4.2 %collective-permute-start.15 = (bf16[16,64,128]{2,1,0:T(8,128)(2,1)S(1)}, bf16[16,64,128]{2,1,0:T(8,128)(2,1)S(1)}, u32[]{:S(2)}, u32[]{:S(2)}) collective-permute-start(bf16[16,64,128]{2,1,0:T(8,128)(2,1)S(1)} %shard_map.73.refs_1_), channel_id=1, source_target_pairs={{8,16},{16,8},{24,32},{32,24},{40,48},{48,40},{56,64},{64,56},{72,... | collective-permute-start | bytes 786440 | tf_op jit(solution)/shard_map/ppermute | solution.py:28
  47.7 3.8 %collective-permute-done.24.partner_ref.own_ref = bf16[8,64,128]{2,1,0:T(8,128)(2,1)S(1)} collective-permute-done((bf16[8,64,128]{2,1,0:T(8,128)(2,1)S(1)}, bf16[8,64,128]{2,1,0:T(8,128)(2,1)S(1)}, u32[]{:S(2)}, u32[]{:S(2)}) %collective-permute-start.24) | collective-permute-done | bytes 131104 | tf_op jit(solution)/shard_map/ppermute | solution.py:20
  53.6 1.8 %collective-permute-start.8 = (bf16[8,64,128]{2,1,0:T(8,128)(2,1)S(1)}, bf16[8,64,128]{2,1,0:T(8,128)(2,1)S(1)}, u32[]{:S(2)}, u32[]{:S(2)}) collective-permute-start(bf16[8,64,128]{2,1,0:T(8,128)(2,1)S(1)} %shard_map.64), channel_id=1, source_target_pairs={{0,96},{8,104},{16,112},{24,120},{32,64},{40,72},{48,80},{56,88},{... | collective-permute-start | bytes 393224 | tf_op jit(solution)/shard_map/ppermute | solution.py:20
  64.4 2.5 %collective-permute-start.27 = (bf16[16,64,128]{2,1,0:T(8,128)(2,1)S(1)}, bf16[16,64,128]{2,1,0:T(8,128)(2,1)S(1)}, u32[]{:S(2)}, u32[]{:S(2)}) collective-permute-start(bf16[16,64,128]{2,1,0:T(8,128)(2,1)S(1)} %shard_map.91.refs_1_), channel_id=1, source_target_pairs={{8,16},{16,8},{24,32},{32,24},{40,48},{48,40},{56,64},{64,56},{72,... | collective-permute-start | bytes 786440 | tf_op jit(solution)/shard_map/ppermute | solution.py:28
  68.5 1.9 %collective-permute-start.37 = (bf16[8,64,128]{2,1,0:T(8,128)(2,1)S(1)}, bf16[8,64,128]{2,1,0:T(8,128)(2,1)S(1)}, u32[]{:S(2)}, u32[]{:S(2)}) collective-permute-start(bf16[8,64,128]{2,1,0:T(8,128)(2,1)S(1)} %shard_map.107), channel_id=1, source_target_pairs={{0,6},{1,7},{2,4},{3,5},{4,2},{5,3},{6,0},{7,1},{8,14},{9,15},{10,... | collective-permute-start | bytes 393224 | tf_op jit(solution)/shard_map/ppermute | solution.py:20
  70.6 1.8 %collective-permute-start.19 = (bf16[8,64,128]{2,1,0:T(8,128)(2,1)S(1)}, bf16[8,64,128]{2,1,0:T(8,128)(2,1)S(1)}, u32[]{:S(2)}, u32[]{:S(2)}) collective-permute-start(bf16[8,64,128]{2,1,0:T(8,128)(2,1)S(1)} %shard_map.80), channel_id=1, source_target_pairs={{0,6},{1,7},{2,4},{3,5},{4,2},{5,3},{6,0},{7,1},{8,14},{9,15},{10,... | collective-permute-start | bytes 393224 | tf_op jit(solution)/shard_map/ppermute | solution.py:20
  72.7 3.5 %collective-permute-done.37.partner_ref = bf16[8,64,128]{2,1,0:T(8,128)(2,1)S(1)} collective-permute-done((bf16[8,64,128]{2,1,0:T(8,128)(2,1)S(1)}, bf16[8,64,128]{2,1,0:T(8,128)(2,1)S(1)}, u32[]{:S(2)}, u32[]{:S(2)}) %collective-permute-start.37) | collective-permute-done | bytes 131104 | tf_op jit(solution)/shard_map/ppermute | solution.py:20
  80.2 1.9 %collective-permute-done.38.partner_ref.own_ref = bf16[8,64,128]{2,1,0:T(8,128)(2,1)S(1)} collective-permute-done((bf16[8,64,128]{2,1,0:T(8,128)(2,1)S(1)}, bf16[8,64,128]{2,1,0:T(8,128)(2,1)S(1)}, u32[]{:S(2)}, u32[]{:S(2)}) %collective-permute-start.38) | collective-permute-done | bytes 131104 | tf_op jit(solution)/shard_map/ppermute | solution.py:20
  83.8 2.2 %collective-permute-start.21 = (bf16[8,64,128]{2,1,0:T(8,128)(2,1)S(1)}, bf16[8,64,128]{2,1,0:T(8,128)(2,1)S(1)}, u32[]{:S(2)}, u32[]{:S(2)}) collective-permute-start(bf16[8,64,128]{2,1,0:T(8,128)(2,1)S(1)} %shard_map.83), channel_id=1, source_target_pairs={{0,24},{8,16},{16,8},{24,0},{32,56},{40,48},{48,40},{56,32},{64,88... | collective-permute-start | bytes 393224 | tf_op jit(solution)/shard_map/ppermute | solution.py:20
  86.2 2.4 %collective-permute-done.39.partner_ref = bf16[8,64,128]{2,1,0:T(8,128)(2,1)S(1)} collective-permute-done((bf16[8,64,128]{2,1,0:T(8,128)(2,1)S(1)}, bf16[8,64,128]{2,1,0:T(8,128)(2,1)S(1)}, u32[]{:S(2)}, u32[]{:S(2)}) %collective-permute-start.39) | collective-permute-done | bytes 131104 | tf_op jit(solution)/shard_map/ppermute | solution.py:20
  95.9 1.8 %collective-permute-start.23 = (bf16[8,64,128]{2,1,0:T(8,128)(2,1)S(1)}, bf16[8,64,128]{2,1,0:T(8,128)(2,1)S(1)}, u32[]{:S(2)}, u32[]{:S(2)}) collective-permute-start(bf16[8,64,128]{2,1,0:T(8,128)(2,1)S(1)} %shard_map.86), channel_id=1, source_target_pairs={{0,96},{8,104},{16,112},{24,120},{32,64},{40,72},{48,80},{56,88},{... | collective-permute-start | bytes 393224 | tf_op jit(solution)/shard_map/ppermute | solution.py:20
  98.2 2.2 %collective-permute-done.41.partner_ref = bf16[8,64,128]{2,1,0:T(8,128)(2,1)S(1)} collective-permute-done((bf16[8,64,128]{2,1,0:T(8,128)(2,1)S(1)}, bf16[8,64,128]{2,1,0:T(8,128)(2,1)S(1)}, u32[]{:S(2)}, u32[]{:S(2)}) %collective-permute-start.41) | collective-permute-done | bytes 131104 | tf_op jit(solution)/shard_map/ppermute | solution.py:20
  105.8 2.7 %collective-permute-start.43 = (bf16[16,64,128]{2,1,0:T(8,128)(2,1)S(1)}, bf16[16,64,128]{2,1,0:T(8,128)(2,1)S(1)}, u32[]{:S(2)}, u32[]{:S(2)}) collective-permute-start(bf16[16,64,128]{2,1,0:T(8,128)(2,1)S(1)} %shard_map.116.refs_1_), channel_id=1, source_target_pairs={{8,16},{16,8},{24,32},{32,24},{40,48},{48,40},{56,64},{64,56},{72,... | collective-permute-start | bytes 786440 | tf_op jit(solution)/shard_map/ppermute | solution.py:28
  109.9 2.2 %collective-permute-start.46 = (bf16[8,64,128]{2,1,0:T(8,128)(2,1)S(1)}, bf16[8,64,128]{2,1,0:T(8,128)(2,1)S(1)}, u32[]{:S(2)}, u32[]{:S(2)}) collective-permute-start(bf16[8,64,128]{2,1,0:T(8,128)(2,1)S(1)} %shard_map.121), channel_id=1, source_target_pairs={{0,6},{1,7},{2,4},{3,5},{4,2},{5,3},{6,0},{7,1},{8,14},{9,15},{10,... | collective-permute-start | bytes 393224 | tf_op jit(solution)/shard_map/ppermute | solution.py:20
  112.4 2.4 %collective-permute-start.30 = (bf16[8,64,128]{2,1,0:T(8,128)(2,1)S(1)}, bf16[8,64,128]{2,1,0:T(8,128)(2,1)S(1)}, u32[]{:S(2)}, u32[]{:S(2)}) collective-permute-start(bf16[8,64,128]{2,1,0:T(8,128)(2,1)S(1)} %shard_map.97), channel_id=1, source_target_pairs={{0,6},{1,7},{2,4},{3,5},{4,2},{5,3},{6,0},{7,1},{8,14},{9,15},{10,... | collective-permute-start | bytes 393224 | tf_op jit(solution)/shard_map/ppermute | solution.py:20
  116.5 2.5 %collective-permute-done.30.partner_ref = bf16[8,64,128]{2,1,0:T(8,128)(2,1)S(1)} collective-permute-done((bf16[8,64,128]{2,1,0:T(8,128)(2,1)S(1)}, bf16[8,64,128]{2,1,0:T(8,128)(2,1)S(1)}, u32[]{:S(2)}, u32[]{:S(2)}) %collective-permute-start.30) | collective-permute-done | bytes 131104 | tf_op jit(solution)/shard_map/ppermute | solution.py:20
  120.5 1.8 %collective-permute-done.47.partner_ref.own_ref = bf16[8,64,128]{2,1,0:T(8,128)(2,1)S(1)} collective-permute-done((bf16[8,64,128]{2,1,0:T(8,128)(2,1)S(1)}, bf16[8,64,128]{2,1,0:T(8,128)(2,1)S(1)}, u32[]{:S(2)}, u32[]{:S(2)}) %collective-permute-start.47) | collective-permute-done | bytes 131104 | tf_op jit(solution)/shard_map/ppermute | solution.py:20
  124.5 1.8 %collective-permute-start.32 = (bf16[8,64,128]{2,1,0:T(8,128)(2,1)S(1)}, bf16[8,64,128]{2,1,0:T(8,128)(2,1)S(1)}, u32[]{:S(2)}, u32[]{:S(2)}) collective-permute-start(bf16[8,64,128]{2,1,0:T(8,128)(2,1)S(1)} %shard_map.100), channel_id=1, source_target_pairs={{0,24},{8,16},{16,8},{24,0},{32,56},{40,48},{48,40},{56,32},{64,88... | collective-permute-start | bytes 393224 | tf_op jit(solution)/shard_map/ppermute | solution.py:20
  126.8 2.9 %collective-permute-done.48.partner_ref = bf16[8,64,128]{2,1,0:T(8,128)(2,1)S(1)} collective-permute-done((bf16[8,64,128]{2,1,0:T(8,128)(2,1)S(1)}, bf16[8,64,128]{2,1,0:T(8,128)(2,1)S(1)}, u32[]{:S(2)}, u32[]{:S(2)}) %collective-permute-start.48) | collective-permute-done | bytes 131104 | tf_op jit(solution)/shard_map/ppermute | solution.py:20
  135.2 1.8 %collective-permute-start.50 = (bf16[8,64,128]{2,1,0:T(8,128)(2,1)S(1)}, bf16[8,64,128]{2,1,0:T(8,128)(2,1)S(1)}, u32[]{:S(2)}, u32[]{:S(2)}) collective-permute-start(bf16[8,64,128]{2,1,0:T(8,128)(2,1)S(1)} %shard_map.128), channel_id=1, source_target_pairs={{0,96},{8,104},{16,112},{24,120},{32,64},{40,72},{48,80},{56,88},{... | collective-permute-start | bytes 393224 | tf_op jit(solution)/shard_map/ppermute | solution.py:20
  139.3 2.2 %collective-permute-done.50.partner_ref = bf16[8,64,128]{2,1,0:T(8,128)(2,1)S(1)} collective-permute-done((bf16[8,64,128]{2,1,0:T(8,128)(2,1)S(1)}, bf16[8,64,128]{2,1,0:T(8,128)(2,1)S(1)}, u32[]{:S(2)}, u32[]{:S(2)}) %collective-permute-start.50) | collective-permute-done | bytes 131104 | tf_op jit(solution)/shard_map/ppermute | solution.py:20
  (163 shorter events, 64.9 us)
Async XLA Ops:
  1.7 32.0 %collective-permute-start.4 = (bf16[1,16,2,128,128]{4,3,2,1,0:T(8,128)(2,1)S(1)}, bf16[1,16,2,128,128]{4,3,2,1,0:T(8,128)(2,1)S(1)}, u32[]{:S(2)}, u32[]{:S(2)}) collective-permute-start(bf16[1,16,2,128,128]{4,3,2,1,0:T(8,128)(2,1)S(1)} %get-tuple-element.6), channel_id=1, source_target_pairs={{0,8},{8,0},{16,24},{24,16},{32,40},{40,32},{48,56},{56,48},{64,72... | collective-permute-start | bytes 3145736 | tf_op jit(solution)/shard_map/ppermute | solution.py:20
  3.8 43.0 %collective-permute-start.7 = (bf16[1,16,2,128,128]{4,3,2,1,0:T(8,128)(2,1)S(1)}, bf16[1,16,2,128,128]{4,3,2,1,0:T(8,128)(2,1)S(1)}, u32[]{:S(2)}, u32[]{:S(2)}) collective-permute-start(bf16[1,16,2,128,128]{4,3,2,1,0:T(8,128)(2,1)S(1)} %get-tuple-element.5), channel_id=1, source_target_pairs={{0,32},{8,40},{16,48},{24,56},{32,0},{40,8},{48,16},{56,24},{64,96... | collective-permute-start | bytes 3145736 | tf_op jit(solution)/shard_map/ppermute | solution.py:20
  10.3 6.4 %collective-permute-start.10 = (bf16[8,64,128]{2,1,0:T(8,128)(2,1)S(1)}, bf16[8,64,128]{2,1,0:T(8,128)(2,1)S(1)}, u32[]{:S(2)}, u32[]{:S(2)}) collective-permute-start(bf16[8,64,128]{2,1,0:T(8,128)(2,1)S(1)} %shard_map.67.own_ref), channel_id=1, source_target_pairs={{0,2},{1,3},{2,0},{3,1},{4,6},{5,7},{6,4},{7,5},{8,10},{9,11},{10,... | collective-permute-start | bytes 393224 | tf_op jit(solution)/shard_map/ppermute | solution.py:20
  12.1 8.0 %collective-permute-start.1 = (bf16[8,64,128]{2,1,0:T(8,128)(2,1)S(1)}, bf16[8,64,128]{2,1,0:T(8,128)(2,1)S(1)}, u32[]{:S(2)}, u32[]{:S(2)}) collective-permute-start(bf16[8,64,128]{2,1,0:T(8,128)(2,1)S(1)} %shard_map.57.own_ref), channel_id=1, source_target_pairs={{0,2},{1,3},{2,0},{3,1},{4,6},{5,7},{6,4},{7,5},{8,10},{9,11},{10,... | collective-permute-start | bytes 393224 | tf_op jit(solution)/shard_map/ppermute | solution.py:20
  17.0 7.8 %collective-permute-start.11 = (bf16[8,64,128]{2,1,0:T(8,128)(2,1)S(1)}, bf16[8,64,128]{2,1,0:T(8,128)(2,1)S(1)}, u32[]{:S(2)}, u32[]{:S(2)}) collective-permute-start(bf16[8,64,128]{2,1,0:T(8,128)(2,1)S(1)} %shard_map.68.own_ref), channel_id=1, source_target_pairs={{0,4},{1,5},{2,6},{3,7},{4,0},{5,1},{6,2},{7,3},{8,12},{9,13},{10,... | collective-permute-start | bytes 393224 | tf_op jit(solution)/shard_map/ppermute | solution.py:20
  20.3 6.6 %collective-permute-start.2 = (bf16[8,64,128]{2,1,0:T(8,128)(2,1)S(1)}, bf16[8,64,128]{2,1,0:T(8,128)(2,1)S(1)}, u32[]{:S(2)}, u32[]{:S(2)}) collective-permute-start(bf16[8,64,128]{2,1,0:T(8,128)(2,1)S(1)} %shard_map.58.own_ref), channel_id=1, source_target_pairs={{0,4},{1,5},{2,6},{3,7},{4,0},{5,1},{6,2},{7,3},{8,12},{9,13},{10,... | collective-permute-start | bytes 393224 | tf_op jit(solution)/shard_map/ppermute | solution.py:20
  27.2 39.8 %collective-permute-start.18 = (bf16[1,16,2,128,128]{4,3,2,1,0:T(8,128)(2,1)S(1)}, bf16[1,16,2,128,128]{4,3,2,1,0:T(8,128)(2,1)S(1)}, u32[]{:S(2)}, u32[]{:S(2)}) collective-permute-start(bf16[1,16,2,128,128]{4,3,2,1,0:T(8,128)(2,1)S(1)} %shard_map.79), channel_id=1, source_target_pairs={{0,2},{1,3},{2,0},{3,1},{4,6},{5,7},{6,4},{7,5},{8,10},{9,11},{10,... | collective-permute-start | bytes 3145736 | tf_op jit(solution)/shard_map/ppermute | solution.py:20
  28.3 8.2 %collective-permute-start.3 = (bf16[8,64,128]{2,1,0:T(8,128)(2,1)S(1)}, bf16[8,64,128]{2,1,0:T(8,128)(2,1)S(1)}, u32[]{:S(2)}, u32[]{:S(2)}) collective-permute-start(bf16[8,64,128]{2,1,0:T(8,128)(2,1)S(1)} %shard_map.59.own_ref.partner_ref.refs_1_), channel_id=1, source_target_pairs={{0,8},{8,0},{16,24},{24,16},{32,40},{40,32},{48,56},{56,48},{64,72... | collective-permute-start | bytes 393224 | tf_op jit(solution)/shard_map/ppermute | solution.py:20
  34.0 6.6 %collective-permute-start.13 = (bf16[8,64,128]{2,1,0:T(8,128)(2,1)S(1)}, bf16[8,64,128]{2,1,0:T(8,128)(2,1)S(1)}, u32[]{:S(2)}, u32[]{:S(2)}) collective-permute-start(bf16[8,64,128]{2,1,0:T(8,128)(2,1)S(1)} %shard_map.71), channel_id=1, source_target_pairs={{0,24},{8,16},{16,8},{24,0},{32,56},{40,48},{48,40},{56,32},{64,88... | collective-permute-start | bytes 393224 | tf_op jit(solution)/shard_map/ppermute | solution.py:20
  36.8 8.3 %collective-permute-start.5 = (bf16[8,64,128]{2,1,0:T(8,128)(2,1)S(1)}, bf16[8,64,128]{2,1,0:T(8,128)(2,1)S(1)}, u32[]{:S(2)}, u32[]{:S(2)}) collective-permute-start(bf16[8,64,128]{2,1,0:T(8,128)(2,1)S(1)} %shard_map.61), channel_id=1, source_target_pairs={{0,24},{8,16},{16,8},{24,0},{32,56},{40,48},{48,40},{56,32},{64,88... | collective-permute-start | bytes 393224 | tf_op jit(solution)/shard_map/ppermute | solution.py:20
  40.8 15.1 %collective-permute-start.14 = (bf16[16,64,128]{2,1,0:T(8,128)(2,1)S(1)}, bf16[16,64,128]{2,1,0:T(8,128)(2,1)S(1)}, u32[]{:S(2)}, u32[]{:S(2)}) collective-permute-start(bf16[16,64,128]{2,1,0:T(8,128)(2,1)S(1)} %shard_map.73.refs_1_), channel_id=1, source_target_pairs={{0,8},{8,0},{16,24},{24,16},{32,40},{40,32},{48,56},{56,48},{64,72... | collective-permute-start | bytes 786440 | tf_op jit(solution)/shard_map/ppermute | solution.py:20
  40.9 15.0 %collective-permute-start.15 = (bf16[16,64,128]{2,1,0:T(8,128)(2,1)S(1)}, bf16[16,64,128]{2,1,0:T(8,128)(2,1)S(1)}, u32[]{:S(2)}, u32[]{:S(2)}) collective-permute-start(bf16[16,64,128]{2,1,0:T(8,128)(2,1)S(1)} %shard_map.73.refs_1_), channel_id=1, source_target_pairs={{8,16},{16,8},{24,32},{32,24},{40,48},{48,40},{56,64},{64,56},{72,... | collective-permute-start | bytes 786440 | tf_op jit(solution)/shard_map/ppermute | solution.py:28
  45.1 6.4 %collective-permute-start.24 = (bf16[8,64,128]{2,1,0:T(8,128)(2,1)S(1)}, bf16[8,64,128]{2,1,0:T(8,128)(2,1)S(1)}, u32[]{:S(2)}, u32[]{:S(2)}) collective-permute-start(bf16[8,64,128]{2,1,0:T(8,128)(2,1)S(1)} %shard_map.72.refs_2_.own_ref.partner_ref), channel_id=1, source_target_pairs={{0,32},{8,40},{16,48},{24,56},{32,0},{40,8},{48,16},{56,24},{64,96... | collective-permute-start | bytes 393224 | tf_op jit(solution)/shard_map/ppermute | solution.py:20
  46.8 6.5 %collective-permute-start.6 = (bf16[8,64,128]{2,1,0:T(8,128)(2,1)S(1)}, bf16[8,64,128]{2,1,0:T(8,128)(2,1)S(1)}, u32[]{:S(2)}, u32[]{:S(2)}) collective-permute-start(bf16[8,64,128]{2,1,0:T(8,128)(2,1)S(1)} %shard_map.62.own_ref.partner_ref), channel_id=1, source_target_pairs={{0,32},{8,40},{16,48},{24,56},{32,0},{40,8},{48,16},{56,24},{64,96... | collective-permute-start | bytes 393224 | tf_op jit(solution)/shard_map/ppermute | solution.py:20
  51.8 6.3 %collective-permute-start.25 = (bf16[8,64,128]{2,1,0:T(8,128)(2,1)S(1)}, bf16[8,64,128]{2,1,0:T(8,128)(2,1)S(1)}, u32[]{:S(2)}, u32[]{:S(2)}) collective-permute-start(bf16[8,64,128]{2,1,0:T(8,128)(2,1)S(1)} %shard_map.88), channel_id=1, source_target_pairs={{0,96},{8,104},{16,112},{24,120},{32,64},{40,72},{48,80},{56,88},{... | collective-permute-start | bytes 393224 | tf_op jit(solution)/shard_map/ppermute | solution.py:20
  53.6 6.5 %collective-permute-start.8 = (bf16[8,64,128]{2,1,0:T(8,128)(2,1)S(1)}, bf16[8,64,128]{2,1,0:T(8,128)(2,1)S(1)}, u32[]{:S(2)}, u32[]{:S(2)}) collective-permute-start(bf16[8,64,128]{2,1,0:T(8,128)(2,1)S(1)} %shard_map.64), channel_id=1, source_target_pairs={{0,96},{8,104},{16,112},{24,120},{32,64},{40,72},{48,80},{56,88},{... | collective-permute-start | bytes 393224 | tf_op jit(solution)/shard_map/ppermute | solution.py:20
  61.9 6.4 %collective-permute-start.36 = (bf16[8,64,128]{2,1,0:T(8,128)(2,1)S(1)}, bf16[8,64,128]{2,1,0:T(8,128)(2,1)S(1)}, u32[]{:S(2)}, u32[]{:S(2)}) collective-permute-start(bf16[8,64,128]{2,1,0:T(8,128)(2,1)S(1)} %shard_map.105.own_ref.partner_ref), channel_id=1, source_target_pairs={{0,2},{1,3},{2,0},{3,1},{4,6},{5,7},{6,4},{7,5},{8,10},{9,11},{10,... | collective-permute-start | bytes 393224 | tf_op jit(solution)/shard_map/ppermute | solution.py:20
  62.1 10.6 %collective-permute-start.26 = (bf16[16,64,128]{2,1,0:T(8,128)(2,1)S(1)}, bf16[16,64,128]{2,1,0:T(8,128)(2,1)S(1)}, u32[]{:S(2)}, u32[]{:S(2)}) collective-permute-start(bf16[16,64,128]{2,1,0:T(8,128)(2,1)S(1)} %shard_map.91.refs_1_), channel_id=1, source_target_pairs={{0,8},{8,0},{16,24},{24,16},{32,40},{40,32},{48,56},{56,48},{64,72... | collective-permute-start | bytes 786440 | tf_op jit(solution)/shard_map/ppermute | solution.py:20
  62.9 7.6 %collective-permute-start.17 = (bf16[8,64,128]{2,1,0:T(8,128)(2,1)S(1)}, bf16[8,64,128]{2,1,0:T(8,128)(2,1)S(1)}, u32[]{:S(2)}, u32[]{:S(2)}) collective-permute-start(bf16[8,64,128]{2,1,0:T(8,128)(2,1)S(1)} %shard_map.77.own_ref.partner_ref), channel_id=1, source_target_pairs={{0,2},{1,3},{2,0},{3,1},{4,6},{5,7},{6,4},{7,5},{8,10},{9,11},{10,... | collective-permute-start | bytes 393224 | tf_op jit(solution)/shard_map/ppermute | solution.py:20
  64.4 14.6 %collective-permute-start.27 = (bf16[16,64,128]{2,1,0:T(8,128)(2,1)S(1)}, bf16[16,64,128]{2,1,0:T(8,128)(2,1)S(1)}, u32[]{:S(2)}, u32[]{:S(2)}) collective-permute-start(bf16[16,64,128]{2,1,0:T(8,128)(2,1)S(1)} %shard_map.91.refs_1_), channel_id=1, source_target_pairs={{8,16},{16,8},{24,32},{32,24},{40,48},{48,40},{56,64},{64,56},{72,... | collective-permute-start | bytes 786440 | tf_op jit(solution)/shard_map/ppermute | solution.py:28
  68.5 7.6 %collective-permute-start.37 = (bf16[8,64,128]{2,1,0:T(8,128)(2,1)S(1)}, bf16[8,64,128]{2,1,0:T(8,128)(2,1)S(1)}, u32[]{:S(2)}, u32[]{:S(2)}) collective-permute-start(bf16[8,64,128]{2,1,0:T(8,128)(2,1)S(1)} %shard_map.107), channel_id=1, source_target_pairs={{0,6},{1,7},{2,4},{3,5},{4,2},{5,3},{6,0},{7,1},{8,14},{9,15},{10,... | collective-permute-start | bytes 393224 | tf_op jit(solution)/shard_map/ppermute | solution.py:20
  70.6 7.0 %collective-permute-start.19 = (bf16[8,64,128]{2,1,0:T(8,128)(2,1)S(1)}, bf16[8,64,128]{2,1,0:T(8,128)(2,1)S(1)}, u32[]{:S(2)}, u32[]{:S(2)}) collective-permute-start(bf16[8,64,128]{2,1,0:T(8,128)(2,1)S(1)} %shard_map.80), channel_id=1, source_target_pairs={{0,6},{1,7},{2,4},{3,5},{4,2},{5,3},{6,0},{7,1},{8,14},{9,15},{10,... | collective-permute-start | bytes 393224 | tf_op jit(solution)/shard_map/ppermute | solution.py:20
  82.3 6.3 %collective-permute-start.39 = (bf16[8,64,128]{2,1,0:T(8,128)(2,1)S(1)}, bf16[8,64,128]{2,1,0:T(8,128)(2,1)S(1)}, u32[]{:S(2)}, u32[]{:S(2)}) collective-permute-start(bf16[8,64,128]{2,1,0:T(8,128)(2,1)S(1)} %shard_map.111), channel_id=1, source_target_pairs={{0,24},{8,16},{16,8},{24,0},{32,56},{40,48},{48,40},{56,32},{64,88... | collective-permute-start | bytes 393224 | tf_op jit(solution)/shard_map/ppermute | solution.py:20
  83.8 6.3 %collective-permute-start.21 = (bf16[8,64,128]{2,1,0:T(8,128)(2,1)S(1)}, bf16[8,64,128]{2,1,0:T(8,128)(2,1)S(1)}, u32[]{:S(2)}, u32[]{:S(2)}) collective-permute-start(bf16[8,64,128]{2,1,0:T(8,128)(2,1)S(1)} %shard_map.83), channel_id=1, source_target_pairs={{0,24},{8,16},{16,8},{24,0},{32,56},{40,48},{48,40},{56,32},{64,88... | collective-permute-start | bytes 393224 | tf_op jit(solution)/shard_map/ppermute | solution.py:20
  94.1 6.3 %collective-permute-start.41 = (bf16[8,64,128]{2,1,0:T(8,128)(2,1)S(1)}, bf16[8,64,128]{2,1,0:T(8,128)(2,1)S(1)}, u32[]{:S(2)}, u32[]{:S(2)}) collective-permute-start(bf16[8,64,128]{2,1,0:T(8,128)(2,1)S(1)} %shard_map.114), channel_id=1, source_target_pairs={{0,96},{8,104},{16,112},{24,120},{32,64},{40,72},{48,80},{56,88},{... | collective-permute-start | bytes 393224 | tf_op jit(solution)/shard_map/ppermute | solution.py:20
  103.3 6.4 %collective-permute-start.45 = (bf16[8,64,128]{2,1,0:T(8,128)(2,1)S(1)}, bf16[8,64,128]{2,1,0:T(8,128)(2,1)S(1)}, u32[]{:S(2)}, u32[]{:S(2)}) collective-permute-start(bf16[8,64,128]{2,1,0:T(8,128)(2,1)S(1)} %shard_map.119.own_ref.partner_ref), channel_id=1, source_target_pairs={{0,2},{1,3},{2,0},{3,1},{4,6},{5,7},{6,4},{7,5},{8,10},{9,11},{10,... | collective-permute-start | bytes 393224 | tf_op jit(solution)/shard_map/ppermute | solution.py:20
  103.4 11.8 %collective-permute-start.42 = (bf16[16,64,128]{2,1,0:T(8,128)(2,1)S(1)}, bf16[16,64,128]{2,1,0:T(8,128)(2,1)S(1)}, u32[]{:S(2)}, u32[]{:S(2)}) collective-permute-start(bf16[16,64,128]{2,1,0:T(8,128)(2,1)S(1)} %shard_map.116.refs_1_), channel_id=1, source_target_pairs={{0,8},{8,0},{16,24},{24,16},{32,40},{40,32},{48,56},{56,48},{64,72... | collective-permute-start | bytes 786440 | tf_op jit(solution)/shard_map/ppermute | solution.py:20
  104.6 7.5 %collective-permute-start.29 = (bf16[8,64,128]{2,1,0:T(8,128)(2,1)S(1)}, bf16[8,64,128]{2,1,0:T(8,128)(2,1)S(1)}, u32[]{:S(2)}, u32[]{:S(2)}) collective-permute-start(bf16[8,64,128]{2,1,0:T(8,128)(2,1)S(1)} %shard_map.95.own_ref.partner_ref), channel_id=1, source_target_pairs={{0,2},{1,3},{2,0},{3,1},{4,6},{5,7},{6,4},{7,5},{8,10},{9,11},{10,... | collective-permute-start | bytes 393224 | tf_op jit(solution)/shard_map/ppermute | solution.py:20
  105.8 13.6 %collective-permute-start.43 = (bf16[16,64,128]{2,1,0:T(8,128)(2,1)S(1)}, bf16[16,64,128]{2,1,0:T(8,128)(2,1)S(1)}, u32[]{:S(2)}, u32[]{:S(2)}) collective-permute-start(bf16[16,64,128]{2,1,0:T(8,128)(2,1)S(1)} %shard_map.116.refs_1_), channel_id=1, source_target_pairs={{8,16},{16,8},{24,32},{32,24},{40,48},{48,40},{56,64},{64,56},{72,... | collective-permute-start | bytes 786440 | tf_op jit(solution)/shard_map/ppermute | solution.py:28
  112.4 6.6 %collective-permute-start.30 = (bf16[8,64,128]{2,1,0:T(8,128)(2,1)S(1)}, bf16[8,64,128]{2,1,0:T(8,128)(2,1)S(1)}, u32[]{:S(2)}, u32[]{:S(2)}) collective-permute-start(bf16[8,64,128]{2,1,0:T(8,128)(2,1)S(1)} %shard_map.97), channel_id=1, source_target_pairs={{0,6},{1,7},{2,4},{3,5},{4,2},{5,3},{6,0},{7,1},{8,14},{9,15},{10,... | collective-permute-start | bytes 393224 | tf_op jit(solution)/shard_map/ppermute | solution.py:20
  122.5 7.1 %collective-permute-start.48 = (bf16[8,64,128]{2,1,0:T(8,128)(2,1)S(1)}, bf16[8,64,128]{2,1,0:T(8,128)(2,1)S(1)}, u32[]{:S(2)}, u32[]{:S(2)}) collective-permute-start(bf16[8,64,128]{2,1,0:T(8,128)(2,1)S(1)} %shard_map.125), channel_id=1, source_target_pairs={{0,24},{8,16},{16,8},{24,0},{32,56},{40,48},{48,40},{56,32},{64,88... | collective-permute-start | bytes 393224 | tf_op jit(solution)/shard_map/ppermute | solution.py:20
  124.5 6.5 %collective-permute-start.32 = (bf16[8,64,128]{2,1,0:T(8,128)(2,1)S(1)}, bf16[8,64,128]{2,1,0:T(8,128)(2,1)S(1)}, u32[]{:S(2)}, u32[]{:S(2)}) collective-permute-start(bf16[8,64,128]{2,1,0:T(8,128)(2,1)S(1)} %shard_map.100), channel_id=1, source_target_pairs={{0,24},{8,16},{16,8},{24,0},{32,56},{40,48},{48,40},{56,32},{64,88... | collective-permute-start | bytes 393224 | tf_op jit(solution)/shard_map/ppermute | solution.py:20
  (26 other events, 137.1 us)

commit v5 on v4

--- a/solution.py
+++ b/solution.py
@@ -212,7 +212,7 @@
             ties = {}
             window = window_of()
             near = [near_of(c) for c in chains]
-            ties[0, 1, 0] = window[0]
+            ties[0, 1, 0] = window[2]
             for c in chains:
                 ties[NEAR_TIES[c]] = near[c]
         for c in chains:

time: 145 us -> 144 us (level)
  waiting for transfers between devices: 52.5 us -> 44.4 us
  starting transfers between devices: 62.4 us -> 69.9 us
    ppermute x48, waiting for transfers between devices: 52.5 us -> 43.5 us  [exchange(): return lax.ppermute(block, axis, route)]
    ppermute x48, starting transfers between devices: 53 us -> 60 us  [exchange(): return lax.ppermute(block, axis, route)]
  transfers between devices with their start and end apart: 51 -> 51, of which waited for: 29 -> 31; matrix products, arithmetic and copies ran while one was open for 2% -> 2% of each run, Pallas kernels for 16% -> 16%
where the time goes in v5:
time: 144 us
  starting transfers between devices  69.9 us (49%)
  waiting for transfers between devices  44.4 us (31%)
  Pallas kernels  24.2 us (17%)
  local copies, waits for them, and re-layouts  4.41 us (3%)
    ppermute x48, starting transfers between devices, exchange(): return lax.ppermute(block, axis, route)  60 us
    ppermute x48, waiting for transfers between devices, exchange(): return lax.ppermute(block, axis, route)  43.5 us
    pallas_call x76, Pallas kernels, call(): pl.pallas_call(kernel, out_shape=out_shape, in_specs=[place(op) for op in...  24.2 us
    ppermute x3, starting transfers between devices, exchange_next(): return lax.ppermute(block, axis, route)  9.86 us
  transfers between devices with their start and end apart: 51, of which 31 were waited for; matrix products, arithmetic and copies ran while one was open for 2% of the time, Pallas kernels for 16%

profile of v5, /device:TPU:0, one launch (start us, length us, event | category | flops | bytes accessed | tf_op | source)
XLA Modules:
  0.0 143.7 jit_solution(2248976176466674732)
XLA Ops:
  0.0 1.7 %fusion = (bf16[1,16,2,128,128]{4,3,2,1,0:T(8,128)(2,1)S(1)}, bf16[1,16,2,128,128]{4,3,2,1,0:T(8,128)(2,1)S(1)}) fusion(bf16[10,16,2,128,128]{4,3,2,1,0:T(8,128)(2,1)} %factor_ref.71), kind=kLoop, calls=%fused_computation | loop fusion | bytes 4194304 | tf_op jit(solution)/shard_map/slice | solution.py:171
  1.7 2.1 %collective-permute-start.4 = (bf16[1,16,2,128,128]{4,3,2,1,0:T(8,128)(2,1)S(1)}, bf16[1,16,2,128,128]{4,3,2,1,0:T(8,128)(2,1)S(1)}, u32[]{:S(2)}, u32[]{:S(2)}) collective-permute-start(bf16[1,16,2,128,128]{4,3,2,1,0:T(8,128)(2,1)S(1)} %get-tuple-element.6), channel_id=1, source_target_pairs={{0,8},{8,0},{16,24},{24,16},{32,40},{40,32},{48,56},{56,48},{64,72... | collective-permute-start | bytes 3145736 | tf_op jit(solution)/shard_map/ppermute | solution.py:20
  5.4 2.6 %slice.9.factor_ref = bf16[4,16,2,128,128]{4,3,2,1,0:T(8,128)(2,1)S(1)} slice(bf16[10,16,2,128,128]{4,3,2,1,0:T(8,128)(2,1)} %factor_ref.71), slice={[0:4], [0:16], [0:2], [0:128], [0:128]} | slice | bytes 8388608 | tf_op jit(solution)/shard_map/slice | solution.py:162
  12.7 4.0 %collective-permute-done.10.partner_ref = bf16[8,64,128]{2,1,0:T(8,128)(2,1)S(1)} collective-permute-done((bf16[8,64,128]{2,1,0:T(8,128)(2,1)S(1)}, bf16[8,64,128]{2,1,0:T(8,128)(2,1)S(1)}, u32[]{:S(2)}, u32[]{:S(2)}) %collective-permute-start.10) | collective-permute-done | bytes 131104 | tf_op jit(solution)/shard_map/ppermute | solution.py:20
  17.0 3.1 %collective-permute-start.11 = (bf16[8,64,128]{2,1,0:T(8,128)(2,1)S(1)}, bf16[8,64,128]{2,1,0:T(8,128)(2,1)S(1)}, u32[]{:S(2)}, u32[]{:S(2)}) collective-permute-start(bf16[8,64,128]{2,1,0:T(8,128)(2,1)S(1)} %shard_map.68.own_ref), channel_id=1, source_target_pairs={{0,4},{1,5},{2,6},{3,7},{4,0},{5,1},{6,2},{7,3},{8,12},{9,13},{10,... | collective-permute-start | bytes 393224 | tf_op jit(solution)/shard_map/ppermute | solution.py:20
  20.3 1.8 %collective-permute-start.2 = (bf16[8,64,128]{2,1,0:T(8,128)(2,1)S(1)}, bf16[8,64,128]{2,1,0:T(8,128)(2,1)S(1)}, u32[]{:S(2)}, u32[]{:S(2)}) collective-permute-start(bf16[8,64,128]{2,1,0:T(8,128)(2,1)S(1)} %shard_map.58.own_ref), channel_id=1, source_target_pairs={{0,4},{1,5},{2,6},{3,7},{4,0},{5,1},{6,2},{7,3},{8,12},{9,13},{10,... | collective-permute-start | bytes 393224 | tf_op jit(solution)/shard_map/ppermute | solution.py:20
  22.1 2.7 %collective-permute-done.11.partner_ref = bf16[8,64,128]{2,1,0:T(8,128)(2,1)S(1)} collective-permute-done((bf16[8,64,128]{2,1,0:T(8,128)(2,1)S(1)}, bf16[8,64,128]{2,1,0:T(8,128)(2,1)S(1)}, u32[]{:S(2)}, u32[]{:S(2)}) %collective-permute-start.11) | collective-permute-done | bytes 131104 | tf_op jit(solution)/shard_map/ppermute | solution.py:20
  25.0 1.8 %collective-permute-done.2.partner_ref = bf16[8,64,128]{2,1,0:T(8,128)(2,1)S(1)} collective-permute-done((bf16[8,64,128]{2,1,0:T(8,128)(2,1)S(1)}, bf16[8,64,128]{2,1,0:T(8,128)(2,1)S(1)}, u32[]{:S(2)}, u32[]{:S(2)}) %collective-permute-start.2) | collective-permute-done | bytes 131104 | tf_op jit(solution)/shard_map/ppermute | solution.py:20
  28.3 1.9 %collective-permute-start.3 = (bf16[8,64,128]{2,1,0:T(8,128)(2,1)S(1)}, bf16[8,64,128]{2,1,0:T(8,128)(2,1)S(1)}, u32[]{:S(2)}, u32[]{:S(2)}) collective-permute-start(bf16[8,64,128]{2,1,0:T(8,128)(2,1)S(1)} %shard_map.59.own_ref.partner_ref.refs_1_), channel_id=1, source_target_pairs={{0,8},{8,0},{16,24},{24,16},{32,40},{40,32},{48,56},{56,48},{64,72... | collective-permute-start | bytes 393224 | tf_op jit(solution)/shard_map/ppermute | solution.py:20
  30.2 3.5 %collective-permute-done.12.partner_ref.own_ref = bf16[8,64,128]{2,1,0:T(8,128)(2,1)S(1)} collective-permute-done((bf16[8,64,128]{2,1,0:T(8,128)(2,1)S(1)}, bf16[8,64,128]{2,1,0:T(8,128)(2,1)S(1)}, u32[]{:S(2)}, u32[]{:S(2)}) %collective-permute-start.12) | collective-permute-done | bytes 131104 | tf_op jit(solution)/shard_map/ppermute | solution.py:20
  34.0 2.6 %collective-permute-start.13 = (bf16[8,64,128]{2,1,0:T(8,128)(2,1)S(1)}, bf16[8,64,128]{2,1,0:T(8,128)(2,1)S(1)}, u32[]{:S(2)}, u32[]{:S(2)}) collective-permute-start(bf16[8,64,128]{2,1,0:T(8,128)(2,1)S(1)} %shard_map.71), channel_id=1, source_target_pairs={{0,24},{8,16},{16,8},{24,0},{32,56},{40,48},{48,40},{56,32},{64,88... | collective-permute-start | bytes 393224 | tf_op jit(solution)/shard_map/ppermute | solution.py:20
  38.2 2.3 %collective-permute-done.13.partner_ref = bf16[8,64,128]{2,1,0:T(8,128)(2,1)S(1)} collective-permute-done((bf16[8,64,128]{2,1,0:T(8,128)(2,1)S(1)}, bf16[8,64,128]{2,1,0:T(8,128)(2,1)S(1)}, u32[]{:S(2)}, u32[]{:S(2)}) %collective-permute-start.13) | collective-permute-done | bytes 131104 | tf_op jit(solution)/shard_map/ppermute | solution.py:20
  40.9 4.2 %collective-permute-start.15 = (bf16[16,64,128]{2,1,0:T(8,128)(2,1)S(1)}, bf16[16,64,128]{2,1,0:T(8,128)(2,1)S(1)}, u32[]{:S(2)}, u32[]{:S(2)}) collective-permute-start(bf16[16,64,128]{2,1,0:T(8,128)(2,1)S(1)} %shard_map.73.refs_1_), channel_id=1, source_target_pairs={{8,16},{16,8},{24,32},{32,24},{40,48},{48,40},{56,64},{64,56},{72,... | collective-permute-start | bytes 786440 | tf_op jit(solution)/shard_map/ppermute | solution.py:28
  47.7 3.8 %collective-permute-done.24.partner_ref.own_ref = bf16[8,64,128]{2,1,0:T(8,128)(2,1)S(1)} collective-permute-done((bf16[8,64,128]{2,1,0:T(8,128)(2,1)S(1)}, bf16[8,64,128]{2,1,0:T(8,128)(2,1)S(1)}, u32[]{:S(2)}, u32[]{:S(2)}) %collective-permute-start.24) | collective-permute-done | bytes 131104 | tf_op jit(solution)/shard_map/ppermute | solution.py:20
  53.6 1.8 %collective-permute-start.8 = (bf16[8,64,128]{2,1,0:T(8,128)(2,1)S(1)}, bf16[8,64,128]{2,1,0:T(8,128)(2,1)S(1)}, u32[]{:S(2)}, u32[]{:S(2)}) collective-permute-start(bf16[8,64,128]{2,1,0:T(8,128)(2,1)S(1)} %shard_map.64), channel_id=1, source_target_pairs={{0,96},{8,104},{16,112},{24,120},{32,64},{40,72},{48,80},{56,88},{... | collective-permute-start | bytes 393224 | tf_op jit(solution)/shard_map/ppermute | solution.py:20
  62.1 2.7 %collective-permute-start.27 = (bf16[16,64,128]{2,1,0:T(8,128)(2,1)S(1)}, bf16[16,64,128]{2,1,0:T(8,128)(2,1)S(1)}, u32[]{:S(2)}, u32[]{:S(2)}) collective-permute-start(bf16[16,64,128]{2,1,0:T(8,128)(2,1)S(1)} %shard_map.91.refs_1_), channel_id=1, source_target_pairs={{8,16},{16,8},{24,32},{32,24},{40,48},{48,40},{56,64},{64,56},{72,... | collective-permute-start | bytes 786440 | tf_op jit(solution)/shard_map/ppermute | solution.py:28
  65.0 1.9 %collective-permute-start.17 = (bf16[8,64,128]{2,1,0:T(8,128)(2,1)S(1)}, bf16[8,64,128]{2,1,0:T(8,128)(2,1)S(1)}, u32[]{:S(2)}, u32[]{:S(2)}) collective-permute-start(bf16[8,64,128]{2,1,0:T(8,128)(2,1)S(1)} %shard_map.77.own_ref.partner_ref), channel_id=1, source_target_pairs={{0,2},{1,3},{2,0},{3,1},{4,6},{5,7},{6,4},{7,5},{8,10},{9,11},{10,... | collective-permute-start | bytes 393224 | tf_op jit(solution)/shard_map/ppermute | solution.py:20
  67.7 2.0 %collective-permute-start.37 = (bf16[8,64,128]{2,1,0:T(8,128)(2,1)S(1)}, bf16[8,64,128]{2,1,0:T(8,128)(2,1)S(1)}, u32[]{:S(2)}, u32[]{:S(2)}) collective-permute-start(bf16[8,64,128]{2,1,0:T(8,128)(2,1)S(1)} %shard_map.107), channel_id=1, source_target_pairs={{0,6},{1,7},{2,4},{3,5},{4,2},{5,3},{6,0},{7,1},{8,14},{9,15},{10,... | collective-permute-start | bytes 393224 | tf_op jit(solution)/shard_map/ppermute | solution.py:20
  70.4 2.3 %collective-permute-start.19 = (bf16[8,64,128]{2,1,0:T(8,128)(2,1)S(1)}, bf16[8,64,128]{2,1,0:T(8,128)(2,1)S(1)}, u32[]{:S(2)}, u32[]{:S(2)}) collective-permute-start(bf16[8,64,128]{2,1,0:T(8,128)(2,1)S(1)} %shard_map.80), channel_id=1, source_target_pairs={{0,6},{1,7},{2,4},{3,5},{4,2},{5,3},{6,0},{7,1},{8,14},{9,15},{10,... | collective-permute-start | bytes 393224 | tf_op jit(solution)/shard_map/ppermute | solution.py:20
  75.0 1.9 %collective-permute-start.38 = (bf16[8,64,128]{2,1,0:T(8,128)(2,1)S(1)}, bf16[8,64,128]{2,1,0:T(8,128)(2,1)S(1)}, u32[]{:S(2)}, u32[]{:S(2)}) collective-permute-start(bf16[8,64,128]{2,1,0:T(8,128)(2,1)S(1)} %shard_map.108.own_ref.partner_ref), channel_id=1, source_target_pairs={{0,8},{8,0},{16,24},{24,16},{32,40},{40,32},{48,56},{56,48},{64,72... | collective-permute-start | bytes 393224 | tf_op jit(solution)/shard_map/ppermute | solution.py:20
  82.7 2.0 %collective-permute-start.21 = (bf16[8,64,128]{2,1,0:T(8,128)(2,1)S(1)}, bf16[8,64,128]{2,1,0:T(8,128)(2,1)S(1)}, u32[]{:S(2)}, u32[]{:S(2)}) collective-permute-start(bf16[8,64,128]{2,1,0:T(8,128)(2,1)S(1)} %shard_map.83), channel_id=1, source_target_pairs={{0,24},{8,16},{16,8},{24,0},{32,56},{40,48},{48,40},{56,32},{64,88... | collective-permute-start | bytes 393224 | tf_op jit(solution)/shard_map/ppermute | solution.py:20
  84.9 2.4 %collective-permute-done.39.partner_ref = bf16[8,64,128]{2,1,0:T(8,128)(2,1)S(1)} collective-permute-done((bf16[8,64,128]{2,1,0:T(8,128)(2,1)S(1)}, bf16[8,64,128]{2,1,0:T(8,128)(2,1)S(1)}, u32[]{:S(2)}, u32[]{:S(2)}) %collective-permute-start.39) | collective-permute-done | bytes 131104 | tf_op jit(solution)/shard_map/ppermute | solution.py:20
  92.8 2.8 %collective-permute-start.41 = (bf16[8,64,128]{2,1,0:T(8,128)(2,1)S(1)}, bf16[8,64,128]{2,1,0:T(8,128)(2,1)S(1)}, u32[]{:S(2)}, u32[]{:S(2)}) collective-permute-start(bf16[8,64,128]{2,1,0:T(8,128)(2,1)S(1)} %shard_map.114), channel_id=1, source_target_pairs={{0,96},{8,104},{16,112},{24,120},{32,64},{40,72},{48,80},{56,88},{... | collective-permute-start | bytes 393224 | tf_op jit(solution)/shard_map/ppermute | solution.py:20
  100.0 2.2 %collective-permute-done.23.partner_ref = bf16[8,64,128]{2,1,0:T(8,128)(2,1)S(1)} collective-permute-done((bf16[8,64,128]{2,1,0:T(8,128)(2,1)S(1)}, bf16[8,64,128]{2,1,0:T(8,128)(2,1)S(1)}, u32[]{:S(2)}, u32[]{:S(2)}) %collective-permute-start.23) | collective-permute-done | bytes 131104 | tf_op jit(solution)/shard_map/ppermute | solution.py:20
  103.4 2.9 %collective-permute-start.43 = (bf16[16,64,128]{2,1,0:T(8,128)(2,1)S(1)}, bf16[16,64,128]{2,1,0:T(8,128)(2,1)S(1)}, u32[]{:S(2)}, u32[]{:S(2)}) collective-permute-start(bf16[16,64,128]{2,1,0:T(8,128)(2,1)S(1)} %shard_map.116.refs_1_), channel_id=1, source_target_pairs={{8,16},{16,8},{24,32},{32,24},{40,48},{48,40},{56,64},{64,56},{72,... | collective-permute-start | bytes 786440 | tf_op jit(solution)/shard_map/ppermute | solution.py:28
  106.6 2.0 %collective-permute-start.29 = (bf16[8,64,128]{2,1,0:T(8,128)(2,1)S(1)}, bf16[8,64,128]{2,1,0:T(8,128)(2,1)S(1)}, u32[]{:S(2)}, u32[]{:S(2)}) collective-permute-start(bf16[8,64,128]{2,1,0:T(8,128)(2,1)S(1)} %shard_map.95.own_ref.partner_ref), channel_id=1, source_target_pairs={{0,2},{1,3},{2,0},{3,1},{4,6},{5,7},{6,4},{7,5},{8,10},{9,11},{10,... | collective-permute-start | bytes 393224 | tf_op jit(solution)/shard_map/ppermute | solution.py:20
  109.5 2.2 %collective-permute-start.46 = (bf16[8,64,128]{2,1,0:T(8,128)(2,1)S(1)}, bf16[8,64,128]{2,1,0:T(8,128)(2,1)S(1)}, u32[]{:S(2)}, u32[]{:S(2)}) collective-permute-start(bf16[8,64,128]{2,1,0:T(8,128)(2,1)S(1)} %shard_map.121), channel_id=1, source_target_pairs={{0,6},{1,7},{2,4},{3,5},{4,2},{5,3},{6,0},{7,1},{8,14},{9,15},{10,... | collective-permute-start | bytes 393224 | tf_op jit(solution)/shard_map/ppermute | solution.py:20
  112.5 2.3 %collective-permute-start.30 = (bf16[8,64,128]{2,1,0:T(8,128)(2,1)S(1)}, bf16[8,64,128]{2,1,0:T(8,128)(2,1)S(1)}, u32[]{:S(2)}, u32[]{:S(2)}) collective-permute-start(bf16[8,64,128]{2,1,0:T(8,128)(2,1)S(1)} %shard_map.97), channel_id=1, source_target_pairs={{0,6},{1,7},{2,4},{3,5},{4,2},{5,3},{6,0},{7,1},{8,14},{9,15},{10,... | collective-permute-start | bytes 393224 | tf_op jit(solution)/shard_map/ppermute | solution.py:20
  116.2 2.1 %collective-permute-start.47 = (bf16[8,64,128]{2,1,0:T(8,128)(2,1)S(1)}, bf16[8,64,128]{2,1,0:T(8,128)(2,1)S(1)}, u32[]{:S(2)}, u32[]{:S(2)}) collective-permute-start(bf16[8,64,128]{2,1,0:T(8,128)(2,1)S(1)} %shard_map.122.own_ref.partner_ref), channel_id=1, source_target_pairs={{0,8},{8,0},{16,24},{24,16},{32,40},{40,32},{48,56},{56,48},{64,72... | collective-permute-start | bytes 393224 | tf_op jit(solution)/shard_map/ppermute | solution.py:20
  126.7 2.7 %collective-permute-done.48.partner_ref = bf16[8,64,128]{2,1,0:T(8,128)(2,1)S(1)} collective-permute-done((bf16[8,64,128]{2,1,0:T(8,128)(2,1)S(1)}, bf16[8,64,128]{2,1,0:T(8,128)(2,1)S(1)}, u32[]{:S(2)}, u32[]{:S(2)}) %collective-permute-start.48) | collective-permute-done | bytes 131104 | tf_op jit(solution)/shard_map/ppermute | solution.py:20
  136.5 2.0 %collective-permute-start.34 = (bf16[8,64,128]{2,1,0:T(8,128)(2,1)S(1)}, bf16[8,64,128]{2,1,0:T(8,128)(2,1)S(1)}, u32[]{:S(2)}, u32[]{:S(2)}) collective-permute-start(bf16[8,64,128]{2,1,0:T(8,128)(2,1)S(1)} %shard_map.103), channel_id=1, source_target_pairs={{0,96},{8,104},{16,112},{24,120},{32,64},{40,72},{48,80},{56,88},{... | collective-permute-start | bytes 393224 | tf_op jit(solution)/shard_map/ppermute | solution.py:20
  139.0 2.2 %collective-permute-done.50.partner_ref = bf16[8,64,128]{2,1,0:T(8,128)(2,1)S(1)} collective-permute-done((bf16[8,64,128]{2,1,0:T(8,128)(2,1)S(1)}, bf16[8,64,128]{2,1,0:T(8,128)(2,1)S(1)}, u32[]{:S(2)}, u32[]{:S(2)}) %collective-permute-start.50) | collective-permute-done | bytes 131104 | tf_op jit(solution)/shard_map/ppermute | solution.py:20
  (163 shorter events, 64.3 us)
Async XLA Ops:
  1.7 32.0 %collective-permute-start.4 = (bf16[1,16,2,128,128]{4,3,2,1,0:T(8,128)(2,1)S(1)}, bf16[1,16,2,128,128]{4,3,2,1,0:T(8,128)(2,1)S(1)}, u32[]{:S(2)}, u32[]{:S(2)}) collective-permute-start(bf16[1,16,2,128,128]{4,3,2,1,0:T(8,128)(2,1)S(1)} %get-tuple-element.6), channel_id=1, source_target_pairs={{0,8},{8,0},{16,24},{24,16},{32,40},{40,32},{48,56},{56,48},{64,72... | collective-permute-start | bytes 3145736 | tf_op jit(solution)/shard_map/ppermute | solution.py:20
  3.8 43.0 %collective-permute-start.7 = (bf16[1,16,2,128,128]{4,3,2,1,0:T(8,128)(2,1)S(1)}, bf16[1,16,2,128,128]{4,3,2,1,0:T(8,128)(2,1)S(1)}, u32[]{:S(2)}, u32[]{:S(2)}) collective-permute-start(bf16[1,16,2,128,128]{4,3,2,1,0:T(8,128)(2,1)S(1)} %get-tuple-element.5), channel_id=1, source_target_pairs={{0,32},{8,40},{16,48},{24,56},{32,0},{40,8},{48,16},{56,24},{64,96... | collective-permute-start | bytes 3145736 | tf_op jit(solution)/shard_map/ppermute | solution.py:20
  10.3 6.4 %collective-permute-start.10 = (bf16[8,64,128]{2,1,0:T(8,128)(2,1)S(1)}, bf16[8,64,128]{2,1,0:T(8,128)(2,1)S(1)}, u32[]{:S(2)}, u32[]{:S(2)}) collective-permute-start(bf16[8,64,128]{2,1,0:T(8,128)(2,1)S(1)} %shard_map.67.own_ref), channel_id=1, source_target_pairs={{0,2},{1,3},{2,0},{3,1},{4,6},{5,7},{6,4},{7,5},{8,10},{9,11},{10,... | collective-permute-start | bytes 393224 | tf_op jit(solution)/shard_map/ppermute | solution.py:20
  12.1 8.0 %collective-permute-start.1 = (bf16[8,64,128]{2,1,0:T(8,128)(2,1)S(1)}, bf16[8,64,128]{2,1,0:T(8,128)(2,1)S(1)}, u32[]{:S(2)}, u32[]{:S(2)}) collective-permute-start(bf16[8,64,128]{2,1,0:T(8,128)(2,1)S(1)} %shard_map.57.own_ref), channel_id=1, source_target_pairs={{0,2},{1,3},{2,0},{3,1},{4,6},{5,7},{6,4},{7,5},{8,10},{9,11},{10,... | collective-permute-start | bytes 393224 | tf_op jit(solution)/shard_map/ppermute | solution.py:20
  17.0 7.8 %collective-permute-start.11 = (bf16[8,64,128]{2,1,0:T(8,128)(2,1)S(1)}, bf16[8,64,128]{2,1,0:T(8,128)(2,1)S(1)}, u32[]{:S(2)}, u32[]{:S(2)}) collective-permute-start(bf16[8,64,128]{2,1,0:T(8,128)(2,1)S(1)} %shard_map.68.own_ref), channel_id=1, source_target_pairs={{0,4},{1,5},{2,6},{3,7},{4,0},{5,1},{6,2},{7,3},{8,12},{9,13},{10,... | collective-permute-start | bytes 393224 | tf_op jit(solution)/shard_map/ppermute | solution.py:20
  20.3 6.6 %collective-permute-start.2 = (bf16[8,64,128]{2,1,0:T(8,128)(2,1)S(1)}, bf16[8,64,128]{2,1,0:T(8,128)(2,1)S(1)}, u32[]{:S(2)}, u32[]{:S(2)}) collective-permute-start(bf16[8,64,128]{2,1,0:T(8,128)(2,1)S(1)} %shard_map.58.own_ref), channel_id=1, source_target_pairs={{0,4},{1,5},{2,6},{3,7},{4,0},{5,1},{6,2},{7,3},{8,12},{9,13},{10,... | collective-permute-start | bytes 393224 | tf_op jit(solution)/shard_map/ppermute | solution.py:20
  27.2 39.8 %collective-permute-start.18 = (bf16[1,16,2,128,128]{4,3,2,1,0:T(8,128)(2,1)S(1)}, bf16[1,16,2,128,128]{4,3,2,1,0:T(8,128)(2,1)S(1)}, u32[]{:S(2)}, u32[]{:S(2)}) collective-permute-start(bf16[1,16,2,128,128]{4,3,2,1,0:T(8,128)(2,1)S(1)} %shard_map.79), channel_id=1, source_target_pairs={{0,2},{1,3},{2,0},{3,1},{4,6},{5,7},{6,4},{7,5},{8,10},{9,11},{10,... | collective-permute-start | bytes 3145736 | tf_op jit(solution)/shard_map/ppermute | solution.py:20
  28.3 8.2 %collective-permute-start.3 = (bf16[8,64,128]{2,1,0:T(8,128)(2,1)S(1)}, bf16[8,64,128]{2,1,0:T(8,128)(2,1)S(1)}, u32[]{:S(2)}, u32[]{:S(2)}) collective-permute-start(bf16[8,64,128]{2,1,0:T(8,128)(2,1)S(1)} %shard_map.59.own_ref.partner_ref.refs_1_), channel_id=1, source_target_pairs={{0,8},{8,0},{16,24},{24,16},{32,40},{40,32},{48,56},{56,48},{64,72... | collective-permute-start | bytes 393224 | tf_op jit(solution)/shard_map/ppermute | solution.py:20
  34.0 6.6 %collective-permute-start.13 = (bf16[8,64,128]{2,1,0:T(8,128)(2,1)S(1)}, bf16[8,64,128]{2,1,0:T(8,128)(2,1)S(1)}, u32[]{:S(2)}, u32[]{:S(2)}) collective-permute-start(bf16[8,64,128]{2,1,0:T(8,128)(2,1)S(1)} %shard_map.71), channel_id=1, source_target_pairs={{0,24},{8,16},{16,8},{24,0},{32,56},{40,48},{48,40},{56,32},{64,88... | collective-permute-start | bytes 393224 | tf_op jit(solution)/shard_map/ppermute | solution.py:20
  36.8 8.3 %collective-permute-start.5 = (bf16[8,64,128]{2,1,0:T(8,128)(2,1)S(1)}, bf16[8,64,128]{2,1,0:T(8,128)(2,1)S(1)}, u32[]{:S(2)}, u32[]{:S(2)}) collective-permute-start(bf16[8,64,128]{2,1,0:T(8,128)(2,1)S(1)} %shard_map.61), channel_id=1, source_target_pairs={{0,24},{8,16},{16,8},{24,0},{32,56},{40,48},{48,40},{56,32},{64,88... | collective-permute-start | bytes 393224 | tf_op jit(solution)/shard_map/ppermute | solution.py:20
  40.8 15.1 %collective-permute-start.14 = (bf16[16,64,128]{2,1,0:T(8,128)(2,1)S(1)}, bf16[16,64,128]{2,1,0:T(8,128)(2,1)S(1)}, u32[]{:S(2)}, u32[]{:S(2)}) collective-permute-start(bf16[16,64,128]{2,1,0:T(8,128)(2,1)S(1)} %shard_map.73.refs_1_), channel_id=1, source_target_pairs={{0,8},{8,0},{16,24},{24,16},{32,40},{40,32},{48,56},{56,48},{64,72... | collective-permute-start | bytes 786440 | tf_op jit(solution)/shard_map/ppermute | solution.py:20
  40.9 15.0 %collective-permute-start.15 = (bf16[16,64,128]{2,1,0:T(8,128)(2,1)S(1)}, bf16[16,64,128]{2,1,0:T(8,128)(2,1)S(1)}, u32[]{:S(2)}, u32[]{:S(2)}) collective-permute-start(bf16[16,64,128]{2,1,0:T(8,128)(2,1)S(1)} %shard_map.73.refs_1_), channel_id=1, source_target_pairs={{8,16},{16,8},{24,32},{32,24},{40,48},{48,40},{56,64},{64,56},{72,... | collective-permute-start | bytes 786440 | tf_op jit(solution)/shard_map/ppermute | solution.py:28
  45.1 6.4 %collective-permute-start.24 = (bf16[8,64,128]{2,1,0:T(8,128)(2,1)S(1)}, bf16[8,64,128]{2,1,0:T(8,128)(2,1)S(1)}, u32[]{:S(2)}, u32[]{:S(2)}) collective-permute-start(bf16[8,64,128]{2,1,0:T(8,128)(2,1)S(1)} %shard_map.72.refs_2_.own_ref.partner_ref), channel_id=1, source_target_pairs={{0,32},{8,40},{16,48},{24,56},{32,0},{40,8},{48,16},{56,24},{64,96... | collective-permute-start | bytes 393224 | tf_op jit(solution)/shard_map/ppermute | solution.py:20
  46.8 6.5 %collective-permute-start.6 = (bf16[8,64,128]{2,1,0:T(8,128)(2,1)S(1)}, bf16[8,64,128]{2,1,0:T(8,128)(2,1)S(1)}, u32[]{:S(2)}, u32[]{:S(2)}) collective-permute-start(bf16[8,64,128]{2,1,0:T(8,128)(2,1)S(1)} %shard_map.62.own_ref.partner_ref), channel_id=1, source_target_pairs={{0,32},{8,40},{16,48},{24,56},{32,0},{40,8},{48,16},{56,24},{64,96... | collective-permute-start | bytes 393224 | tf_op jit(solution)/shard_map/ppermute | solution.py:20
  53.6 6.5 %collective-permute-start.8 = (bf16[8,64,128]{2,1,0:T(8,128)(2,1)S(1)}, bf16[8,64,128]{2,1,0:T(8,128)(2,1)S(1)}, u32[]{:S(2)}, u32[]{:S(2)}) collective-permute-start(bf16[8,64,128]{2,1,0:T(8,128)(2,1)S(1)} %shard_map.64), channel_id=1, source_target_pairs={{0,96},{8,104},{16,112},{24,120},{32,64},{40,72},{48,80},{56,88},{... | collective-permute-start | bytes 393224 | tf_op jit(solution)/shard_map/ppermute | solution.py:20
  62.1 11.5 %collective-permute-start.27 = (bf16[16,64,128]{2,1,0:T(8,128)(2,1)S(1)}, bf16[16,64,128]{2,1,0:T(8,128)(2,1)S(1)}, u32[]{:S(2)}, u32[]{:S(2)}) collective-permute-start(bf16[16,64,128]{2,1,0:T(8,128)(2,1)S(1)} %shard_map.91.refs_1_), channel_id=1, source_target_pairs={{8,16},{16,8},{24,32},{32,24},{40,48},{48,40},{56,64},{64,56},{72,... | collective-permute-start | bytes 786440 | tf_op jit(solution)/shard_map/ppermute | solution.py:28
  67.0 11.4 %collective-permute-start.26 = (bf16[16,64,128]{2,1,0:T(8,128)(2,1)S(1)}, bf16[16,64,128]{2,1,0:T(8,128)(2,1)S(1)}, u32[]{:S(2)}, u32[]{:S(2)}) collective-permute-start(bf16[16,64,128]{2,1,0:T(8,128)(2,1)S(1)} %shard_map.91.refs_1_), channel_id=1, source_target_pairs={{0,8},{8,0},{16,24},{24,16},{32,40},{40,32},{48,56},{56,48},{64,72... | collective-permute-start | bytes 786440 | tf_op jit(solution)/shard_map/ppermute | solution.py:20
  67.7 7.2 %collective-permute-start.37 = (bf16[8,64,128]{2,1,0:T(8,128)(2,1)S(1)}, bf16[8,64,128]{2,1,0:T(8,128)(2,1)S(1)}, u32[]{:S(2)}, u32[]{:S(2)}) collective-permute-start(bf16[8,64,128]{2,1,0:T(8,128)(2,1)S(1)} %shard_map.107), channel_id=1, source_target_pairs={{0,6},{1,7},{2,4},{3,5},{4,2},{5,3},{6,0},{7,1},{8,14},{9,15},{10,... | collective-permute-start | bytes 393224 | tf_op jit(solution)/shard_map/ppermute | solution.py:20
  70.4 6.8 %collective-permute-start.19 = (bf16[8,64,128]{2,1,0:T(8,128)(2,1)S(1)}, bf16[8,64,128]{2,1,0:T(8,128)(2,1)S(1)}, u32[]{:S(2)}, u32[]{:S(2)}) collective-permute-start(bf16[8,64,128]{2,1,0:T(8,128)(2,1)S(1)} %shard_map.80), channel_id=1, source_target_pairs={{0,6},{1,7},{2,4},{3,5},{4,2},{5,3},{6,0},{7,1},{8,14},{9,15},{10,... | collective-permute-start | bytes 393224 | tf_op jit(solution)/shard_map/ppermute | solution.py:20
  81.1 6.3 %collective-permute-start.39 = (bf16[8,64,128]{2,1,0:T(8,128)(2,1)S(1)}, bf16[8,64,128]{2,1,0:T(8,128)(2,1)S(1)}, u32[]{:S(2)}, u32[]{:S(2)}) collective-permute-start(bf16[8,64,128]{2,1,0:T(8,128)(2,1)S(1)} %shard_map.111), channel_id=1, source_target_pairs={{0,24},{8,16},{16,8},{24,0},{32,56},{40,48},{48,40},{56,32},{64,88... | collective-permute-start | bytes 393224 | tf_op jit(solution)/shard_map/ppermute | solution.py:20
  82.7 6.3 %collective-permute-start.21 = (bf16[8,64,128]{2,1,0:T(8,128)(2,1)S(1)}, bf16[8,64,128]{2,1,0:T(8,128)(2,1)S(1)}, u32[]{:S(2)}, u32[]{:S(2)}) collective-permute-start(bf16[8,64,128]{2,1,0:T(8,128)(2,1)S(1)} %shard_map.83), channel_id=1, source_target_pairs={{0,24},{8,16},{16,8},{24,0},{32,56},{40,48},{48,40},{56,32},{64,88... | collective-permute-start | bytes 393224 | tf_op jit(solution)/shard_map/ppermute | solution.py:20
  89.2 6.5 %collective-permute-start.22 = (bf16[8,64,128]{2,1,0:T(8,128)(2,1)S(1)}, bf16[8,64,128]{2,1,0:T(8,128)(2,1)S(1)}, u32[]{:S(2)}, u32[]{:S(2)}) collective-permute-start(bf16[8,64,128]{2,1,0:T(8,128)(2,1)S(1)} %shard_map.84.own_ref.partner_ref), channel_id=1, source_target_pairs={{0,32},{8,40},{16,48},{24,56},{32,0},{40,8},{48,16},{56,24},{64,96... | collective-permute-start | bytes 393224 | tf_op jit(solution)/shard_map/ppermute | solution.py:20
  92.8 6.3 %collective-permute-start.41 = (bf16[8,64,128]{2,1,0:T(8,128)(2,1)S(1)}, bf16[8,64,128]{2,1,0:T(8,128)(2,1)S(1)}, u32[]{:S(2)}, u32[]{:S(2)}) collective-permute-start(bf16[8,64,128]{2,1,0:T(8,128)(2,1)S(1)} %shard_map.114), channel_id=1, source_target_pairs={{0,96},{8,104},{16,112},{24,120},{32,64},{40,72},{48,80},{56,88},{... | collective-permute-start | bytes 393224 | tf_op jit(solution)/shard_map/ppermute | solution.py:20
  95.9 6.3 %collective-permute-start.23 = (bf16[8,64,128]{2,1,0:T(8,128)(2,1)S(1)}, bf16[8,64,128]{2,1,0:T(8,128)(2,1)S(1)}, u32[]{:S(2)}, u32[]{:S(2)}) collective-permute-start(bf16[8,64,128]{2,1,0:T(8,128)(2,1)S(1)} %shard_map.86), channel_id=1, source_target_pairs={{0,96},{8,104},{16,112},{24,120},{32,64},{40,72},{48,80},{56,88},{... | collective-permute-start | bytes 393224 | tf_op jit(solution)/shard_map/ppermute | solution.py:20
  103.4 12.1 %collective-permute-start.43 = (bf16[16,64,128]{2,1,0:T(8,128)(2,1)S(1)}, bf16[16,64,128]{2,1,0:T(8,128)(2,1)S(1)}, u32[]{:S(2)}, u32[]{:S(2)}) collective-permute-start(bf16[16,64,128]{2,1,0:T(8,128)(2,1)S(1)} %shard_map.116.refs_1_), channel_id=1, source_target_pairs={{8,16},{16,8},{24,32},{32,24},{40,48},{48,40},{56,64},{64,56},{72,... | collective-permute-start | bytes 786440 | tf_op jit(solution)/shard_map/ppermute | solution.py:28
  108.6 11.6 %collective-permute-start.42 = (bf16[16,64,128]{2,1,0:T(8,128)(2,1)S(1)}, bf16[16,64,128]{2,1,0:T(8,128)(2,1)S(1)}, u32[]{:S(2)}, u32[]{:S(2)}) collective-permute-start(bf16[16,64,128]{2,1,0:T(8,128)(2,1)S(1)} %shard_map.116.refs_1_), channel_id=1, source_target_pairs={{0,8},{8,0},{16,24},{24,16},{32,40},{40,32},{48,56},{56,48},{64,72... | collective-permute-start | bytes 786440 | tf_op jit(solution)/shard_map/ppermute | solution.py:20
  109.5 6.4 %collective-permute-start.46 = (bf16[8,64,128]{2,1,0:T(8,128)(2,1)S(1)}, bf16[8,64,128]{2,1,0:T(8,128)(2,1)S(1)}, u32[]{:S(2)}, u32[]{:S(2)}) collective-permute-start(bf16[8,64,128]{2,1,0:T(8,128)(2,1)S(1)} %shard_map.121), channel_id=1, source_target_pairs={{0,6},{1,7},{2,4},{3,5},{4,2},{5,3},{6,0},{7,1},{8,14},{9,15},{10,... | collective-permute-start | bytes 393224 | tf_op jit(solution)/shard_map/ppermute | solution.py:20
  112.5 6.5 %collective-permute-start.30 = (bf16[8,64,128]{2,1,0:T(8,128)(2,1)S(1)}, bf16[8,64,128]{2,1,0:T(8,128)(2,1)S(1)}, u32[]{:S(2)}, u32[]{:S(2)}) collective-permute-start(bf16[8,64,128]{2,1,0:T(8,128)(2,1)S(1)} %shard_map.97), channel_id=1, source_target_pairs={{0,6},{1,7},{2,4},{3,5},{4,2},{5,3},{6,0},{7,1},{8,14},{9,15},{10,... | collective-permute-start | bytes 393224 | tf_op jit(solution)/shard_map/ppermute | solution.py:20
  122.6 6.8 %collective-permute-start.48 = (bf16[8,64,128]{2,1,0:T(8,128)(2,1)S(1)}, bf16[8,64,128]{2,1,0:T(8,128)(2,1)S(1)}, u32[]{:S(2)}, u32[]{:S(2)}) collective-permute-start(bf16[8,64,128]{2,1,0:T(8,128)(2,1)S(1)} %shard_map.125), channel_id=1, source_target_pairs={{0,24},{8,16},{16,8},{24,0},{32,56},{40,48},{48,40},{56,32},{64,88... | collective-permute-start | bytes 393224 | tf_op jit(solution)/shard_map/ppermute | solution.py:20
  124.5 6.3 %collective-permute-start.32 = (bf16[8,64,128]{2,1,0:T(8,128)(2,1)S(1)}, bf16[8,64,128]{2,1,0:T(8,128)(2,1)S(1)}, u32[]{:S(2)}, u32[]{:S(2)}) collective-permute-start(bf16[8,64,128]{2,1,0:T(8,128)(2,1)S(1)} %shard_map.100), channel_id=1, source_target_pairs={{0,24},{8,16},{16,8},{24,0},{32,56},{40,48},{48,40},{56,32},{64,88... | collective-permute-start | bytes 393224 | tf_op jit(solution)/shard_map/ppermute | solution.py:20
  134.9 6.3 %collective-permute-start.50 = (bf16[8,64,128]{2,1,0:T(8,128)(2,1)S(1)}, bf16[8,64,128]{2,1,0:T(8,128)(2,1)S(1)}, u32[]{:S(2)}, u32[]{:S(2)}) collective-permute-start(bf16[8,64,128]{2,1,0:T(8,128)(2,1)S(1)} %shard_map.128), channel_id=1, source_target_pairs={{0,96},{8,104},{16,112},{24,120},{32,64},{40,72},{48,80},{56,88},{... | collective-permute-start | bytes 393224 | tf_op jit(solution)/shard_map/ppermute | solution.py:20
  136.5 6.3 %collective-permute-start.34 = (bf16[8,64,128]{2,1,0:T(8,128)(2,1)S(1)}, bf16[8,64,128]{2,1,0:T(8,128)(2,1)S(1)}, u32[]{:S(2)}, u32[]{:S(2)}) collective-permute-start(bf16[8,64,128]{2,1,0:T(8,128)(2,1)S(1)} %shard_map.103), channel_id=1, source_target_pairs={{0,96},{8,104},{16,112},{24,120},{32,64},{40,72},{48,80},{56,88},{... | collective-permute-start | bytes 393224 | tf_op jit(solution)/shard_map/ppermute | solution.py:20
  (26 other events, 139.8 us)

commit v6 on v5

--- a/solution.py
+++ b/solution.py
@@ -213,6 +213,7 @@
             window = window_of()
             near = [near_of(c) for c in chains]
             ties[0, 1, 0] = window[2]
+            ties[0, 1, 1] = window[0]
             for c in chains:
                 ties[NEAR_TIES[c]] = near[c]
         for c in chains:

time: 144 us -> 144 us (level)
  no operation moved by 1% of the time
where the time goes in v6:
time: 144 us
  starting transfers between devices  69.7 us (48%)
  waiting for transfers between devices  44.8 us (31%)
  Pallas kernels  24.2 us (17%)
  local copies, waits for them, and re-layouts  4.41 us (3%)
    ppermute x48, starting transfers between devices, exchange(): return lax.ppermute(block, axis, route)  60 us
    ppermute x48, waiting for transfers between devices, exchange(): return lax.ppermute(block, axis, route)  43.7 us
    pallas_call x76, Pallas kernels, call(): pl.pallas_call(kernel, out_shape=out_shape, in_specs=[place(op) for op in...  24.2 us
    ppermute x3, starting transfers between devices, exchange_next(): return lax.ppermute(block, axis, route)  9.69 us
  transfers between devices with their start and end apart: 51, of which 31 were waited for; matrix products, arithmetic and copies ran while one was open for 2% of the time, Pallas kernels for 16%

profile of v6, /device:TPU:0, one launch (start us, length us, event | category | flops | bytes accessed | tf_op | source)
XLA Modules:
  0.0 144.0 jit_solution(16686749595378835173)
XLA Ops:
  1.7 2.1 %collective-permute-start.4 = (bf16[1,16,2,128,128]{4,3,2,1,0:T(8,128)(2,1)S(1)}, bf16[1,16,2,128,128]{4,3,2,1,0:T(8,128)(2,1)S(1)}, u32[]{:S(2)}, u32[]{:S(2)}) collective-permute-start(bf16[1,16,2,128,128]{4,3,2,1,0:T(8,128)(2,1)S(1)} %get-tuple-element.6), channel_id=1, source_target_pairs={{0,8},{8,0},{16,24},{24,16},{32,40},{40,32},{48,56},{56,48},{64,72... | collective-permute-start | bytes 3145736 | tf_op jit(solution)/shard_map/ppermute | solution.py:20
  5.4 2.6 %slice.9.factor_ref = bf16[4,16,2,128,128]{4,3,2,1,0:T(8,128)(2,1)S(1)} slice(bf16[10,16,2,128,128]{4,3,2,1,0:T(8,128)(2,1)} %factor_ref.71), slice={[0:4], [0:16], [0:2], [0:128], [0:128]} | slice | bytes 8388608 | tf_op jit(solution)/shard_map/slice | solution.py:162
  12.7 4.0 %collective-permute-done.10.partner_ref = bf16[8,64,128]{2,1,0:T(8,128)(2,1)S(1)} collective-permute-done((bf16[8,64,128]{2,1,0:T(8,128)(2,1)S(1)}, bf16[8,64,128]{2,1,0:T(8,128)(2,1)S(1)}, u32[]{:S(2)}, u32[]{:S(2)}) %collective-permute-start.10) | collective-permute-done | bytes 131104 | tf_op jit(solution)/shard_map/ppermute | solution.py:20
  17.0 3.1 %collective-permute-start.11 = (bf16[8,64,128]{2,1,0:T(8,128)(2,1)S(1)}, bf16[8,64,128]{2,1,0:T(8,128)(2,1)S(1)}, u32[]{:S(2)}, u32[]{:S(2)}) collective-permute-start(bf16[8,64,128]{2,1,0:T(8,128)(2,1)S(1)} %shard_map.68.own_ref), channel_id=1, source_target_pairs={{0,4},{1,5},{2,6},{3,7},{4,0},{5,1},{6,2},{7,3},{8,12},{9,13},{10,... | collective-permute-start | bytes 393224 | tf_op jit(solution)/shard_map/ppermute | solution.py:20
  20.3 1.8 %collective-permute-start.2 = (bf16[8,64,128]{2,1,0:T(8,128)(2,1)S(1)}, bf16[8,64,128]{2,1,0:T(8,128)(2,1)S(1)}, u32[]{:S(2)}, u32[]{:S(2)}) collective-permute-start(bf16[8,64,128]{2,1,0:T(8,128)(2,1)S(1)} %shard_map.58.own_ref), channel_id=1, source_target_pairs={{0,4},{1,5},{2,6},{3,7},{4,0},{5,1},{6,2},{7,3},{8,12},{9,13},{10,... | collective-permute-start | bytes 393224 | tf_op jit(solution)/shard_map/ppermute | solution.py:20
  22.1 2.7 %collective-permute-done.11.partner_ref = bf16[8,64,128]{2,1,0:T(8,128)(2,1)S(1)} collective-permute-done((bf16[8,64,128]{2,1,0:T(8,128)(2,1)S(1)}, bf16[8,64,128]{2,1,0:T(8,128)(2,1)S(1)}, u32[]{:S(2)}, u32[]{:S(2)}) %collective-permute-start.11) | collective-permute-done | bytes 131104 | tf_op jit(solution)/shard_map/ppermute | solution.py:20
  25.0 1.8 %collective-permute-done.2.partner_ref = bf16[8,64,128]{2,1,0:T(8,128)(2,1)S(1)} collective-permute-done((bf16[8,64,128]{2,1,0:T(8,128)(2,1)S(1)}, bf16[8,64,128]{2,1,0:T(8,128)(2,1)S(1)}, u32[]{:S(2)}, u32[]{:S(2)}) %collective-permute-start.2) | collective-permute-done | bytes 131104 | tf_op jit(solution)/shard_map/ppermute | solution.py:20
  28.3 1.9 %collective-permute-start.3 = (bf16[8,64,128]{2,1,0:T(8,128)(2,1)S(1)}, bf16[8,64,128]{2,1,0:T(8,128)(2,1)S(1)}, u32[]{:S(2)}, u32[]{:S(2)}) collective-permute-start(bf16[8,64,128]{2,1,0:T(8,128)(2,1)S(1)} %shard_map.59.own_ref.partner_ref.refs_1_), channel_id=1, source_target_pairs={{0,8},{8,0},{16,24},{24,16},{32,40},{40,32},{48,56},{56,48},{64,72... | collective-permute-start | bytes 393224 | tf_op jit(solution)/shard_map/ppermute | solution.py:20
  30.2 3.5 %collective-permute-done.12.partner_ref.own_ref = bf16[8,64,128]{2,1,0:T(8,128)(2,1)S(1)} collective-permute-done((bf16[8,64,128]{2,1,0:T(8,128)(2,1)S(1)}, bf16[8,64,128]{2,1,0:T(8,128)(2,1)S(1)}, u32[]{:S(2)}, u32[]{:S(2)}) %collective-permute-start.12) | collective-permute-done | bytes 131104 | tf_op jit(solution)/shard_map/ppermute | solution.py:20
  34.0 2.6 %collective-permute-start.13 = (bf16[8,64,128]{2,1,0:T(8,128)(2,1)S(1)}, bf16[8,64,128]{2,1,0:T(8,128)(2,1)S(1)}, u32[]{:S(2)}, u32[]{:S(2)}) collective-permute-start(bf16[8,64,128]{2,1,0:T(8,128)(2,1)S(1)} %shard_map.71), channel_id=1, source_target_pairs={{0,24},{8,16},{16,8},{24,0},{32,56},{40,48},{48,40},{56,32},{64,88... | collective-permute-start | bytes 393224 | tf_op jit(solution)/shard_map/ppermute | solution.py:20
  38.2 2.3 %collective-permute-done.13.partner_ref = bf16[8,64,128]{2,1,0:T(8,128)(2,1)S(1)} collective-permute-done((bf16[8,64,128]{2,1,0:T(8,128)(2,1)S(1)}, bf16[8,64,128]{2,1,0:T(8,128)(2,1)S(1)}, u32[]{:S(2)}, u32[]{:S(2)}) %collective-permute-start.13) | collective-permute-done | bytes 131104 | tf_op jit(solution)/shard_map/ppermute | solution.py:20
  40.9 4.2 %collective-permute-start.15 = (bf16[16,64,128]{2,1,0:T(8,128)(2,1)S(1)}, bf16[16,64,128]{2,1,0:T(8,128)(2,1)S(1)}, u32[]{:S(2)}, u32[]{:S(2)}) collective-permute-start(bf16[16,64,128]{2,1,0:T(8,128)(2,1)S(1)} %shard_map.73.refs_1_), channel_id=1, source_target_pairs={{8,16},{16,8},{24,32},{32,24},{40,48},{48,40},{56,64},{64,56},{72,... | collective-permute-start | bytes 786440 | tf_op jit(solution)/shard_map/ppermute | solution.py:28
  47.7 3.8 %collective-permute-done.20.partner_ref.own_ref = bf16[8,64,128]{2,1,0:T(8,128)(2,1)S(1)} collective-permute-done((bf16[8,64,128]{2,1,0:T(8,128)(2,1)S(1)}, bf16[8,64,128]{2,1,0:T(8,128)(2,1)S(1)}, u32[]{:S(2)}, u32[]{:S(2)}) %collective-permute-start.20) | collective-permute-done | bytes 131104 | tf_op jit(solution)/shard_map/ppermute | solution.py:20
  53.6 1.8 %collective-permute-start.8 = (bf16[8,64,128]{2,1,0:T(8,128)(2,1)S(1)}, bf16[8,64,128]{2,1,0:T(8,128)(2,1)S(1)}, u32[]{:S(2)}, u32[]{:S(2)}) collective-permute-start(bf16[8,64,128]{2,1,0:T(8,128)(2,1)S(1)} %shard_map.64), channel_id=1, source_target_pairs={{0,96},{8,104},{16,112},{24,120},{32,64},{40,72},{48,80},{56,88},{... | collective-permute-start | bytes 393224 | tf_op jit(solution)/shard_map/ppermute | solution.py:20
  62.1 2.7 %collective-permute-start.27 = (bf16[16,64,128]{2,1,0:T(8,128)(2,1)S(1)}, bf16[16,64,128]{2,1,0:T(8,128)(2,1)S(1)}, u32[]{:S(2)}, u32[]{:S(2)}) collective-permute-start(bf16[16,64,128]{2,1,0:T(8,128)(2,1)S(1)} %shard_map.85.refs_1_), channel_id=1, source_target_pairs={{8,16},{16,8},{24,32},{32,24},{40,48},{48,40},{56,64},{64,56},{72,... | collective-permute-start | bytes 786440 | tf_op jit(solution)/shard_map/ppermute | solution.py:28
  65.0 1.9 %collective-permute-start.17 = (bf16[8,64,128]{2,1,0:T(8,128)(2,1)S(1)}, bf16[8,64,128]{2,1,0:T(8,128)(2,1)S(1)}, u32[]{:S(2)}, u32[]{:S(2)}) collective-permute-start(bf16[8,64,128]{2,1,0:T(8,128)(2,1)S(1)} %shard_map.77.own_ref.partner_ref), channel_id=1, source_target_pairs={{0,2},{1,3},{2,0},{3,1},{4,6},{5,7},{6,4},{7,5},{8,10},{9,11},{10,... | collective-permute-start | bytes 393224 | tf_op jit(solution)/shard_map/ppermute | solution.py:20
  67.6 2.0 %collective-permute-start.33 = (bf16[8,64,128]{2,1,0:T(8,128)(2,1)S(1)}, bf16[8,64,128]{2,1,0:T(8,128)(2,1)S(1)}, u32[]{:S(2)}, u32[]{:S(2)}) collective-permute-start(bf16[8,64,128]{2,1,0:T(8,128)(2,1)S(1)} %shard_map.101), channel_id=1, source_target_pairs={{0,6},{1,7},{2,4},{3,5},{4,2},{5,3},{6,0},{7,1},{8,14},{9,15},{10,... | collective-permute-start | bytes 393224 | tf_op jit(solution)/shard_map/ppermute | solution.py:20
  70.4 2.3 %collective-permute-start.19 = (bf16[8,64,128]{2,1,0:T(8,128)(2,1)S(1)}, bf16[8,64,128]{2,1,0:T(8,128)(2,1)S(1)}, u32[]{:S(2)}, u32[]{:S(2)}) collective-permute-start(bf16[8,64,128]{2,1,0:T(8,128)(2,1)S(1)} %shard_map.80), channel_id=1, source_target_pairs={{0,6},{1,7},{2,4},{3,5},{4,2},{5,3},{6,0},{7,1},{8,14},{9,15},{10,... | collective-permute-start | bytes 393224 | tf_op jit(solution)/shard_map/ppermute | solution.py:20
  75.0 1.9 %collective-permute-start.34 = (bf16[8,64,128]{2,1,0:T(8,128)(2,1)S(1)}, bf16[8,64,128]{2,1,0:T(8,128)(2,1)S(1)}, u32[]{:S(2)}, u32[]{:S(2)}) collective-permute-start(bf16[8,64,128]{2,1,0:T(8,128)(2,1)S(1)} %shard_map.102.own_ref.partner_ref), channel_id=1, source_target_pairs={{0,8},{8,0},{16,24},{24,16},{32,40},{40,32},{48,56},{56,48},{64,72... | collective-permute-start | bytes 393224 | tf_op jit(solution)/shard_map/ppermute | solution.py:20
  82.7 2.0 %collective-permute-start.24 = (bf16[8,64,128]{2,1,0:T(8,128)(2,1)S(1)}, bf16[8,64,128]{2,1,0:T(8,128)(2,1)S(1)}, u32[]{:S(2)}, u32[]{:S(2)}) collective-permute-start(bf16[8,64,128]{2,1,0:T(8,128)(2,1)S(1)} %shard_map.88), channel_id=1, source_target_pairs={{0,24},{8,16},{16,8},{24,0},{32,56},{40,48},{48,40},{56,32},{64,88... | collective-permute-start | bytes 393224 | tf_op jit(solution)/shard_map/ppermute | solution.py:20
  84.9 2.4 %collective-permute-done.35.partner_ref = bf16[8,64,128]{2,1,0:T(8,128)(2,1)S(1)} collective-permute-done((bf16[8,64,128]{2,1,0:T(8,128)(2,1)S(1)}, bf16[8,64,128]{2,1,0:T(8,128)(2,1)S(1)}, u32[]{:S(2)}, u32[]{:S(2)}) %collective-permute-start.35) | collective-permute-done | bytes 131104 | tf_op jit(solution)/shard_map/ppermute | solution.py:20
  92.8 3.0 %collective-permute-start.37 = (bf16[8,64,128]{2,1,0:T(8,128)(2,1)S(1)}, bf16[8,64,128]{2,1,0:T(8,128)(2,1)S(1)}, u32[]{:S(2)}, u32[]{:S(2)}) collective-permute-start(bf16[8,64,128]{2,1,0:T(8,128)(2,1)S(1)} %shard_map.108), channel_id=1, source_target_pairs={{0,96},{8,104},{16,112},{24,120},{32,64},{40,72},{48,80},{56,88},{... | collective-permute-start | bytes 393224 | tf_op jit(solution)/shard_map/ppermute | solution.py:20
  100.0 2.3 %collective-permute-done.26.partner_ref = bf16[8,64,128]{2,1,0:T(8,128)(2,1)S(1)} collective-permute-done((bf16[8,64,128]{2,1,0:T(8,128)(2,1)S(1)}, bf16[8,64,128]{2,1,0:T(8,128)(2,1)S(1)}, u32[]{:S(2)}, u32[]{:S(2)}) %collective-permute-start.26) | collective-permute-done | bytes 131104 | tf_op jit(solution)/shard_map/ppermute | solution.py:20
  103.6 2.8 %collective-permute-start.43 = (bf16[16,64,128]{2,1,0:T(8,128)(2,1)S(1)}, bf16[16,64,128]{2,1,0:T(8,128)(2,1)S(1)}, u32[]{:S(2)}, u32[]{:S(2)}) collective-permute-start(bf16[16,64,128]{2,1,0:T(8,128)(2,1)S(1)} %shard_map.110.refs_1_), channel_id=1, source_target_pairs={{8,16},{16,8},{24,32},{32,24},{40,48},{48,40},{56,64},{64,56},{72,... | collective-permute-start | bytes 786440 | tf_op jit(solution)/shard_map/ppermute | solution.py:28
  106.5 2.1 %collective-permute-start.29 = (bf16[8,64,128]{2,1,0:T(8,128)(2,1)S(1)}, bf16[8,64,128]{2,1,0:T(8,128)(2,1)S(1)}, u32[]{:S(2)}, u32[]{:S(2)}) collective-permute-start(bf16[8,64,128]{2,1,0:T(8,128)(2,1)S(1)} %shard_map.95.own_ref.partner_ref), channel_id=1, source_target_pairs={{0,2},{1,3},{2,0},{3,1},{4,6},{5,7},{6,4},{7,5},{8,10},{9,11},{10,... | collective-permute-start | bytes 393224 | tf_op jit(solution)/shard_map/ppermute | solution.py:20
  109.6 2.1 %collective-permute-start.46 = (bf16[8,64,128]{2,1,0:T(8,128)(2,1)S(1)}, bf16[8,64,128]{2,1,0:T(8,128)(2,1)S(1)}, u32[]{:S(2)}, u32[]{:S(2)}) collective-permute-start(bf16[8,64,128]{2,1,0:T(8,128)(2,1)S(1)} %shard_map.121), channel_id=1, source_target_pairs={{0,6},{1,7},{2,4},{3,5},{4,2},{5,3},{6,0},{7,1},{8,14},{9,15},{10,... | collective-permute-start | bytes 393224 | tf_op jit(solution)/shard_map/ppermute | solution.py:20
  112.5 2.3 %collective-permute-start.30 = (bf16[8,64,128]{2,1,0:T(8,128)(2,1)S(1)}, bf16[8,64,128]{2,1,0:T(8,128)(2,1)S(1)}, u32[]{:S(2)}, u32[]{:S(2)}) collective-permute-start(bf16[8,64,128]{2,1,0:T(8,128)(2,1)S(1)} %shard_map.97), channel_id=1, source_target_pairs={{0,6},{1,7},{2,4},{3,5},{4,2},{5,3},{6,0},{7,1},{8,14},{9,15},{10,... | collective-permute-start | bytes 393224 | tf_op jit(solution)/shard_map/ppermute | solution.py:20
  116.3 1.9 %collective-permute-start.47 = (bf16[8,64,128]{2,1,0:T(8,128)(2,1)S(1)}, bf16[8,64,128]{2,1,0:T(8,128)(2,1)S(1)}, u32[]{:S(2)}, u32[]{:S(2)}) collective-permute-start(bf16[8,64,128]{2,1,0:T(8,128)(2,1)S(1)} %shard_map.122.own_ref.partner_ref), channel_id=1, source_target_pairs={{0,8},{8,0},{16,24},{24,16},{32,40},{40,32},{48,56},{56,48},{64,72... | collective-permute-start | bytes 393224 | tf_op jit(solution)/shard_map/ppermute | solution.py:20
  124.4 1.9 %collective-permute-start.40 = (bf16[8,64,128]{2,1,0:T(8,128)(2,1)S(1)}, bf16[8,64,128]{2,1,0:T(8,128)(2,1)S(1)}, u32[]{:S(2)}, u32[]{:S(2)}) collective-permute-start(bf16[8,64,128]{2,1,0:T(8,128)(2,1)S(1)} %shard_map.113), channel_id=1, source_target_pairs={{0,24},{8,16},{16,8},{24,0},{32,56},{40,48},{48,40},{56,32},{64,88... | collective-permute-start | bytes 393224 | tf_op jit(solution)/shard_map/ppermute | solution.py:20
  126.8 2.7 %collective-permute-done.48.partner_ref = bf16[8,64,128]{2,1,0:T(8,128)(2,1)S(1)} collective-permute-done((bf16[8,64,128]{2,1,0:T(8,128)(2,1)S(1)}, bf16[8,64,128]{2,1,0:T(8,128)(2,1)S(1)}, u32[]{:S(2)}, u32[]{:S(2)}) %collective-permute-start.48) | collective-permute-done | bytes 131104 | tf_op jit(solution)/shard_map/ppermute | solution.py:20
  136.8 1.9 %collective-permute-start.42 = (bf16[8,64,128]{2,1,0:T(8,128)(2,1)S(1)}, bf16[8,64,128]{2,1,0:T(8,128)(2,1)S(1)}, u32[]{:S(2)}, u32[]{:S(2)}) collective-permute-start(bf16[8,64,128]{2,1,0:T(8,128)(2,1)S(1)} %shard_map.116), channel_id=1, source_target_pairs={{0,96},{8,104},{16,112},{24,120},{32,64},{40,72},{48,80},{56,88},{... | collective-permute-start | bytes 393224 | tf_op jit(solution)/shard_map/ppermute | solution.py:20
  139.2 2.2 %collective-permute-done.50.partner_ref = bf16[8,64,128]{2,1,0:T(8,128)(2,1)S(1)} collective-permute-done((bf16[8,64,128]{2,1,0:T(8,128)(2,1)S(1)}, bf16[8,64,128]{2,1,0:T(8,128)(2,1)S(1)}, u32[]{:S(2)}, u32[]{:S(2)}) %collective-permute-start.50) | collective-permute-done | bytes 131104 | tf_op jit(solution)/shard_map/ppermute | solution.py:20
  (163 shorter events, 64.3 us)
Async XLA Ops:
  1.7 32.0 %collective-permute-start.4 = (bf16[1,16,2,128,128]{4,3,2,1,0:T(8,128)(2,1)S(1)}, bf16[1,16,2,128,128]{4,3,2,1,0:T(8,128)(2,1)S(1)}, u32[]{:S(2)}, u32[]{:S(2)}) collective-permute-start(bf16[1,16,2,128,128]{4,3,2,1,0:T(8,128)(2,1)S(1)} %get-tuple-element.6), channel_id=1, source_target_pairs={{0,8},{8,0},{16,24},{24,16},{32,40},{40,32},{48,56},{56,48},{64,72... | collective-permute-start | bytes 3145736 | tf_op jit(solution)/shard_map/ppermute | solution.py:20
  3.8 43.0 %collective-permute-start.7 = (bf16[1,16,2,128,128]{4,3,2,1,0:T(8,128)(2,1)S(1)}, bf16[1,16,2,128,128]{4,3,2,1,0:T(8,128)(2,1)S(1)}, u32[]{:S(2)}, u32[]{:S(2)}) collective-permute-start(bf16[1,16,2,128,128]{4,3,2,1,0:T(8,128)(2,1)S(1)} %get-tuple-element.5), channel_id=1, source_target_pairs={{0,32},{8,40},{16,48},{24,56},{32,0},{40,8},{48,16},{56,24},{64,96... | collective-permute-start | bytes 3145736 | tf_op jit(solution)/shard_map/ppermute | solution.py:20
  10.3 6.4 %collective-permute-start.10 = (bf16[8,64,128]{2,1,0:T(8,128)(2,1)S(1)}, bf16[8,64,128]{2,1,0:T(8,128)(2,1)S(1)}, u32[]{:S(2)}, u32[]{:S(2)}) collective-permute-start(bf16[8,64,128]{2,1,0:T(8,128)(2,1)S(1)} %shard_map.67.own_ref), channel_id=1, source_target_pairs={{0,2},{1,3},{2,0},{3,1},{4,6},{5,7},{6,4},{7,5},{8,10},{9,11},{10,... | collective-permute-start | bytes 393224 | tf_op jit(solution)/shard_map/ppermute | solution.py:20
  12.1 8.0 %collective-permute-start.1 = (bf16[8,64,128]{2,1,0:T(8,128)(2,1)S(1)}, bf16[8,64,128]{2,1,0:T(8,128)(2,1)S(1)}, u32[]{:S(2)}, u32[]{:S(2)}) collective-permute-start(bf16[8,64,128]{2,1,0:T(8,128)(2,1)S(1)} %shard_map.57.own_ref), channel_id=1, source_target_pairs={{0,2},{1,3},{2,0},{3,1},{4,6},{5,7},{6,4},{7,5},{8,10},{9,11},{10,... | collective-permute-start | bytes 393224 | tf_op jit(solution)/shard_map/ppermute | solution.py:20
  17.0 7.8 %collective-permute-start.11 = (bf16[8,64,128]{2,1,0:T(8,128)(2,1)S(1)}, bf16[8,64,128]{2,1,0:T(8,128)(2,1)S(1)}, u32[]{:S(2)}, u32[]{:S(2)}) collective-permute-start(bf16[8,64,128]{2,1,0:T(8,128)(2,1)S(1)} %shard_map.68.own_ref), channel_id=1, source_target_pairs={{0,4},{1,5},{2,6},{3,7},{4,0},{5,1},{6,2},{7,3},{8,12},{9,13},{10,... | collective-permute-start | bytes 393224 | tf_op jit(solution)/shard_map/ppermute | solution.py:20
  20.3 6.6 %collective-permute-start.2 = (bf16[8,64,128]{2,1,0:T(8,128)(2,1)S(1)}, bf16[8,64,128]{2,1,0:T(8,128)(2,1)S(1)}, u32[]{:S(2)}, u32[]{:S(2)}) collective-permute-start(bf16[8,64,128]{2,1,0:T(8,128)(2,1)S(1)} %shard_map.58.own_ref), channel_id=1, source_target_pairs={{0,4},{1,5},{2,6},{3,7},{4,0},{5,1},{6,2},{7,3},{8,12},{9,13},{10,... | collective-permute-start | bytes 393224 | tf_op jit(solution)/shard_map/ppermute | solution.py:20
  27.2 39.8 %collective-permute-start.18 = (bf16[1,16,2,128,128]{4,3,2,1,0:T(8,128)(2,1)S(1)}, bf16[1,16,2,128,128]{4,3,2,1,0:T(8,128)(2,1)S(1)}, u32[]{:S(2)}, u32[]{:S(2)}) collective-permute-start(bf16[1,16,2,128,128]{4,3,2,1,0:T(8,128)(2,1)S(1)} %shard_map.79), channel_id=1, source_target_pairs={{0,2},{1,3},{2,0},{3,1},{4,6},{5,7},{6,4},{7,5},{8,10},{9,11},{10,... | collective-permute-start | bytes 3145736 | tf_op jit(solution)/shard_map/ppermute | solution.py:20
  28.3 8.2 %collective-permute-start.3 = (bf16[8,64,128]{2,1,0:T(8,128)(2,1)S(1)}, bf16[8,64,128]{2,1,0:T(8,128)(2,1)S(1)}, u32[]{:S(2)}, u32[]{:S(2)}) collective-permute-start(bf16[8,64,128]{2,1,0:T(8,128)(2,1)S(1)} %shard_map.59.own_ref.partner_ref.refs_1_), channel_id=1, source_target_pairs={{0,8},{8,0},{16,24},{24,16},{32,40},{40,32},{48,56},{56,48},{64,72... | collective-permute-start | bytes 393224 | tf_op jit(solution)/shard_map/ppermute | solution.py:20
  34.0 6.6 %collective-permute-start.13 = (bf16[8,64,128]{2,1,0:T(8,128)(2,1)S(1)}, bf16[8,64,128]{2,1,0:T(8,128)(2,1)S(1)}, u32[]{:S(2)}, u32[]{:S(2)}) collective-permute-start(bf16[8,64,128]{2,1,0:T(8,128)(2,1)S(1)} %shard_map.71), channel_id=1, source_target_pairs={{0,24},{8,16},{16,8},{24,0},{32,56},{40,48},{48,40},{56,32},{64,88... | collective-permute-start | bytes 393224 | tf_op jit(solution)/shard_map/ppermute | solution.py:20
  36.8 8.3 %collective-permute-start.5 = (bf16[8,64,128]{2,1,0:T(8,128)(2,1)S(1)}, bf16[8,64,128]{2,1,0:T(8,128)(2,1)S(1)}, u32[]{:S(2)}, u32[]{:S(2)}) collective-permute-start(bf16[8,64,128]{2,1,0:T(8,128)(2,1)S(1)} %shard_map.61), channel_id=1, source_target_pairs={{0,24},{8,16},{16,8},{24,0},{32,56},{40,48},{48,40},{56,32},{64,88... | collective-permute-start | bytes 393224 | tf_op jit(solution)/shard_map/ppermute | solution.py:20
  40.8 15.1 %collective-permute-start.14 = (bf16[16,64,128]{2,1,0:T(8,128)(2,1)S(1)}, bf16[16,64,128]{2,1,0:T(8,128)(2,1)S(1)}, u32[]{:S(2)}, u32[]{:S(2)}) collective-permute-start(bf16[16,64,128]{2,1,0:T(8,128)(2,1)S(1)} %shard_map.73.refs_1_), channel_id=1, source_target_pairs={{0,8},{8,0},{16,24},{24,16},{32,40},{40,32},{48,56},{56,48},{64,72... | collective-permute-start | bytes 786440 | tf_op jit(solution)/shard_map/ppermute | solution.py:20
  40.9 15.0 %collective-permute-start.15 = (bf16[16,64,128]{2,1,0:T(8,128)(2,1)S(1)}, bf16[16,64,128]{2,1,0:T(8,128)(2,1)S(1)}, u32[]{:S(2)}, u32[]{:S(2)}) collective-permute-start(bf16[16,64,128]{2,1,0:T(8,128)(2,1)S(1)} %shard_map.73.refs_1_), channel_id=1, source_target_pairs={{8,16},{16,8},{24,32},{32,24},{40,48},{48,40},{56,64},{64,56},{72,... | collective-permute-start | bytes 786440 | tf_op jit(solution)/shard_map/ppermute | solution.py:28
  45.1 6.4 %collective-permute-start.20 = (bf16[8,64,128]{2,1,0:T(8,128)(2,1)S(1)}, bf16[8,64,128]{2,1,0:T(8,128)(2,1)S(1)}, u32[]{:S(2)}, u32[]{:S(2)}) collective-permute-start(bf16[8,64,128]{2,1,0:T(8,128)(2,1)S(1)} %shard_map.72.refs_2_.own_ref.partner_ref), channel_id=1, source_target_pairs={{0,32},{8,40},{16,48},{24,56},{32,0},{40,8},{48,16},{56,24},{64,96... | collective-permute-start | bytes 393224 | tf_op jit(solution)/shard_map/ppermute | solution.py:20
  46.8 6.5 %collective-permute-start.6 = (bf16[8,64,128]{2,1,0:T(8,128)(2,1)S(1)}, bf16[8,64,128]{2,1,0:T(8,128)(2,1)S(1)}, u32[]{:S(2)}, u32[]{:S(2)}) collective-permute-start(bf16[8,64,128]{2,1,0:T(8,128)(2,1)S(1)} %shard_map.62.own_ref.partner_ref), channel_id=1, source_target_pairs={{0,32},{8,40},{16,48},{24,56},{32,0},{40,8},{48,16},{56,24},{64,96... | collective-permute-start | bytes 393224 | tf_op jit(solution)/shard_map/ppermute | solution.py:20
  51.8 6.3 %collective-permute-start.21 = (bf16[8,64,128]{2,1,0:T(8,128)(2,1)S(1)}, bf16[8,64,128]{2,1,0:T(8,128)(2,1)S(1)}, u32[]{:S(2)}, u32[]{:S(2)}) collective-permute-start(bf16[8,64,128]{2,1,0:T(8,128)(2,1)S(1)} %shard_map.82), channel_id=1, source_target_pairs={{0,96},{8,104},{16,112},{24,120},{32,64},{40,72},{48,80},{56,88},{... | collective-permute-start | bytes 393224 | tf_op jit(solution)/shard_map/ppermute | solution.py:20
  53.6 6.5 %collective-permute-start.8 = (bf16[8,64,128]{2,1,0:T(8,128)(2,1)S(1)}, bf16[8,64,128]{2,1,0:T(8,128)(2,1)S(1)}, u32[]{:S(2)}, u32[]{:S(2)}) collective-permute-start(bf16[8,64,128]{2,1,0:T(8,128)(2,1)S(1)} %shard_map.64), channel_id=1, source_target_pairs={{0,96},{8,104},{16,112},{24,120},{32,64},{40,72},{48,80},{56,88},{... | collective-permute-start | bytes 393224 | tf_op jit(solution)/shard_map/ppermute | solution.py:20
  62.1 11.5 %collective-permute-start.27 = (bf16[16,64,128]{2,1,0:T(8,128)(2,1)S(1)}, bf16[16,64,128]{2,1,0:T(8,128)(2,1)S(1)}, u32[]{:S(2)}, u32[]{:S(2)}) collective-permute-start(bf16[16,64,128]{2,1,0:T(8,128)(2,1)S(1)} %shard_map.85.refs_1_), channel_id=1, source_target_pairs={{8,16},{16,8},{24,32},{32,24},{40,48},{48,40},{56,64},{64,56},{72,... | collective-permute-start | bytes 786440 | tf_op jit(solution)/shard_map/ppermute | solution.py:28
  67.0 10.2 %collective-permute-start.22 = (bf16[16,64,128]{2,1,0:T(8,128)(2,1)S(1)}, bf16[16,64,128]{2,1,0:T(8,128)(2,1)S(1)}, u32[]{:S(2)}, u32[]{:S(2)}) collective-permute-start(bf16[16,64,128]{2,1,0:T(8,128)(2,1)S(1)} %shard_map.85.refs_1_), channel_id=1, source_target_pairs={{0,8},{8,0},{16,24},{24,16},{32,40},{40,32},{48,56},{56,48},{64,72... | collective-permute-start | bytes 786440 | tf_op jit(solution)/shard_map/ppermute | solution.py:20
  67.6 7.1 %collective-permute-start.33 = (bf16[8,64,128]{2,1,0:T(8,128)(2,1)S(1)}, bf16[8,64,128]{2,1,0:T(8,128)(2,1)S(1)}, u32[]{:S(2)}, u32[]{:S(2)}) collective-permute-start(bf16[8,64,128]{2,1,0:T(8,128)(2,1)S(1)} %shard_map.101), channel_id=1, source_target_pairs={{0,6},{1,7},{2,4},{3,5},{4,2},{5,3},{6,0},{7,1},{8,14},{9,15},{10,... | collective-permute-start | bytes 393224 | tf_op jit(solution)/shard_map/ppermute | solution.py:20
  70.4 6.8 %collective-permute-start.19 = (bf16[8,64,128]{2,1,0:T(8,128)(2,1)S(1)}, bf16[8,64,128]{2,1,0:T(8,128)(2,1)S(1)}, u32[]{:S(2)}, u32[]{:S(2)}) collective-permute-start(bf16[8,64,128]{2,1,0:T(8,128)(2,1)S(1)} %shard_map.80), channel_id=1, source_target_pairs={{0,6},{1,7},{2,4},{3,5},{4,2},{5,3},{6,0},{7,1},{8,14},{9,15},{10,... | collective-permute-start | bytes 393224 | tf_op jit(solution)/shard_map/ppermute | solution.py:20
  81.1 6.3 %collective-permute-start.35 = (bf16[8,64,128]{2,1,0:T(8,128)(2,1)S(1)}, bf16[8,64,128]{2,1,0:T(8,128)(2,1)S(1)}, u32[]{:S(2)}, u32[]{:S(2)}) collective-permute-start(bf16[8,64,128]{2,1,0:T(8,128)(2,1)S(1)} %shard_map.105), channel_id=1, source_target_pairs={{0,24},{8,16},{16,8},{24,0},{32,56},{40,48},{48,40},{56,32},{64,88... | collective-permute-start | bytes 393224 | tf_op jit(solution)/shard_map/ppermute | solution.py:20
  82.7 6.3 %collective-permute-start.24 = (bf16[8,64,128]{2,1,0:T(8,128)(2,1)S(1)}, bf16[8,64,128]{2,1,0:T(8,128)(2,1)S(1)}, u32[]{:S(2)}, u32[]{:S(2)}) collective-permute-start(bf16[8,64,128]{2,1,0:T(8,128)(2,1)S(1)} %shard_map.88), channel_id=1, source_target_pairs={{0,24},{8,16},{16,8},{24,0},{32,56},{40,48},{48,40},{56,32},{64,88... | collective-permute-start | bytes 393224 | tf_op jit(solution)/shard_map/ppermute | solution.py:20
  89.2 6.6 %collective-permute-start.25 = (bf16[8,64,128]{2,1,0:T(8,128)(2,1)S(1)}, bf16[8,64,128]{2,1,0:T(8,128)(2,1)S(1)}, u32[]{:S(2)}, u32[]{:S(2)}) collective-permute-start(bf16[8,64,128]{2,1,0:T(8,128)(2,1)S(1)} %shard_map.89.own_ref.partner_ref), channel_id=1, source_target_pairs={{0,32},{8,40},{16,48},{24,56},{32,0},{40,8},{48,16},{56,24},{64,96... | collective-permute-start | bytes 393224 | tf_op jit(solution)/shard_map/ppermute | solution.py:20
  92.8 6.3 %collective-permute-start.37 = (bf16[8,64,128]{2,1,0:T(8,128)(2,1)S(1)}, bf16[8,64,128]{2,1,0:T(8,128)(2,1)S(1)}, u32[]{:S(2)}, u32[]{:S(2)}) collective-permute-start(bf16[8,64,128]{2,1,0:T(8,128)(2,1)S(1)} %shard_map.108), channel_id=1, source_target_pairs={{0,96},{8,104},{16,112},{24,120},{32,64},{40,72},{48,80},{56,88},{... | collective-permute-start | bytes 393224 | tf_op jit(solution)/shard_map/ppermute | solution.py:20
  96.1 6.3 %collective-permute-start.26 = (bf16[8,64,128]{2,1,0:T(8,128)(2,1)S(1)}, bf16[8,64,128]{2,1,0:T(8,128)(2,1)S(1)}, u32[]{:S(2)}, u32[]{:S(2)}) collective-permute-start(bf16[8,64,128]{2,1,0:T(8,128)(2,1)S(1)} %shard_map.91), channel_id=1, source_target_pairs={{0,96},{8,104},{16,112},{24,120},{32,64},{40,72},{48,80},{56,88},{... | collective-permute-start | bytes 393224 | tf_op jit(solution)/shard_map/ppermute | solution.py:20
  103.6 12.1 %collective-permute-start.43 = (bf16[16,64,128]{2,1,0:T(8,128)(2,1)S(1)}, bf16[16,64,128]{2,1,0:T(8,128)(2,1)S(1)}, u32[]{:S(2)}, u32[]{:S(2)}) collective-permute-start(bf16[16,64,128]{2,1,0:T(8,128)(2,1)S(1)} %shard_map.110.refs_1_), channel_id=1, source_target_pairs={{8,16},{16,8},{24,32},{32,24},{40,48},{48,40},{56,64},{64,56},{72,... | collective-permute-start | bytes 786440 | tf_op jit(solution)/shard_map/ppermute | solution.py:28
  108.6 9.6 %collective-permute-start.38 = (bf16[16,64,128]{2,1,0:T(8,128)(2,1)S(1)}, bf16[16,64,128]{2,1,0:T(8,128)(2,1)S(1)}, u32[]{:S(2)}, u32[]{:S(2)}) collective-permute-start(bf16[16,64,128]{2,1,0:T(8,128)(2,1)S(1)} %shard_map.110.refs_1_), channel_id=1, source_target_pairs={{0,8},{8,0},{16,24},{24,16},{32,40},{40,32},{48,56},{56,48},{64,72... | collective-permute-start | bytes 786440 | tf_op jit(solution)/shard_map/ppermute | solution.py:20
  109.6 6.4 %collective-permute-start.46 = (bf16[8,64,128]{2,1,0:T(8,128)(2,1)S(1)}, bf16[8,64,128]{2,1,0:T(8,128)(2,1)S(1)}, u32[]{:S(2)}, u32[]{:S(2)}) collective-permute-start(bf16[8,64,128]{2,1,0:T(8,128)(2,1)S(1)} %shard_map.121), channel_id=1, source_target_pairs={{0,6},{1,7},{2,4},{3,5},{4,2},{5,3},{6,0},{7,1},{8,14},{9,15},{10,... | collective-permute-start | bytes 393224 | tf_op jit(solution)/shard_map/ppermute | solution.py:20
  112.5 6.5 %collective-permute-start.30 = (bf16[8,64,128]{2,1,0:T(8,128)(2,1)S(1)}, bf16[8,64,128]{2,1,0:T(8,128)(2,1)S(1)}, u32[]{:S(2)}, u32[]{:S(2)}) collective-permute-start(bf16[8,64,128]{2,1,0:T(8,128)(2,1)S(1)} %shard_map.97), channel_id=1, source_target_pairs={{0,6},{1,7},{2,4},{3,5},{4,2},{5,3},{6,0},{7,1},{8,14},{9,15},{10,... | collective-permute-start | bytes 393224 | tf_op jit(solution)/shard_map/ppermute | solution.py:20
  122.8 6.8 %collective-permute-start.48 = (bf16[8,64,128]{2,1,0:T(8,128)(2,1)S(1)}, bf16[8,64,128]{2,1,0:T(8,128)(2,1)S(1)}, u32[]{:S(2)}, u32[]{:S(2)}) collective-permute-start(bf16[8,64,128]{2,1,0:T(8,128)(2,1)S(1)} %shard_map.125), channel_id=1, source_target_pairs={{0,24},{8,16},{16,8},{24,0},{32,56},{40,48},{48,40},{56,32},{64,88... | collective-permute-start | bytes 393224 | tf_op jit(solution)/shard_map/ppermute | solution.py:20
  124.4 6.5 %collective-permute-start.40 = (bf16[8,64,128]{2,1,0:T(8,128)(2,1)S(1)}, bf16[8,64,128]{2,1,0:T(8,128)(2,1)S(1)}, u32[]{:S(2)}, u32[]{:S(2)}) collective-permute-start(bf16[8,64,128]{2,1,0:T(8,128)(2,1)S(1)} %shard_map.113), channel_id=1, source_target_pairs={{0,24},{8,16},{16,8},{24,0},{32,56},{40,48},{48,40},{56,32},{64,88... | collective-permute-start | bytes 393224 | tf_op jit(solution)/shard_map/ppermute | solution.py:20
  136.8 6.3 %collective-permute-start.42 = (bf16[8,64,128]{2,1,0:T(8,128)(2,1)S(1)}, bf16[8,64,128]{2,1,0:T(8,128)(2,1)S(1)}, u32[]{:S(2)}, u32[]{:S(2)}) collective-permute-start(bf16[8,64,128]{2,1,0:T(8,128)(2,1)S(1)} %shard_map.116), channel_id=1, source_target_pairs={{0,96},{8,104},{16,112},{24,120},{32,64},{40,72},{48,80},{56,88},{... | collective-permute-start | bytes 393224 | tf_op jit(solution)/shard_map/ppermute | solution.py:20
  (26 other events, 139.9 us)

commit v7 on v5

--- a/solution.py
+++ b/solution.py
@@ -9,7 +9,7 @@
 
 ITERS = 3
 CHAINS = 2
-NEAR_TIES = ((1, 0, 0), (2, 0, 0))
+NEAR_TIES = ((1, 0, 0), (1, 1, 0))
 
 
 coupling = 0.4

time: 144 us -> 144 us (level)
  no operation moved by 1% of the time
where the time goes in v7:
time: 144 us
  starting transfers between devices  69.9 us (49%)
  waiting for transfers between devices  44.4 us (31%)
  Pallas kernels  24.2 us (17%)
  local copies, waits for them, and re-layouts  4.41 us (3%)
    ppermute x48, starting transfers between devices, exchange(): return lax.ppermute(block, axis, route)  60.1 us
    ppermute x48, waiting for transfers between devices, exchange(): return lax.ppermute(block, axis, route)  43.4 us
    pallas_call x76, Pallas kernels, call(): pl.pallas_call(kernel, out_shape=out_shape, in_specs=[place(op) for op in...  24.2 us
    ppermute x3, starting transfers between devices, exchange_next(): return lax.ppermute(block, axis, route)  9.84 us
  transfers between devices with their start and end apart: 51, of which 31 were waited for; matrix products, arithmetic and copies ran while one was open for 2% of the time, Pallas kernels for 16%

profile of v7, /device:TPU:0, one launch (start us, length us, event | category | flops | bytes accessed | tf_op | source)
XLA Modules:
  0.0 143.8 jit_solution(9249973182225638410)
XLA Ops:
  1.7 2.1 %collective-permute-start.4 = (bf16[1,16,2,128,128]{4,3,2,1,0:T(8,128)(2,1)S(1)}, bf16[1,16,2,128,128]{4,3,2,1,0:T(8,128)(2,1)S(1)}, u32[]{:S(2)}, u32[]{:S(2)}) collective-permute-start(bf16[1,16,2,128,128]{4,3,2,1,0:T(8,128)(2,1)S(1)} %get-tuple-element.6), channel_id=1, source_target_pairs={{0,8},{8,0},{16,24},{24,16},{32,40},{40,32},{48,56},{56,48},{64,72... | collective-permute-start | bytes 3145736 | tf_op jit(solution)/shard_map/ppermute | solution.py:20
  5.4 2.6 %slice.9.factor_ref = bf16[4,16,2,128,128]{4,3,2,1,0:T(8,128)(2,1)S(1)} slice(bf16[10,16,2,128,128]{4,3,2,1,0:T(8,128)(2,1)} %factor_ref.71), slice={[0:4], [0:16], [0:2], [0:128], [0:128]} | slice | bytes 8388608 | tf_op jit(solution)/shard_map/slice | solution.py:162
  12.7 4.0 %collective-permute-done.10.partner_ref = bf16[8,64,128]{2,1,0:T(8,128)(2,1)S(1)} collective-permute-done((bf16[8,64,128]{2,1,0:T(8,128)(2,1)S(1)}, bf16[8,64,128]{2,1,0:T(8,128)(2,1)S(1)}, u32[]{:S(2)}, u32[]{:S(2)}) %collective-permute-start.10) | collective-permute-done | bytes 131104 | tf_op jit(solution)/shard_map/ppermute | solution.py:20
  17.0 3.1 %collective-permute-start.11 = (bf16[8,64,128]{2,1,0:T(8,128)(2,1)S(1)}, bf16[8,64,128]{2,1,0:T(8,128)(2,1)S(1)}, u32[]{:S(2)}, u32[]{:S(2)}) collective-permute-start(bf16[8,64,128]{2,1,0:T(8,128)(2,1)S(1)} %shard_map.68.own_ref), channel_id=1, source_target_pairs={{0,4},{1,5},{2,6},{3,7},{4,0},{5,1},{6,2},{7,3},{8,12},{9,13},{10,... | collective-permute-start | bytes 393224 | tf_op jit(solution)/shard_map/ppermute | solution.py:20
  20.3 1.8 %collective-permute-start.2 = (bf16[8,64,128]{2,1,0:T(8,128)(2,1)S(1)}, bf16[8,64,128]{2,1,0:T(8,128)(2,1)S(1)}, u32[]{:S(2)}, u32[]{:S(2)}) collective-permute-start(bf16[8,64,128]{2,1,0:T(8,128)(2,1)S(1)} %shard_map.58.own_ref), channel_id=1, source_target_pairs={{0,4},{1,5},{2,6},{3,7},{4,0},{5,1},{6,2},{7,3},{8,12},{9,13},{10,... | collective-permute-start | bytes 393224 | tf_op jit(solution)/shard_map/ppermute | solution.py:20
  22.1 2.7 %collective-permute-done.11.partner_ref = bf16[8,64,128]{2,1,0:T(8,128)(2,1)S(1)} collective-permute-done((bf16[8,64,128]{2,1,0:T(8,128)(2,1)S(1)}, bf16[8,64,128]{2,1,0:T(8,128)(2,1)S(1)}, u32[]{:S(2)}, u32[]{:S(2)}) %collective-permute-start.11) | collective-permute-done | bytes 131104 | tf_op jit(solution)/shard_map/ppermute | solution.py:20
  25.0 1.8 %collective-permute-done.2.partner_ref = bf16[8,64,128]{2,1,0:T(8,128)(2,1)S(1)} collective-permute-done((bf16[8,64,128]{2,1,0:T(8,128)(2,1)S(1)}, bf16[8,64,128]{2,1,0:T(8,128)(2,1)S(1)}, u32[]{:S(2)}, u32[]{:S(2)}) %collective-permute-start.2) | collective-permute-done | bytes 131104 | tf_op jit(solution)/shard_map/ppermute | solution.py:20
  28.3 1.9 %collective-permute-start.3 = (bf16[8,64,128]{2,1,0:T(8,128)(2,1)S(1)}, bf16[8,64,128]{2,1,0:T(8,128)(2,1)S(1)}, u32[]{:S(2)}, u32[]{:S(2)}) collective-permute-start(bf16[8,64,128]{2,1,0:T(8,128)(2,1)S(1)} %shard_map.59.own_ref.partner_ref.refs_1_), channel_id=1, source_target_pairs={{0,8},{8,0},{16,24},{24,16},{32,40},{40,32},{48,56},{56,48},{64,72... | collective-permute-start | bytes 393224 | tf_op jit(solution)/shard_map/ppermute | solution.py:20
  30.2 3.5 %collective-permute-done.12.partner_ref.own_ref = bf16[8,64,128]{2,1,0:T(8,128)(2,1)S(1)} collective-permute-done((bf16[8,64,128]{2,1,0:T(8,128)(2,1)S(1)}, bf16[8,64,128]{2,1,0:T(8,128)(2,1)S(1)}, u32[]{:S(2)}, u32[]{:S(2)}) %collective-permute-start.12) | collective-permute-done | bytes 131104 | tf_op jit(solution)/shard_map/ppermute | solution.py:20
  34.0 2.6 %collective-permute-start.13 = (bf16[8,64,128]{2,1,0:T(8,128)(2,1)S(1)}, bf16[8,64,128]{2,1,0:T(8,128)(2,1)S(1)}, u32[]{:S(2)}, u32[]{:S(2)}) collective-permute-start(bf16[8,64,128]{2,1,0:T(8,128)(2,1)S(1)} %shard_map.71), channel_id=1, source_target_pairs={{0,24},{8,16},{16,8},{24,0},{32,56},{40,48},{48,40},{56,32},{64,88... | collective-permute-start | bytes 393224 | tf_op jit(solution)/shard_map/ppermute | solution.py:20
  38.2 2.3 %collective-permute-done.13.partner_ref = bf16[8,64,128]{2,1,0:T(8,128)(2,1)S(1)} collective-permute-done((bf16[8,64,128]{2,1,0:T(8,128)(2,1)S(1)}, bf16[8,64,128]{2,1,0:T(8,128)(2,1)S(1)}, u32[]{:S(2)}, u32[]{:S(2)}) %collective-permute-start.13) | collective-permute-done | bytes 131104 | tf_op jit(solution)/shard_map/ppermute | solution.py:20
  40.9 4.2 %collective-permute-start.15 = (bf16[16,64,128]{2,1,0:T(8,128)(2,1)S(1)}, bf16[16,64,128]{2,1,0:T(8,128)(2,1)S(1)}, u32[]{:S(2)}, u32[]{:S(2)}) collective-permute-start(bf16[16,64,128]{2,1,0:T(8,128)(2,1)S(1)} %shard_map.73.refs_1_), channel_id=1, source_target_pairs={{8,16},{16,8},{24,32},{32,24},{40,48},{48,40},{56,64},{64,56},{72,... | collective-permute-start | bytes 786440 | tf_op jit(solution)/shard_map/ppermute | solution.py:28
  47.7 3.8 %collective-permute-done.24.partner_ref.own_ref = bf16[8,64,128]{2,1,0:T(8,128)(2,1)S(1)} collective-permute-done((bf16[8,64,128]{2,1,0:T(8,128)(2,1)S(1)}, bf16[8,64,128]{2,1,0:T(8,128)(2,1)S(1)}, u32[]{:S(2)}, u32[]{:S(2)}) %collective-permute-start.24) | collective-permute-done | bytes 131104 | tf_op jit(solution)/shard_map/ppermute | solution.py:20
  53.6 1.8 %collective-permute-start.8 = (bf16[8,64,128]{2,1,0:T(8,128)(2,1)S(1)}, bf16[8,64,128]{2,1,0:T(8,128)(2,1)S(1)}, u32[]{:S(2)}, u32[]{:S(2)}) collective-permute-start(bf16[8,64,128]{2,1,0:T(8,128)(2,1)S(1)} %shard_map.64), channel_id=1, source_target_pairs={{0,96},{8,104},{16,112},{24,120},{32,64},{40,72},{48,80},{56,88},{... | collective-permute-start | bytes 393224 | tf_op jit(solution)/shard_map/ppermute | solution.py:20
  62.1 2.7 %collective-permute-start.27 = (bf16[16,64,128]{2,1,0:T(8,128)(2,1)S(1)}, bf16[16,64,128]{2,1,0:T(8,128)(2,1)S(1)}, u32[]{:S(2)}, u32[]{:S(2)}) collective-permute-start(bf16[16,64,128]{2,1,0:T(8,128)(2,1)S(1)} %shard_map.91.refs_1_), channel_id=1, source_target_pairs={{8,16},{16,8},{24,32},{32,24},{40,48},{48,40},{56,64},{64,56},{72,... | collective-permute-start | bytes 786440 | tf_op jit(solution)/shard_map/ppermute | solution.py:28
  65.0 1.9 %collective-permute-start.17 = (bf16[8,64,128]{2,1,0:T(8,128)(2,1)S(1)}, bf16[8,64,128]{2,1,0:T(8,128)(2,1)S(1)}, u32[]{:S(2)}, u32[]{:S(2)}) collective-permute-start(bf16[8,64,128]{2,1,0:T(8,128)(2,1)S(1)} %shard_map.77.own_ref.partner_ref), channel_id=1, source_target_pairs={{0,2},{1,3},{2,0},{3,1},{4,6},{5,7},{6,4},{7,5},{8,10},{9,11},{10,... | collective-permute-start | bytes 393224 | tf_op jit(solution)/shard_map/ppermute | solution.py:20
  67.7 2.0 %collective-permute-start.37 = (bf16[8,64,128]{2,1,0:T(8,128)(2,1)S(1)}, bf16[8,64,128]{2,1,0:T(8,128)(2,1)S(1)}, u32[]{:S(2)}, u32[]{:S(2)}) collective-permute-start(bf16[8,64,128]{2,1,0:T(8,128)(2,1)S(1)} %shard_map.107), channel_id=1, source_target_pairs={{0,6},{1,7},{2,4},{3,5},{4,2},{5,3},{6,0},{7,1},{8,14},{9,15},{10,... | collective-permute-start | bytes 393224 | tf_op jit(solution)/shard_map/ppermute | solution.py:20
  70.4 2.3 %collective-permute-start.19 = (bf16[8,64,128]{2,1,0:T(8,128)(2,1)S(1)}, bf16[8,64,128]{2,1,0:T(8,128)(2,1)S(1)}, u32[]{:S(2)}, u32[]{:S(2)}) collective-permute-start(bf16[8,64,128]{2,1,0:T(8,128)(2,1)S(1)} %shard_map.80), channel_id=1, source_target_pairs={{0,6},{1,7},{2,4},{3,5},{4,2},{5,3},{6,0},{7,1},{8,14},{9,15},{10,... | collective-permute-start | bytes 393224 | tf_op jit(solution)/shard_map/ppermute | solution.py:20
  75.0 1.9 %collective-permute-start.38 = (bf16[8,64,128]{2,1,0:T(8,128)(2,1)S(1)}, bf16[8,64,128]{2,1,0:T(8,128)(2,1)S(1)}, u32[]{:S(2)}, u32[]{:S(2)}) collective-permute-start(bf16[8,64,128]{2,1,0:T(8,128)(2,1)S(1)} %shard_map.108.own_ref.partner_ref), channel_id=1, source_target_pairs={{0,8},{8,0},{16,24},{24,16},{32,40},{40,32},{48,56},{56,48},{64,72... | collective-permute-start | bytes 393224 | tf_op jit(solution)/shard_map/ppermute | solution.py:20
  82.7 2.0 %collective-permute-start.21 = (bf16[8,64,128]{2,1,0:T(8,128)(2,1)S(1)}, bf16[8,64,128]{2,1,0:T(8,128)(2,1)S(1)}, u32[]{:S(2)}, u32[]{:S(2)}) collective-permute-start(bf16[8,64,128]{2,1,0:T(8,128)(2,1)S(1)} %shard_map.83), channel_id=1, source_target_pairs={{0,24},{8,16},{16,8},{24,0},{32,56},{40,48},{48,40},{56,32},{64,88... | collective-permute-start | bytes 393224 | tf_op jit(solution)/shard_map/ppermute | solution.py:20
  90.2 2.4 %collective-permute-done.40.partner_ref.own_ref = bf16[8,64,128]{2,1,0:T(8,128)(2,1)S(1)} collective-permute-done((bf16[8,64,128]{2,1,0:T(8,128)(2,1)S(1)}, bf16[8,64,128]{2,1,0:T(8,128)(2,1)S(1)}, u32[]{:S(2)}, u32[]{:S(2)}) %collective-permute-start.40) | collective-permute-done | bytes 131104 | tf_op jit(solution)/shard_map/ppermute | solution.py:20
  92.9 2.8 %collective-permute-start.41 = (bf16[8,64,128]{2,1,0:T(8,128)(2,1)S(1)}, bf16[8,64,128]{2,1,0:T(8,128)(2,1)S(1)}, u32[]{:S(2)}, u32[]{:S(2)}) collective-permute-start(bf16[8,64,128]{2,1,0:T(8,128)(2,1)S(1)} %shard_map.114), channel_id=1, source_target_pairs={{0,96},{8,104},{16,112},{24,120},{32,64},{40,72},{48,80},{56,88},{... | collective-permute-start | bytes 393224 | tf_op jit(solution)/shard_map/ppermute | solution.py:20
  100.0 2.2 %collective-permute-done.23.partner_ref = bf16[8,64,128]{2,1,0:T(8,128)(2,1)S(1)} collective-permute-done((bf16[8,64,128]{2,1,0:T(8,128)(2,1)S(1)}, bf16[8,64,128]{2,1,0:T(8,128)(2,1)S(1)}, u32[]{:S(2)}, u32[]{:S(2)}) %collective-permute-start.23) | collective-permute-done | bytes 131104 | tf_op jit(solution)/shard_map/ppermute | solution.py:20
  103.4 2.9 %collective-permute-start.43 = (bf16[16,64,128]{2,1,0:T(8,128)(2,1)S(1)}, bf16[16,64,128]{2,1,0:T(8,128)(2,1)S(1)}, u32[]{:S(2)}, u32[]{:S(2)}) collective-permute-start(bf16[16,64,128]{2,1,0:T(8,128)(2,1)S(1)} %shard_map.116.refs_1_), channel_id=1, source_target_pairs={{8,16},{16,8},{24,32},{32,24},{40,48},{48,40},{56,64},{64,56},{72,... | collective-permute-start | bytes 786440 | tf_op jit(solution)/shard_map/ppermute | solution.py:28
  106.6 2.0 %collective-permute-start.29 = (bf16[8,64,128]{2,1,0:T(8,128)(2,1)S(1)}, bf16[8,64,128]{2,1,0:T(8,128)(2,1)S(1)}, u32[]{:S(2)}, u32[]{:S(2)}) collective-permute-start(bf16[8,64,128]{2,1,0:T(8,128)(2,1)S(1)} %shard_map.95.own_ref.partner_ref), channel_id=1, source_target_pairs={{0,2},{1,3},{2,0},{3,1},{4,6},{5,7},{6,4},{7,5},{8,10},{9,11},{10,... | collective-permute-start | bytes 393224 | tf_op jit(solution)/shard_map/ppermute | solution.py:20
  109.5 2.2 %collective-permute-start.46 = (bf16[8,64,128]{2,1,0:T(8,128)(2,1)S(1)}, bf16[8,64,128]{2,1,0:T(8,128)(2,1)S(1)}, u32[]{:S(2)}, u32[]{:S(2)}) collective-permute-start(bf16[8,64,128]{2,1,0:T(8,128)(2,1)S(1)} %shard_map.121), channel_id=1, source_target_pairs={{0,6},{1,7},{2,4},{3,5},{4,2},{5,3},{6,0},{7,1},{8,14},{9,15},{10,... | collective-permute-start | bytes 393224 | tf_op jit(solution)/shard_map/ppermute | solution.py:20
  112.5 2.3 %collective-permute-start.30 = (bf16[8,64,128]{2,1,0:T(8,128)(2,1)S(1)}, bf16[8,64,128]{2,1,0:T(8,128)(2,1)S(1)}, u32[]{:S(2)}, u32[]{:S(2)}) collective-permute-start(bf16[8,64,128]{2,1,0:T(8,128)(2,1)S(1)} %shard_map.97), channel_id=1, source_target_pairs={{0,6},{1,7},{2,4},{3,5},{4,2},{5,3},{6,0},{7,1},{8,14},{9,15},{10,... | collective-permute-start | bytes 393224 | tf_op jit(solution)/shard_map/ppermute | solution.py:20
  116.2 2.0 %collective-permute-start.47 = (bf16[8,64,128]{2,1,0:T(8,128)(2,1)S(1)}, bf16[8,64,128]{2,1,0:T(8,128)(2,1)S(1)}, u32[]{:S(2)}, u32[]{:S(2)}) collective-permute-start(bf16[8,64,128]{2,1,0:T(8,128)(2,1)S(1)} %shard_map.122.own_ref.partner_ref), channel_id=1, source_target_pairs={{0,8},{8,0},{16,24},{24,16},{32,40},{40,32},{48,56},{56,48},{64,72... | collective-permute-start | bytes 393224 | tf_op jit(solution)/shard_map/ppermute | solution.py:20
  124.5 1.7 %collective-permute-start.32 = (bf16[8,64,128]{2,1,0:T(8,128)(2,1)S(1)}, bf16[8,64,128]{2,1,0:T(8,128)(2,1)S(1)}, u32[]{:S(2)}, u32[]{:S(2)}) collective-permute-start(bf16[8,64,128]{2,1,0:T(8,128)(2,1)S(1)} %shard_map.100), channel_id=1, source_target_pairs={{0,24},{8,16},{16,8},{24,0},{32,56},{40,48},{48,40},{56,32},{64,88... | collective-permute-start | bytes 393224 | tf_op jit(solution)/shard_map/ppermute | solution.py:20
  132.0 2.6 %collective-permute-done.49.partner_ref.own_ref = bf16[8,64,128]{2,1,0:T(8,128)(2,1)S(1)} collective-permute-done((bf16[8,64,128]{2,1,0:T(8,128)(2,1)S(1)}, bf16[8,64,128]{2,1,0:T(8,128)(2,1)S(1)}, u32[]{:S(2)}, u32[]{:S(2)}) %collective-permute-start.49) | collective-permute-done | bytes 131104 | tf_op jit(solution)/shard_map/ppermute | solution.py:20
  136.6 2.0 %collective-permute-start.34 = (bf16[8,64,128]{2,1,0:T(8,128)(2,1)S(1)}, bf16[8,64,128]{2,1,0:T(8,128)(2,1)S(1)}, u32[]{:S(2)}, u32[]{:S(2)}) collective-permute-start(bf16[8,64,128]{2,1,0:T(8,128)(2,1)S(1)} %shard_map.103), channel_id=1, source_target_pairs={{0,96},{8,104},{16,112},{24,120},{32,64},{40,72},{48,80},{56,88},{... | collective-permute-start | bytes 393224 | tf_op jit(solution)/shard_map/ppermute | solution.py:20
  139.0 2.2 %collective-permute-done.50.partner_ref = bf16[8,64,128]{2,1,0:T(8,128)(2,1)S(1)} collective-permute-done((bf16[8,64,128]{2,1,0:T(8,128)(2,1)S(1)}, bf16[8,64,128]{2,1,0:T(8,128)(2,1)S(1)}, u32[]{:S(2)}, u32[]{:S(2)}) %collective-permute-start.50) | collective-permute-done | bytes 131104 | tf_op jit(solution)/shard_map/ppermute | solution.py:20
  (163 shorter events, 64.4 us)
Async XLA Ops:
  1.7 32.0 %collective-permute-start.4 = (bf16[1,16,2,128,128]{4,3,2,1,0:T(8,128)(2,1)S(1)}, bf16[1,16,2,128,128]{4,3,2,1,0:T(8,128)(2,1)S(1)}, u32[]{:S(2)}, u32[]{:S(2)}) collective-permute-start(bf16[1,16,2,128,128]{4,3,2,1,0:T(8,128)(2,1)S(1)} %get-tuple-element.6), channel_id=1, source_target_pairs={{0,8},{8,0},{16,24},{24,16},{32,40},{40,32},{48,56},{56,48},{64,72... | collective-permute-start | bytes 3145736 | tf_op jit(solution)/shard_map/ppermute | solution.py:20
  3.8 43.0 %collective-permute-start.7 = (bf16[1,16,2,128,128]{4,3,2,1,0:T(8,128)(2,1)S(1)}, bf16[1,16,2,128,128]{4,3,2,1,0:T(8,128)(2,1)S(1)}, u32[]{:S(2)}, u32[]{:S(2)}) collective-permute-start(bf16[1,16,2,128,128]{4,3,2,1,0:T(8,128)(2,1)S(1)} %get-tuple-element.5), channel_id=1, source_target_pairs={{0,32},{8,40},{16,48},{24,56},{32,0},{40,8},{48,16},{56,24},{64,96... | collective-permute-start | bytes 3145736 | tf_op jit(solution)/shard_map/ppermute | solution.py:20
  10.3 6.4 %collective-permute-start.10 = (bf16[8,64,128]{2,1,0:T(8,128)(2,1)S(1)}, bf16[8,64,128]{2,1,0:T(8,128)(2,1)S(1)}, u32[]{:S(2)}, u32[]{:S(2)}) collective-permute-start(bf16[8,64,128]{2,1,0:T(8,128)(2,1)S(1)} %shard_map.67.own_ref), channel_id=1, source_target_pairs={{0,2},{1,3},{2,0},{3,1},{4,6},{5,7},{6,4},{7,5},{8,10},{9,11},{10,... | collective-permute-start | bytes 393224 | tf_op jit(solution)/shard_map/ppermute | solution.py:20
  12.1 8.0 %collective-permute-start.1 = (bf16[8,64,128]{2,1,0:T(8,128)(2,1)S(1)}, bf16[8,64,128]{2,1,0:T(8,128)(2,1)S(1)}, u32[]{:S(2)}, u32[]{:S(2)}) collective-permute-start(bf16[8,64,128]{2,1,0:T(8,128)(2,1)S(1)} %shard_map.57.own_ref), channel_id=1, source_target_pairs={{0,2},{1,3},{2,0},{3,1},{4,6},{5,7},{6,4},{7,5},{8,10},{9,11},{10,... | collective-permute-start | bytes 393224 | tf_op jit(solution)/shard_map/ppermute | solution.py:20
  17.0 7.8 %collective-permute-start.11 = (bf16[8,64,128]{2,1,0:T(8,128)(2,1)S(1)}, bf16[8,64,128]{2,1,0:T(8,128)(2,1)S(1)}, u32[]{:S(2)}, u32[]{:S(2)}) collective-permute-start(bf16[8,64,128]{2,1,0:T(8,128)(2,1)S(1)} %shard_map.68.own_ref), channel_id=1, source_target_pairs={{0,4},{1,5},{2,6},{3,7},{4,0},{5,1},{6,2},{7,3},{8,12},{9,13},{10,... | collective-permute-start | bytes 393224 | tf_op jit(solution)/shard_map/ppermute | solution.py:20
  20.3 6.6 %collective-permute-start.2 = (bf16[8,64,128]{2,1,0:T(8,128)(2,1)S(1)}, bf16[8,64,128]{2,1,0:T(8,128)(2,1)S(1)}, u32[]{:S(2)}, u32[]{:S(2)}) collective-permute-start(bf16[8,64,128]{2,1,0:T(8,128)(2,1)S(1)} %shard_map.58.own_ref), channel_id=1, source_target_pairs={{0,4},{1,5},{2,6},{3,7},{4,0},{5,1},{6,2},{7,3},{8,12},{9,13},{10,... | collective-permute-start | bytes 393224 | tf_op jit(solution)/shard_map/ppermute | solution.py:20
  27.2 39.8 %collective-permute-start.18 = (bf16[1,16,2,128,128]{4,3,2,1,0:T(8,128)(2,1)S(1)}, bf16[1,16,2,128,128]{4,3,2,1,0:T(8,128)(2,1)S(1)}, u32[]{:S(2)}, u32[]{:S(2)}) collective-permute-start(bf16[1,16,2,128,128]{4,3,2,1,0:T(8,128)(2,1)S(1)} %shard_map.79), channel_id=1, source_target_pairs={{0,2},{1,3},{2,0},{3,1},{4,6},{5,7},{6,4},{7,5},{8,10},{9,11},{10,... | collective-permute-start | bytes 3145736 | tf_op jit(solution)/shard_map/ppermute | solution.py:20
  28.3 8.2 %collective-permute-start.3 = (bf16[8,64,128]{2,1,0:T(8,128)(2,1)S(1)}, bf16[8,64,128]{2,1,0:T(8,128)(2,1)S(1)}, u32[]{:S(2)}, u32[]{:S(2)}) collective-permute-start(bf16[8,64,128]{2,1,0:T(8,128)(2,1)S(1)} %shard_map.59.own_ref.partner_ref.refs_1_), channel_id=1, source_target_pairs={{0,8},{8,0},{16,24},{24,16},{32,40},{40,32},{48,56},{56,48},{64,72... | collective-permute-start | bytes 393224 | tf_op jit(solution)/shard_map/ppermute | solution.py:20
  34.0 6.6 %collective-permute-start.13 = (bf16[8,64,128]{2,1,0:T(8,128)(2,1)S(1)}, bf16[8,64,128]{2,1,0:T(8,128)(2,1)S(1)}, u32[]{:S(2)}, u32[]{:S(2)}) collective-permute-start(bf16[8,64,128]{2,1,0:T(8,128)(2,1)S(1)} %shard_map.71), channel_id=1, source_target_pairs={{0,24},{8,16},{16,8},{24,0},{32,56},{40,48},{48,40},{56,32},{64,88... | collective-permute-start | bytes 393224 | tf_op jit(solution)/shard_map/ppermute | solution.py:20
  36.8 8.3 %collective-permute-start.5 = (bf16[8,64,128]{2,1,0:T(8,128)(2,1)S(1)}, bf16[8,64,128]{2,1,0:T(8,128)(2,1)S(1)}, u32[]{:S(2)}, u32[]{:S(2)}) collective-permute-start(bf16[8,64,128]{2,1,0:T(8,128)(2,1)S(1)} %shard_map.61), channel_id=1, source_target_pairs={{0,24},{8,16},{16,8},{24,0},{32,56},{40,48},{48,40},{56,32},{64,88... | collective-permute-start | bytes 393224 | tf_op jit(solution)/shard_map/ppermute | solution.py:20
  40.8 15.1 %collective-permute-start.14 = (bf16[16,64,128]{2,1,0:T(8,128)(2,1)S(1)}, bf16[16,64,128]{2,1,0:T(8,128)(2,1)S(1)}, u32[]{:S(2)}, u32[]{:S(2)}) collective-permute-start(bf16[16,64,128]{2,1,0:T(8,128)(2,1)S(1)} %shard_map.73.refs_1_), channel_id=1, source_target_pairs={{0,8},{8,0},{16,24},{24,16},{32,40},{40,32},{48,56},{56,48},{64,72... | collective-permute-start | bytes 786440 | tf_op jit(solution)/shard_map/ppermute | solution.py:20
  40.9 15.0 %collective-permute-start.15 = (bf16[16,64,128]{2,1,0:T(8,128)(2,1)S(1)}, bf16[16,64,128]{2,1,0:T(8,128)(2,1)S(1)}, u32[]{:S(2)}, u32[]{:S(2)}) collective-permute-start(bf16[16,64,128]{2,1,0:T(8,128)(2,1)S(1)} %shard_map.73.refs_1_), channel_id=1, source_target_pairs={{8,16},{16,8},{24,32},{32,24},{40,48},{48,40},{56,64},{64,56},{72,... | collective-permute-start | bytes 786440 | tf_op jit(solution)/shard_map/ppermute | solution.py:28
  45.1 6.4 %collective-permute-start.24 = (bf16[8,64,128]{2,1,0:T(8,128)(2,1)S(1)}, bf16[8,64,128]{2,1,0:T(8,128)(2,1)S(1)}, u32[]{:S(2)}, u32[]{:S(2)}) collective-permute-start(bf16[8,64,128]{2,1,0:T(8,128)(2,1)S(1)} %shard_map.72.refs_2_.own_ref.partner_ref), channel_id=1, source_target_pairs={{0,32},{8,40},{16,48},{24,56},{32,0},{40,8},{48,16},{56,24},{64,96... | collective-permute-start | bytes 393224 | tf_op jit(solution)/shard_map/ppermute | solution.py:20
  46.8 6.5 %collective-permute-start.6 = (bf16[8,64,128]{2,1,0:T(8,128)(2,1)S(1)}, bf16[8,64,128]{2,1,0:T(8,128)(2,1)S(1)}, u32[]{:S(2)}, u32[]{:S(2)}) collective-permute-start(bf16[8,64,128]{2,1,0:T(8,128)(2,1)S(1)} %shard_map.62.own_ref.partner_ref), channel_id=1, source_target_pairs={{0,32},{8,40},{16,48},{24,56},{32,0},{40,8},{48,16},{56,24},{64,96... | collective-permute-start | bytes 393224 | tf_op jit(solution)/shard_map/ppermute | solution.py:20
  51.8 6.3 %collective-permute-start.25 = (bf16[8,64,128]{2,1,0:T(8,128)(2,1)S(1)}, bf16[8,64,128]{2,1,0:T(8,128)(2,1)S(1)}, u32[]{:S(2)}, u32[]{:S(2)}) collective-permute-start(bf16[8,64,128]{2,1,0:T(8,128)(2,1)S(1)} %shard_map.88), channel_id=1, source_target_pairs={{0,96},{8,104},{16,112},{24,120},{32,64},{40,72},{48,80},{56,88},{... | collective-permute-start | bytes 393224 | tf_op jit(solution)/shard_map/ppermute | solution.py:20
  53.6 6.5 %collective-permute-start.8 = (bf16[8,64,128]{2,1,0:T(8,128)(2,1)S(1)}, bf16[8,64,128]{2,1,0:T(8,128)(2,1)S(1)}, u32[]{:S(2)}, u32[]{:S(2)}) collective-permute-start(bf16[8,64,128]{2,1,0:T(8,128)(2,1)S(1)} %shard_map.64), channel_id=1, source_target_pairs={{0,96},{8,104},{16,112},{24,120},{32,64},{40,72},{48,80},{56,88},{... | collective-permute-start | bytes 393224 | tf_op jit(solution)/shard_map/ppermute | solution.py:20
  62.1 11.5 %collective-permute-start.27 = (bf16[16,64,128]{2,1,0:T(8,128)(2,1)S(1)}, bf16[16,64,128]{2,1,0:T(8,128)(2,1)S(1)}, u32[]{:S(2)}, u32[]{:S(2)}) collective-permute-start(bf16[16,64,128]{2,1,0:T(8,128)(2,1)S(1)} %shard_map.91.refs_1_), channel_id=1, source_target_pairs={{8,16},{16,8},{24,32},{32,24},{40,48},{48,40},{56,64},{64,56},{72,... | collective-permute-start | bytes 786440 | tf_op jit(solution)/shard_map/ppermute | solution.py:28
  67.0 11.4 %collective-permute-start.26 = (bf16[16,64,128]{2,1,0:T(8,128)(2,1)S(1)}, bf16[16,64,128]{2,1,0:T(8,128)(2,1)S(1)}, u32[]{:S(2)}, u32[]{:S(2)}) collective-permute-start(bf16[16,64,128]{2,1,0:T(8,128)(2,1)S(1)} %shard_map.91.refs_1_), channel_id=1, source_target_pairs={{0,8},{8,0},{16,24},{24,16},{32,40},{40,32},{48,56},{56,48},{64,72... | collective-permute-start | bytes 786440 | tf_op jit(solution)/shard_map/ppermute | solution.py:20
  67.7 7.2 %collective-permute-start.37 = (bf16[8,64,128]{2,1,0:T(8,128)(2,1)S(1)}, bf16[8,64,128]{2,1,0:T(8,128)(2,1)S(1)}, u32[]{:S(2)}, u32[]{:S(2)}) collective-permute-start(bf16[8,64,128]{2,1,0:T(8,128)(2,1)S(1)} %shard_map.107), channel_id=1, source_target_pairs={{0,6},{1,7},{2,4},{3,5},{4,2},{5,3},{6,0},{7,1},{8,14},{9,15},{10,... | collective-permute-start | bytes 393224 | tf_op jit(solution)/shard_map/ppermute | solution.py:20
  70.4 6.8 %collective-permute-start.19 = (bf16[8,64,128]{2,1,0:T(8,128)(2,1)S(1)}, bf16[8,64,128]{2,1,0:T(8,128)(2,1)S(1)}, u32[]{:S(2)}, u32[]{:S(2)}) collective-permute-start(bf16[8,64,128]{2,1,0:T(8,128)(2,1)S(1)} %shard_map.80), channel_id=1, source_target_pairs={{0,6},{1,7},{2,4},{3,5},{4,2},{5,3},{6,0},{7,1},{8,14},{9,15},{10,... | collective-permute-start | bytes 393224 | tf_op jit(solution)/shard_map/ppermute | solution.py:20
  81.1 6.3 %collective-permute-start.39 = (bf16[8,64,128]{2,1,0:T(8,128)(2,1)S(1)}, bf16[8,64,128]{2,1,0:T(8,128)(2,1)S(1)}, u32[]{:S(2)}, u32[]{:S(2)}) collective-permute-start(bf16[8,64,128]{2,1,0:T(8,128)(2,1)S(1)} %shard_map.111), channel_id=1, source_target_pairs={{0,24},{8,16},{16,8},{24,0},{32,56},{40,48},{48,40},{56,32},{64,88... | collective-permute-start | bytes 393224 | tf_op jit(solution)/shard_map/ppermute | solution.py:20
  82.7 6.3 %collective-permute-start.21 = (bf16[8,64,128]{2,1,0:T(8,128)(2,1)S(1)}, bf16[8,64,128]{2,1,0:T(8,128)(2,1)S(1)}, u32[]{:S(2)}, u32[]{:S(2)}) collective-permute-start(bf16[8,64,128]{2,1,0:T(8,128)(2,1)S(1)} %shard_map.83), channel_id=1, source_target_pairs={{0,24},{8,16},{16,8},{24,0},{32,56},{40,48},{48,40},{56,32},{64,88... | collective-permute-start | bytes 393224 | tf_op jit(solution)/shard_map/ppermute | solution.py:20
  89.2 6.5 %collective-permute-start.22 = (bf16[8,64,128]{2,1,0:T(8,128)(2,1)S(1)}, bf16[8,64,128]{2,1,0:T(8,128)(2,1)S(1)}, u32[]{:S(2)}, u32[]{:S(2)}) collective-permute-start(bf16[8,64,128]{2,1,0:T(8,128)(2,1)S(1)} %shard_map.84.own_ref.partner_ref), channel_id=1, source_target_pairs={{0,32},{8,40},{16,48},{24,56},{32,0},{40,8},{48,16},{56,24},{64,96... | collective-permute-start | bytes 393224 | tf_op jit(solution)/shard_map/ppermute | solution.py:20
  92.9 6.3 %collective-permute-start.41 = (bf16[8,64,128]{2,1,0:T(8,128)(2,1)S(1)}, bf16[8,64,128]{2,1,0:T(8,128)(2,1)S(1)}, u32[]{:S(2)}, u32[]{:S(2)}) collective-permute-start(bf16[8,64,128]{2,1,0:T(8,128)(2,1)S(1)} %shard_map.114), channel_id=1, source_target_pairs={{0,96},{8,104},{16,112},{24,120},{32,64},{40,72},{48,80},{56,88},{... | collective-permute-start | bytes 393224 | tf_op jit(solution)/shard_map/ppermute | solution.py:20
  95.9 6.3 %collective-permute-start.23 = (bf16[8,64,128]{2,1,0:T(8,128)(2,1)S(1)}, bf16[8,64,128]{2,1,0:T(8,128)(2,1)S(1)}, u32[]{:S(2)}, u32[]{:S(2)}) collective-permute-start(bf16[8,64,128]{2,1,0:T(8,128)(2,1)S(1)} %shard_map.86), channel_id=1, source_target_pairs={{0,96},{8,104},{16,112},{24,120},{32,64},{40,72},{48,80},{56,88},{... | collective-permute-start | bytes 393224 | tf_op jit(solution)/shard_map/ppermute | solution.py:20
  103.4 12.1 %collective-permute-start.43 = (bf16[16,64,128]{2,1,0:T(8,128)(2,1)S(1)}, bf16[16,64,128]{2,1,0:T(8,128)(2,1)S(1)}, u32[]{:S(2)}, u32[]{:S(2)}) collective-permute-start(bf16[16,64,128]{2,1,0:T(8,128)(2,1)S(1)} %shard_map.116.refs_1_), channel_id=1, source_target_pairs={{8,16},{16,8},{24,32},{32,24},{40,48},{48,40},{56,64},{64,56},{72,... | collective-permute-start | bytes 786440 | tf_op jit(solution)/shard_map/ppermute | solution.py:28
  108.6 11.6 %collective-permute-start.42 = (bf16[16,64,128]{2,1,0:T(8,128)(2,1)S(1)}, bf16[16,64,128]{2,1,0:T(8,128)(2,1)S(1)}, u32[]{:S(2)}, u32[]{:S(2)}) collective-permute-start(bf16[16,64,128]{2,1,0:T(8,128)(2,1)S(1)} %shard_map.116.refs_1_), channel_id=1, source_target_pairs={{0,8},{8,0},{16,24},{24,16},{32,40},{40,32},{48,56},{56,48},{64,72... | collective-permute-start | bytes 786440 | tf_op jit(solution)/shard_map/ppermute | solution.py:20
  109.5 6.4 %collective-permute-start.46 = (bf16[8,64,128]{2,1,0:T(8,128)(2,1)S(1)}, bf16[8,64,128]{2,1,0:T(8,128)(2,1)S(1)}, u32[]{:S(2)}, u32[]{:S(2)}) collective-permute-start(bf16[8,64,128]{2,1,0:T(8,128)(2,1)S(1)} %shard_map.121), channel_id=1, source_target_pairs={{0,6},{1,7},{2,4},{3,5},{4,2},{5,3},{6,0},{7,1},{8,14},{9,15},{10,... | collective-permute-start | bytes 393224 | tf_op jit(solution)/shard_map/ppermute | solution.py:20
  112.5 6.5 %collective-permute-start.30 = (bf16[8,64,128]{2,1,0:T(8,128)(2,1)S(1)}, bf16[8,64,128]{2,1,0:T(8,128)(2,1)S(1)}, u32[]{:S(2)}, u32[]{:S(2)}) collective-permute-start(bf16[8,64,128]{2,1,0:T(8,128)(2,1)S(1)} %shard_map.97), channel_id=1, source_target_pairs={{0,6},{1,7},{2,4},{3,5},{4,2},{5,3},{6,0},{7,1},{8,14},{9,15},{10,... | collective-permute-start | bytes 393224 | tf_op jit(solution)/shard_map/ppermute | solution.py:20
  122.6 6.8 %collective-permute-start.48 = (bf16[8,64,128]{2,1,0:T(8,128)(2,1)S(1)}, bf16[8,64,128]{2,1,0:T(8,128)(2,1)S(1)}, u32[]{:S(2)}, u32[]{:S(2)}) collective-permute-start(bf16[8,64,128]{2,1,0:T(8,128)(2,1)S(1)} %shard_map.125), channel_id=1, source_target_pairs={{0,24},{8,16},{16,8},{24,0},{32,56},{40,48},{48,40},{56,32},{64,88... | collective-permute-start | bytes 393224 | tf_op jit(solution)/shard_map/ppermute | solution.py:20
  124.5 6.3 %collective-permute-start.32 = (bf16[8,64,128]{2,1,0:T(8,128)(2,1)S(1)}, bf16[8,64,128]{2,1,0:T(8,128)(2,1)S(1)}, u32[]{:S(2)}, u32[]{:S(2)}) collective-permute-start(bf16[8,64,128]{2,1,0:T(8,128)(2,1)S(1)} %shard_map.100), channel_id=1, source_target_pairs={{0,24},{8,16},{16,8},{24,0},{32,56},{40,48},{48,40},{56,32},{64,88... | collective-permute-start | bytes 393224 | tf_op jit(solution)/shard_map/ppermute | solution.py:20
  136.6 6.3 %collective-permute-start.34 = (bf16[8,64,128]{2,1,0:T(8,128)(2,1)S(1)}, bf16[8,64,128]{2,1,0:T(8,128)(2,1)S(1)}, u32[]{:S(2)}, u32[]{:S(2)}) collective-permute-start(bf16[8,64,128]{2,1,0:T(8,128)(2,1)S(1)} %shard_map.103), channel_id=1, source_target_pairs={{0,96},{8,104},{16,112},{24,120},{32,64},{40,72},{48,80},{56,88},{... | collective-permute-start | bytes 393224 | tf_op jit(solution)/shard_map/ppermute | solution.py:20
  (26 other events, 139.8 us)
